TPU v7x, 32 devices: a whole 2x2x4 slice. The times are simulated.
32 devices in a mesh: gx: 16 (over z, y, core), gy: 2 (over x).
Axes of the slice: x: 2, y: 2, z: 4, core: 2. Of those that a mesh axis runs over, the one named last changes fastest.
Arguments:
- hamiltonian: bfloat16 [32, 4, 8, 128, 128], P('gx', 'gy'), may hold values from -0.078125 to 0.078125
- neighbours: int32 [32, 4, 8], P('gx', 'gy'), may hold values from 0 to 8, as said below
- probe_seeds: int32 [256], replicated, may hold values from 0 to 1073741823
- coefficients: float32 [5], replicated, may hold values from 0.3 to 1
- cotangent: bfloat16 [32, 4, 128, 256], P('gx', 'gy'), may hold values from -6 to 6
Outputs:
- density: float32 [32, 4, 128, 256], P('gx', 'gy')
- grad_hamiltonian: bfloat16 [32, 4, 8, 128, 128], P('gx', 'gy')
Inputs may be any that keep to these rules, and one draw needn't show every extreme that they name: `neighbours`: each block's list holds 8 different codes.
All inputs are finite; a program needn't handle non-finite values.
Results may differ from a plain program's by a relative error of at most 0.0064.
Values may be sent and summed in bfloat16 or wider, within the bound.
No kernel may reach another device: no remote copies, remote signals or barrier semaphores. Data moves between devices by JAX's collectives and lax.ppermute only.
A program may use at most 64 MiB of HBM per device.

v0:
```python
import jax
import jax.numpy as jnp
from jax import lax
from jax.sharding import PartitionSpec as P

offset_table = tuple(((offset_code // 3 - 1, offset_code % 3 - 1) for offset_code in range(9)))


def shifted(value, axis, steps):
    count = lax.axis_size(axis)
    pairs = [(source, (source + steps) % count) for source in range(count)]
    return lax.ppermute(value, axis, pairs)


def padded_2(block, sides, width):
    for axis, dim in sides:
        count = lax.axis_size(axis)
        forward = [(i, i + 1) for i in range(count - 1)]
        forward.append((count - 1, 0))
        backward = [(target, source) for source, target in forward]
        low = lax.ppermute(
            lax.slice_in_dim(block, block.shape[dim] - width, None, axis=dim), axis, forward
        )
        high = lax.ppermute(lax.slice_in_dim(block, 0, width, axis=dim), axis, backward)
        block = jnp.concatenate([low, block, high], axis=dim)
    return block


def probe_signs(global_rows, seed_values):
    hashed = global_rows[..., None] * jnp.int32(-1640531535)
    hashed = hashed ^ seed_values
    hashed = hashed ^ hashed >> 15
    hashed = hashed * jnp.int32(739982445)
    hashed = hashed ^ hashed >> 12
    parity = hashed >> 7 & 1
    return (1 - 2 * parity).astype(jnp.float32)


def by_offset(hamiltonian, neighbours):
    onehot = (neighbours[..., None] == jnp.arange(9, dtype=jnp.int32)).astype(jnp.bfloat16)
    picked = jnp.einsum(
        "abkc,abkxy->abcxy", onehot, hamiltonian, preferred_element_type=jnp.float32
    )
    return picked.astype(jnp.bfloat16)


def forward_apply(selected, padded):
    rows_x, rows_y = (selected.shape[0], selected.shape[1])
    summed = jnp.zeros((rows_x, rows_y, selected.shape[3], padded.shape[3]), jnp.float32)
    for offset_code, (step_x, step_y) in enumerate(offset_table):
        window = padded[1 + step_x : 1 + step_x + rows_x, 1 + step_y : 1 + step_y + rows_y]
        summed = summed + jnp.einsum(
            "abxy,abyp->abxp",
            selected[:, :, offset_code],
            window,
            preferred_element_type=jnp.float32,
        )
    return summed


def push_transpose(selected, adjoint_bf16):
    rows_x, rows_y = (selected.shape[0], selected.shape[1])
    gathered = jnp.zeros((rows_x + 2, rows_y + 2) + adjoint_bf16.shape[2:], jnp.float32)
    for offset_code, (step_x, step_y) in enumerate(offset_table):
        product = jnp.einsum(
            "abyx,abyp->abxp",
            selected[:, :, offset_code],
            adjoint_bf16,
            preferred_element_type=jnp.float32,
        )
        gathered = gathered + jnp.pad(
            product, ((1 + step_x, 1 - step_x), (1 + step_y, 1 - step_y), (0, 0), (0, 0))
        )
    for offset_by, source, target in ((-1, 0, rows_x), (1, rows_x + 1, 1)):
        moved = shifted(gathered[source], "gx", offset_by)
        gathered = gathered.at[target].add(moved)
    middle = gathered[1 : rows_x + 1]
    for offset_by, source, target in ((-1, 0, rows_y), (1, rows_y + 1, 1)):
        moved = shifted(middle[:, source], "gy", offset_by)
        middle = middle.at[:, target].add(moved)
    return middle[:, 1 : rows_y + 1]


def shards(hamiltonian, neighbours, probe_seeds, coefficients, cotangent):
    rows_x, rows_y = (hamiltonian.shape[0], hamiltonian.shape[1])
    width = hamiltonian.shape[3]
    probes = cotangent.shape[3]
    count_terms = coefficients.shape[0]
    span_x = rows_x * lax.axis_size("gx")
    span_y = rows_y * lax.axis_size("gy")
    place_x = (lax.axis_index("gx") * rows_x + jnp.arange(rows_x + 2, dtype=jnp.int32) - 1) % span_x
    place_y = (lax.axis_index("gy") * rows_y + jnp.arange(rows_y + 2, dtype=jnp.int32) - 1) % span_y
    orbital = jnp.arange(width, dtype=jnp.int32)
    global_rows = (place_x[:, None] * span_y + place_y[None, :])[:, :, None] * width + orbital[
        None, None, :
    ]
    start_padded = probe_signs(global_rows, probe_seeds)
    start_term = start_padded[1 : rows_x + 1, 1 : rows_y + 1]
    selected = by_offset(hamiltonian, neighbours)
    term_pads = [start_padded.astype(jnp.bfloat16)]
    previous = start_term
    current = forward_apply(selected, term_pads[0])
    density = coefficients[0] * start_term + coefficients[1] * current
    for index in range(2, count_terms):
        padded = padded_2(current.astype(jnp.bfloat16), (("gx", 0), ("gy", 1)), 1)
        term_pads.append(padded)
        following = 2.0 * forward_apply(selected, padded) - previous
        previous, current = (current, following)
        density = density + coefficients[index] * current
    seed_field = cotangent.astype(jnp.float32)
    adjoints = {}
    adjoint_rounded = {}
    for index in range(count_terms - 1, 0, -1):
        value = coefficients[index] * seed_field
        if index + 1 < count_terms:
            carried = push_transpose(selected, adjoint_rounded[index + 1])
            value = value + 2.0 * carried
        if index + 2 < count_terms:
            value = value - adjoints[index + 2]
        adjoints[index] = value
        adjoint_rounded[index] = value.astype(jnp.bfloat16)
    adjoint_stack = jnp.concatenate(
        [adjoint_rounded[index] * (1.0 if index == 1 else 2.0) for index in range(1, count_terms)],
        axis=3,
    )
    term_stack = jnp.concatenate(term_pads, axis=3)
    gradient = jnp.zeros(hamiltonian.shape, jnp.float32)
    for offset_code, (step_x, step_y) in enumerate(offset_table):
        window = term_stack[1 + step_x : 1 + step_x + rows_x, 1 + step_y : 1 + step_y + rows_y]
        block_grad = jnp.einsum(
            "abxq,abyq->abxy", adjoint_stack, window, preferred_element_type=jnp.float32
        )
        gradient = gradient + jnp.where(
            (neighbours == offset_code)[..., None, None], block_grad[:, :, None], 0.0
        )
    return (density, (gradient * (1.0 / probes)).astype(jnp.bfloat16))


def solution(mesh):
    placed = (
        P("gx", "gy", None, None, None),
        P("gx", "gy", None),
        P(),
        P(),
        P("gx", "gy", None, None),
    )
    return jax.shard_map(
        shards,
        mesh=mesh,
        in_specs=placed,
        out_specs=(P("gx", "gy", None, None), P("gx", "gy", None, None, None)),
        check_vma=False,
    )
```

profile of v0, /device:TPU:28, one launch (start us, length us, event | category | flops | bytes accessed | tf_op | source)
XLA Modules:
  0.0 166.1 jit_solution(869673616104691582)
XLA Ops:
  1.9 1.7 %convolution_convert_fusion = bf16[2,2,9,128,128]{4,2,3,1,0:T(8,128)(2,1)S(1)} fusion(bf16[2,2,8,128,128]{4,3,2,1,0:T(8,128)(2,1)S(1)} %copy-done, s32[2,2,8]{2,1,0:T(2,128)} %param.30), kind=kOutput, calls=%fused_computation.13 | convolution fusion | flops 10027296 | bytes 2228352 | tf_op jit(solution)/shard_map/abkc,abkxy->abcxy/dot_general | solution.py:41
  3.6 2.4 %fusion.247 = (bf16[2,2,1,128,128]{4,2,3,1,0:T(2,128)(2,1)S(1)}, bf16[2,2,1,128,128]{4,2,3,1,0:T(2,128)(2,1)S(1)}, bf16[2,2,1,128,128]{4,2,3,1,0:T(2,128)(2,1)S(...) fusion(bf16[2,2,9,128,128]{4,2,3,1,0:T(8,128)(2,1)S(1)} %convol, ...), kind=kLoop, calls=%fused_computation.325 | loop fusion | bytes 2359296 | tf_op jit(solution)/shard_map/slice | solution.py:54
  21.1 1.6 collective-permute-start.2
  23.6 5.1 %collective-permute-done.2 = bf16[4,1,128,256]{3,2,1,0:T(8,128)(2,1)S(1)} collective-permute-done((bf16[4,1,128,256]{3,2,1,0:T(8,128)(2,1)S(1)}, bf16[4,1,128,256]{3,2,1,0:T(8,128)(2,1)S(1)}, u32[]{:S(2)}, u32[]{:S(2)}) %collective-permute-start.2) | collective-permute-done | bytes 262176 | tf_op jit(solution)/shard_map/ppermute | solution.py:21
  28.7 5.6 %collective-permute-done.3 = bf16[4,1,128,256]{3,2,1,0:T(8,128)(2,1)S(1)} collective-permute-done((bf16[4,1,128,256]{3,2,1,0:T(8,128)(2,1)S(1)}, bf16[4,1,128,256]{3,2,1,0:T(8,128)(2,1)S(1)}, u32[]{:S(2)}, u32[]{:S(2)}) %collective-permute-start.3) | collective-permute-done | bytes 262176 | tf_op jit(solution)/shard_map/ppermute | solution.py:24
  37.8 4.6 %collective-permute-start.13 = (f32[4,128,256]{2,1,0:T(8,128)S(1)}, f32[4,128,256]{2,1,0:T(8,128)S(1)}, u32[]{:S(2)}, u32[]{:S(2)}) collective-permute-start(f32[4,128,256]{2,1,0:T(8,128)S(1)} %slice_bitcast_fusion.6), channel_id=1, source_target_pairs={{0,2},{2,4},{4,6},{6,8},{8,10},{10,12},{12,14},{14,16},{16,18},{18... | collective-permute-start | bytes 1572872 | tf_op jit(solution)/shard_map/ppermute | solution.py:12
  42.8 1.6 collective-permute-start.6
  45.3 2.8 %collective-permute-done.13 = f32[4,128,256]{2,1,0:T(8,128)S(1)} collective-permute-done((f32[4,128,256]{2,1,0:T(8,128)S(1)}, f32[4,128,256]{2,1,0:T(8,128)S(1)}, u32[]{:S(2)}, u32[]{:S(2)}) %collective-permute-start.13) | collective-permute-done | bytes 524320 | tf_op jit(solution)/shard_map/ppermute | solution.py:12
  48.2 1.6 collective-permute-start.14
  50.8 5.6 %collective-permute-done.7 = bf16[4,1,128,256]{3,2,1,0:T(8,128)(2,1)S(1)} collective-permute-done((bf16[4,1,128,256]{3,2,1,0:T(8,128)(2,1)S(1)}, bf16[4,1,128,256]{3,2,1,0:T(8,128)(2,1)S(1)}, u32[]{:S(2)}, u32[]{:S(2)}) %collective-permute-start.7) | collective-permute-done | bytes 262176 | tf_op jit(solution)/shard_map/ppermute | solution.py:24
  56.9 5.2 %collective-permute-done.14 = f32[2,128,256]{2,1,0:T(8,128)S(1)} collective-permute-done((f32[2,128,256]{2,1,0:T(8,128)S(1)}, f32[2,128,256]{2,1,0:T(8,128)S(1)}, u32[]{:S(2)}, u32[]{:S(2)}) %collective-permute-start.14) | collective-permute-done | bytes 262176 | tf_op jit(solution)/shard_map/ppermute | solution.py:12
  64.2 7.1 %collective-permute-done.15 = f32[2,128,256]{2,1,0:T(8,128)S(1)} collective-permute-done((f32[2,128,256]{2,1,0:T(8,128)S(1)}, f32[2,128,256]{2,1,0:T(8,128)S(1)}, u32[]{:S(2)}, u32[]{:S(2)}) %collective-permute-start.15) | collective-permute-done | bytes 262176 | tf_op jit(solution)/shard_map/ppermute | solution.py:12
  75.5 11.8 %collective-permute-done.16 = f32[4,128,256]{2,1,0:T(8,128)S(1)} collective-permute-done((f32[4,128,256]{2,1,0:T(8,128)S(1)}, f32[4,128,256]{2,1,0:T(8,128)S(1)}, u32[]{:S(2)}, u32[]{:S(2)}) %collective-permute-start.16) | collective-permute-done | bytes 524320 | tf_op jit(solution)/shard_map/ppermute | solution.py:12
  87.9 2.0 %collective-permute-start.9 = (bf16[1,2,128,256]{3,2,1,0:T(8,128)(2,1)S(1)}, bf16[1,2,128,256]{3,2,1,0:T(8,128)(2,1)S(1)}, u32[]{:S(2)}, u32[]{:S(2)}) collective-permute-start(bf16[1,2,128,256]{3,2,1,0:T(8,128)(2,1)S(1)} %get-tuple-element.173), channel_id=1, source_target_pairs={{2,0},{4,2},{6,4},{8,6},{10,8},{12,10},{14,12},{16,14},{18,16},{20... | collective-permute-start | bytes 393224 | tf_op jit(solution)/shard_map/ppermute | solution.py:24
  90.3 7.5 %collective-permute-done.17 = f32[4,128,256]{2,1,0:T(8,128)S(1)} collective-permute-done((f32[4,128,256]{2,1,0:T(8,128)S(1)}, f32[4,128,256]{2,1,0:T(8,128)S(1)}, u32[]{:S(2)}, u32[]{:S(2)}) %collective-permute-start.17) | collective-permute-done | bytes 524320 | tf_op jit(solution)/shard_map/ppermute | solution.py:12
  97.8 1.6 collective-permute-start.18
  101.7 5.4 %collective-permute-done.18 = f32[2,128,256]{2,1,0:T(8,128)S(1)} collective-permute-done((f32[2,128,256]{2,1,0:T(8,128)S(1)}, f32[2,128,256]{2,1,0:T(8,128)S(1)}, u32[]{:S(2)}, u32[]{:S(2)}) %collective-permute-start.18) | collective-permute-done | bytes 262176 | tf_op jit(solution)/shard_map/ppermute | solution.py:12
  107.2 1.6 collective-permute-start.19
  109.3 8.7 %collective-permute-done.19 = f32[2,128,256]{2,1,0:T(8,128)S(1)} collective-permute-done((f32[2,128,256]{2,1,0:T(8,128)S(1)}, f32[2,128,256]{2,1,0:T(8,128)S(1)}, u32[]{:S(2)}, u32[]{:S(2)}) %collective-permute-start.19) | collective-permute-done | bytes 262176 | tf_op jit(solution)/shard_map/ppermute | solution.py:12
  123.8 11.4 %collective-permute-done.20 = f32[4,128,256]{2,1,0:T(8,128)S(1)} collective-permute-done((f32[4,128,256]{2,1,0:T(8,128)S(1)}, f32[4,128,256]{2,1,0:T(8,128)S(1)}, u32[]{:S(2)}, u32[]{:S(2)}) %collective-permute-start.20) | collective-permute-done | bytes 524320 | tf_op jit(solution)/shard_map/ppermute | solution.py:12
  136.3 8.0 %collective-permute-done.21 = f32[4,128,256]{2,1,0:T(8,128)S(1)} collective-permute-done((f32[4,128,256]{2,1,0:T(8,128)S(1)}, f32[4,128,256]{2,1,0:T(8,128)S(1)}, u32[]{:S(2)}, u32[]{:S(2)}) %collective-permute-start.21) | collective-permute-done | bytes 524320 | tf_op jit(solution)/shard_map/ppermute | solution.py:12
  146.6 5.0 %collective-permute-done.22 = f32[2,128,256]{2,1,0:T(8,128)S(1)} collective-permute-done((f32[2,128,256]{2,1,0:T(8,128)S(1)}, f32[2,128,256]{2,1,0:T(8,128)S(1)}, u32[]{:S(2)}, u32[]{:S(2)}) %collective-permute-start.22) | collective-permute-done | bytes 262176 | tf_op jit(solution)/shard_map/ppermute | solution.py:12
  153.2 4.3 %fusion.12 = f32[2,2,128,256]{3,2,1,0:T(8,128)} fusion(f32[2,2,128,256]{3,2,1,0:T(8,128)S(1)} %get-tuple-element.197, f32[2,2,128,256]{3,2,1,0:T(8,128)S(1)} %fusion.79, f32[2,2,128,256]{3,2,1,0:T(8,128)S(1)} %fusion.81, f32[2,2,128,256]{3,2,1,0:T(8,128)S(1)} %fusion.83, f32[2,2,128,256]{3,2,1,0:T(8,128)S(1)} %fusion.15, ...), kind=kOutput, calls=%fused_computation.21 | convolution fusion | flops 35520512 | bytes 5111828 | tf_op jit(solution)/shard_map/abxy,abyp->abxp/dot_general | solution.py:52
  163.6 2.5 %multiply_convert_fusion = bf16[2,2,8,128,128]{4,3,2,1,0:T(8,128)(2,1)} fusion(f32[2,2,128,128]{3,2,1,0:T(8,128)S(1)} %fusion.32, f32[2,2,128,128]{3,2,1,0:T(8,128)S(1)} %fusion.34, f32[2,2,128,128]{3,2,1,0:T(8,128)S(1)} %fusion.36, f32[2,2,128,128]{3,2,1,0:T(8,128)S(1)} %fusion.38, f32[2,2,128,128]{3,2,1,0:T(8,128)S(1)} %fusion.40, ...), kind=kLoop, calls=%fused_computation.9 | loop fusion | flops 9961472 | bytes 3408160 | tf_op jit(solution)/shard_map/convert_element_type | solution.py:136
  (178 shorter events, 49.8 us)
Async XLA Ops:
  9.6 11.3 %collective-permute-start.1 = (bf16[1,2,128,256]{3,2,1,0:T(8,128)(2,1)S(1)}, bf16[1,2,128,256]{3,2,1,0:T(8,128)(2,1)S(1)}, u32[]{:S(2)}, u32[]{:S(2)}) collective-permute-start(bf16[1,2,128,256]{3,2,1,0:T(8,128)(2,1)S(1)} %get-tuple-element.177), channel_id=1, source_target_pairs={{2,0},{4,2},{6,4},{8,6},{10,8},{12,10},{14,12},{16,14},{18,16},{20... | collective-permute-start | bytes 393224 | tf_op jit(solution)/shard_map/ppermute | solution.py:24
  9.7 11.3 %collective-permute-start = (bf16[1,2,128,256]{3,2,1,0:T(8,128)(2,1)S(1)}, bf16[1,2,128,256]{3,2,1,0:T(8,128)(2,1)S(1)}, u32[]{:S(2)}, u32[]{:S(2)}) collective-permute-start(bf16[1,2,128,256]{3,2,1,0:T(8,128)(2,1)S(1)} %get-tuple-element.176), channel_id=1, source_target_pairs={{0,2},{2,4},{4,6},{6,8},{8,10},{10,12},{12,14},{14,16},{16,18},{18... | collective-permute-start | bytes 393224 | tf_op jit(solution)/shard_map/ppermute | solution.py:21
  19.3 18.3 %collective-permute-start.12 = (f32[4,128,256]{2,1,0:T(8,128)S(1)}, f32[4,128,256]{2,1,0:T(8,128)S(1)}, u32[]{:S(2)}, u32[]{:S(2)}) collective-permute-start(f32[4,128,256]{2,1,0:T(8,128)S(1)} %slice_bitcast_fusion.8), channel_id=1, source_target_pairs={{0,30},{2,0},{4,2},{6,4},{8,6},{10,8},{12,10},{14,12},{16,14},{18,... | collective-permute-start | bytes 1572872 | tf_op jit(solution)/shard_map/ppermute | solution.py:12
  21.1 7.7 %collective-permute-start.2 = (bf16[4,1,128,256]{3,2,1,0:T(8,128)(2,1)S(1)}, bf16[4,1,128,256]{3,2,1,0:T(8,128)(2,1)S(1)}, u32[]{:S(2)}, u32[]{:S(2)}) collective-permute-start(bf16[4,1,128,256]{3,2,1,0:T(8,128)(2,1)S(1)} %get-tuple-element.169), channel_id=1, source_target_pairs={{0,1},{1,0},{2,3},{3,2},{4,5},{5,4},{6,7},{7,6},{8,9},{9,8},{10,11... | collective-permute-start | bytes 786440 | tf_op jit(solution)/shard_map/ppermute | solution.py:21
  22.6 11.7 %collective-permute-start.3 = (bf16[4,1,128,256]{3,2,1,0:T(8,128)(2,1)S(1)}, bf16[4,1,128,256]{3,2,1,0:T(8,128)(2,1)S(1)}, u32[]{:S(2)}, u32[]{:S(2)}) collective-permute-start(bf16[4,1,128,256]{3,2,1,0:T(8,128)(2,1)S(1)} %get-tuple-element.170), channel_id=1, source_target_pairs={{1,0},{0,1},{3,2},{2,3},{5,4},{4,5},{7,6},{6,7},{9,8},{8,9},{11,10... | collective-permute-start | bytes 786440 | tf_op jit(solution)/shard_map/ppermute | solution.py:24
  35.9 6.5 %collective-permute-start.5 = (bf16[1,2,128,256]{3,2,1,0:T(8,128)(2,1)S(1)}, bf16[1,2,128,256]{3,2,1,0:T(8,128)(2,1)S(1)}, u32[]{:S(2)}, u32[]{:S(2)}) collective-permute-start(bf16[1,2,128,256]{3,2,1,0:T(8,128)(2,1)S(1)} %get-tuple-element.175), channel_id=1, source_target_pairs={{2,0},{4,2},{6,4},{8,6},{10,8},{12,10},{14,12},{16,14},{18,16},{20... | collective-permute-start | bytes 393224 | tf_op jit(solution)/shard_map/ppermute | solution.py:24
  36.0 6.5 %collective-permute-start.4 = (bf16[1,2,128,256]{3,2,1,0:T(8,128)(2,1)S(1)}, bf16[1,2,128,256]{3,2,1,0:T(8,128)(2,1)S(1)}, u32[]{:S(2)}, u32[]{:S(2)}) collective-permute-start(bf16[1,2,128,256]{3,2,1,0:T(8,128)(2,1)S(1)} %get-tuple-element.174), channel_id=1, source_target_pairs={{0,2},{2,4},{4,6},{6,8},{8,10},{10,12},{12,14},{14,16},{16,18},{18... | collective-permute-start | bytes 393224 | tf_op jit(solution)/shard_map/ppermute | solution.py:21
  37.8 10.2 %collective-permute-start.13 = (f32[4,128,256]{2,1,0:T(8,128)S(1)}, f32[4,128,256]{2,1,0:T(8,128)S(1)}, u32[]{:S(2)}, u32[]{:S(2)}) collective-permute-start(f32[4,128,256]{2,1,0:T(8,128)S(1)} %slice_bitcast_fusion.6), channel_id=1, source_target_pairs={{0,2},{2,4},{4,6},{6,8},{8,10},{10,12},{12,14},{14,16},{16,18},{18... | collective-permute-start | bytes 1572872 | tf_op jit(solution)/shard_map/ppermute | solution.py:12
  42.8 8.1 %collective-permute-start.6 = (bf16[4,1,128,256]{3,2,1,0:T(8,128)(2,1)S(1)}, bf16[4,1,128,256]{3,2,1,0:T(8,128)(2,1)S(1)}, u32[]{:S(2)}, u32[]{:S(2)}) collective-permute-start(bf16[4,1,128,256]{3,2,1,0:T(8,128)(2,1)S(1)} %get-tuple-element.165), channel_id=1, source_target_pairs={{0,1},{1,0},{2,3},{3,2},{4,5},{5,4},{6,7},{7,6},{8,9},{9,8},{10,11... | collective-permute-start | bytes 786440 | tf_op jit(solution)/shard_map/ppermute | solution.py:21
  44.3 12.1 %collective-permute-start.7 = (bf16[4,1,128,256]{3,2,1,0:T(8,128)(2,1)S(1)}, bf16[4,1,128,256]{3,2,1,0:T(8,128)(2,1)S(1)}, u32[]{:S(2)}, u32[]{:S(2)}) collective-permute-start(bf16[4,1,128,256]{3,2,1,0:T(8,128)(2,1)S(1)} %get-tuple-element.166), channel_id=1, source_target_pairs={{1,0},{0,1},{3,2},{2,3},{5,4},{4,5},{7,6},{6,7},{9,8},{8,9},{11,10... | collective-permute-start | bytes 786440 | tf_op jit(solution)/shard_map/ppermute | solution.py:24
  48.2 13.9 %collective-permute-start.14 = (f32[2,128,256]{2,1,0:T(8,128)S(1)}, f32[2,128,256]{2,1,0:T(8,128)S(1)}, u32[]{:S(2)}, u32[]{:S(2)}) collective-permute-start(f32[2,128,256]{2,1,0:T(8,128)S(1)} %slice_bitcast_fusion.17), channel_id=1, source_target_pairs={{0,1},{1,0},{2,3},{3,2},{4,5},{5,4},{6,7},{7,6},{8,9},{9,8},{10,11... | collective-permute-start | bytes 786440 | tf_op jit(solution)/shard_map/ppermute | solution.py:12
  62.1 9.2 %collective-permute-start.15 = (f32[2,128,256]{2,1,0:T(8,128)S(1)}, f32[2,128,256]{2,1,0:T(8,128)S(1)}, u32[]{:S(2)}, u32[]{:S(2)}) collective-permute-start(f32[2,128,256]{2,1,0:T(8,128)S(1)} %slice_bitcast_fusion.15), channel_id=1, source_target_pairs={{0,1},{1,0},{2,3},{3,2},{4,5},{5,4},{6,7},{7,6},{8,9},{9,8},{10,11... | collective-permute-start | bytes 786440 | tf_op jit(solution)/shard_map/ppermute | solution.py:12
  75.0 12.4 %collective-permute-start.16 = (f32[4,128,256]{2,1,0:T(8,128)S(1)}, f32[4,128,256]{2,1,0:T(8,128)S(1)}, u32[]{:S(2)}, u32[]{:S(2)}) collective-permute-start(f32[4,128,256]{2,1,0:T(8,128)S(1)} %slice_bitcast_fusion.5), channel_id=1, source_target_pairs={{0,30},{2,0},{4,2},{6,4},{8,6},{10,8},{12,10},{14,12},{16,14},{18,... | collective-permute-start | bytes 1572872 | tf_op jit(solution)/shard_map/ppermute | solution.py:12
  87.5 10.2 %collective-permute-start.17 = (f32[4,128,256]{2,1,0:T(8,128)S(1)}, f32[4,128,256]{2,1,0:T(8,128)S(1)}, u32[]{:S(2)}, u32[]{:S(2)}) collective-permute-start(f32[4,128,256]{2,1,0:T(8,128)S(1)} %slice_bitcast_fusion.3), channel_id=1, source_target_pairs={{0,2},{2,4},{4,6},{6,8},{8,10},{10,12},{12,14},{14,16},{16,18},{18... | collective-permute-start | bytes 1572872 | tf_op jit(solution)/shard_map/ppermute | solution.py:12
  87.9 11.5 %collective-permute-start.9 = (bf16[1,2,128,256]{3,2,1,0:T(8,128)(2,1)S(1)}, bf16[1,2,128,256]{3,2,1,0:T(8,128)(2,1)S(1)}, u32[]{:S(2)}, u32[]{:S(2)}) collective-permute-start(bf16[1,2,128,256]{3,2,1,0:T(8,128)(2,1)S(1)} %get-tuple-element.173), channel_id=1, source_target_pairs={{2,0},{4,2},{6,4},{8,6},{10,8},{12,10},{14,12},{16,14},{18,16},{20... | collective-permute-start | bytes 393224 | tf_op jit(solution)/shard_map/ppermute | solution.py:24
  89.8 9.6 %collective-permute-start.8 = (bf16[1,2,128,256]{3,2,1,0:T(8,128)(2,1)S(1)}, bf16[1,2,128,256]{3,2,1,0:T(8,128)(2,1)S(1)}, u32[]{:S(2)}, u32[]{:S(2)}) collective-permute-start(bf16[1,2,128,256]{3,2,1,0:T(8,128)(2,1)S(1)} %get-tuple-element.172), channel_id=1, source_target_pairs={{0,2},{2,4},{4,6},{6,8},{8,10},{10,12},{12,14},{14,16},{16,18},{18... | collective-permute-start | bytes 393224 | tf_op jit(solution)/shard_map/ppermute | solution.py:21
  97.8 9.3 %collective-permute-start.18 = (f32[2,128,256]{2,1,0:T(8,128)S(1)}, f32[2,128,256]{2,1,0:T(8,128)S(1)}, u32[]{:S(2)}, u32[]{:S(2)}) collective-permute-start(f32[2,128,256]{2,1,0:T(8,128)S(1)} %slice_bitcast_fusion.14), channel_id=1, source_target_pairs={{0,1},{1,0},{2,3},{3,2},{4,5},{5,4},{6,7},{7,6},{8,9},{9,8},{10,11... | collective-permute-start | bytes 786440 | tf_op jit(solution)/shard_map/ppermute | solution.py:12
  99.5 23.3 %collective-permute-start.10 = (bf16[4,1,128,256]{3,2,1,0:T(8,128)(2,1)S(1)}, bf16[4,1,128,256]{3,2,1,0:T(8,128)(2,1)S(1)}, u32[]{:S(2)}, u32[]{:S(2)}) collective-permute-start(bf16[4,1,128,256]{3,2,1,0:T(8,128)(2,1)S(1)} %get-tuple-element.161), channel_id=1, source_target_pairs={{0,1},{1,0},{2,3},{3,2},{4,5},{5,4},{6,7},{7,6},{8,9},{9,8},{10,11... | collective-permute-start | bytes 786440 | tf_op jit(solution)/shard_map/ppermute | solution.py:21
  100.8 22.0 %collective-permute-start.11 = (bf16[4,1,128,256]{3,2,1,0:T(8,128)(2,1)S(1)}, bf16[4,1,128,256]{3,2,1,0:T(8,128)(2,1)S(1)}, u32[]{:S(2)}, u32[]{:S(2)}) collective-permute-start(bf16[4,1,128,256]{3,2,1,0:T(8,128)(2,1)S(1)} %get-tuple-element.162), channel_id=1, source_target_pairs={{1,0},{0,1},{3,2},{2,3},{5,4},{4,5},{7,6},{6,7},{9,8},{8,9},{11,10... | collective-permute-start | bytes 786440 | tf_op jit(solution)/shard_map/ppermute | solution.py:24
  107.2 10.8 %collective-permute-start.19 = (f32[2,128,256]{2,1,0:T(8,128)S(1)}, f32[2,128,256]{2,1,0:T(8,128)S(1)}, u32[]{:S(2)}, u32[]{:S(2)}) collective-permute-start(f32[2,128,256]{2,1,0:T(8,128)S(1)} %slice_bitcast_fusion.12), channel_id=1, source_target_pairs={{0,1},{1,0},{2,3},{3,2},{4,5},{5,4},{6,7},{7,6},{8,9},{9,8},{10,11... | collective-permute-start | bytes 786440 | tf_op jit(solution)/shard_map/ppermute | solution.py:12
  122.3 12.9 %collective-permute-start.20 = (f32[4,128,256]{2,1,0:T(8,128)S(1)}, f32[4,128,256]{2,1,0:T(8,128)S(1)}, u32[]{:S(2)}, u32[]{:S(2)}) collective-permute-start(f32[4,128,256]{2,1,0:T(8,128)S(1)} %slice_bitcast_fusion.2), channel_id=1, source_target_pairs={{0,30},{2,0},{4,2},{6,4},{8,6},{10,8},{12,10},{14,12},{16,14},{18,... | collective-permute-start | bytes 1572872 | tf_op jit(solution)/shard_map/ppermute | solution.py:12
  135.3 9.0 %collective-permute-start.21 = (f32[4,128,256]{2,1,0:T(8,128)S(1)}, f32[4,128,256]{2,1,0:T(8,128)S(1)}, u32[]{:S(2)}, u32[]{:S(2)}) collective-permute-start(f32[4,128,256]{2,1,0:T(8,128)S(1)} %slice_bitcast_fusion), channel_id=1, source_target_pairs={{0,2},{2,4},{4,6},{6,8},{8,10},{10,12},{12,14},{14,16},{16,18},{18... | collective-permute-start | bytes 1572872 | tf_op jit(solution)/shard_map/ppermute | solution.py:12
  144.5 7.1 %collective-permute-start.22 = (f32[2,128,256]{2,1,0:T(8,128)S(1)}, f32[2,128,256]{2,1,0:T(8,128)S(1)}, u32[]{:S(2)}, u32[]{:S(2)}) collective-permute-start(f32[2,128,256]{2,1,0:T(8,128)S(1)} %slice_bitcast_fusion.11), channel_id=1, source_target_pairs={{0,1},{1,0},{2,3},{3,2},{4,5},{5,4},{6,7},{7,6},{8,9},{9,8},{10,11... | collective-permute-start | bytes 786440 | tf_op jit(solution)/shard_map/ppermute | solution.py:12
  151.6 6.4 %collective-permute-start.23 = (f32[2,128,256]{2,1,0:T(8,128)S(1)}, f32[2,128,256]{2,1,0:T(8,128)S(1)}, u32[]{:S(2)}, u32[]{:S(2)}) collective-permute-start(f32[2,128,256]{2,1,0:T(8,128)S(1)} %slice_bitcast_fusion.9), channel_id=1, source_target_pairs={{0,1},{1,0},{2,3},{3,2},{4,5},{5,4},{6,7},{7,6},{8,9},{9,8},{10,11... | collective-permute-start | bytes 786440 | tf_op jit(solution)/shard_map/ppermute | solution.py:12
  (6 other events, 9.6 us)
where the time goes:
time: 166 us
  waiting for transfers between devices  91 us (55%)
  matrix products  30.5 us (18%)
  starting transfers between devices  26.5 us (16%)
  other arithmetic  9.94 us (6%)
  local copies, waits for them, and re-layouts  6.4 us (4%)
  between operations  1.67 us (1%)
    ppermute x12, waiting for transfers between devices, shifted(): return lax.ppermute(value, axis, pairs)  73.5 us
    ppermute x12, starting transfers between devices, shifted(): return lax.ppermute(value, axis, pairs)  16.2 us
    dot_general x27, matrix products, push_transpose(): jnp.einsum('abyx,abyp->abxp', selected[:, :, offset_code], adjoint_bf16,...  12.9 us
    dot_general x36, matrix products, forward_apply(): jnp.einsum('abxy,abyp->abxp', selected[:, :, offset_code], window, prefer...  11.9 us
    ppermute x6, waiting for transfers between devices, padded_2(): lax.ppermute(lax.slice_in_dim(block, 0, width, axis=dim), axis, backward)  11.2 us
    ppermute x6, starting transfers between devices, padded_2(): lax.ppermute(lax.slice_in_dim(block, block.shape[dim] - width, None, axis...  6.36 us
    ppermute x6, waiting for transfers between devices, padded_2(): lax.ppermute(lax.slice_in_dim(block, block.shape[dim] - width, None, axis...  6.25 us
    dot_general x9, matrix products, shards(): jnp.einsum('abxq,abyq->abxy', adjoint_stack, window, preferred_element_ty...  3.97 us
  transfers between devices with their start and end apart: 24, of which 15 were waited for; matrix products, arithmetic and copies ran while one was open for 16% of the time, Pallas kernels for 0%

commit v1 on v0

--- a/solution.py
+++ b/solution.py
@@ -1,6 +1,10 @@
+import functools
+
 import jax
 import jax.numpy as jnp
 from jax import lax
+from jax.experimental import pallas as pl
+from jax.experimental.pallas import tpu as pltpu
 from jax.sharding import PartitionSpec as P
 
 offset_table = tuple(((offset_code // 3 - 1, offset_code % 3 - 1) for offset_code in range(9)))
@@ -81,7 +85,7 @@
     return middle[:, 1 : rows_y + 1]
 
 
-def shards(hamiltonian, neighbours, probe_seeds, coefficients, cotangent):
+def any_shards(hamiltonian, neighbours, probe_seeds, coefficients, cotangent):
     rows_x, rows_y = (hamiltonian.shape[0], hamiltonian.shape[1])
     width = hamiltonian.shape[3]
     probes = cotangent.shape[3]
@@ -136,6 +140,343 @@
     return (density, (gradient * (1.0 / probes)).astype(jnp.bfloat16))
 
 
+bf16 = jnp.bfloat16
+f32 = jnp.float32
+VMEM_BYTES = 48 * 1024 * 1024
+
+
+def swap_y(value):
+    return lax.ppermute(value, "gy", [(0, 1), (1, 0)])
+
+
+def swap_near(value):
+    count = lax.axis_size("gx")
+    return lax.ppermute(value, "gx", [(i, i ^ 1) for i in range(count)])
+
+
+def swap_far(value):
+    count = lax.axis_size("gx")
+    pairs = [(i, (i + 1) % count if i % 2 else (i - 1) % count) for i in range(count)]
+    return lax.ppermute(value, "gx", pairs)
+
+
+def load_window(parts, window, sems):
+    copies = [
+        pltpu.make_async_copy(part, window.at[pl.ds(4 * at, 4)], sems.at[at])
+        for at, part in enumerate(parts)
+    ]
+    for copy in copies:
+        copy.start()
+    for copy in copies:
+        copy.wait()
+
+
+def window_product(slots, step, h_ref, window, listed):
+    total = None
+    for k in range(0, listed, 2):
+        left = jnp.concatenate([h_ref[0, 0, k], h_ref[0, 0, k + 1]], axis=1)
+        right = jnp.concatenate(
+            [window[slots[step * listed + k]], window[slots[step * listed + k + 1]]], axis=0
+        )
+        part = jnp.dot(left, right, preferred_element_type=f32)
+        total = part if total is None else total + part
+    return total
+
+
+def first_forward_kernel(listed, rows, slots, h_ref, w_ref, term_ref, rounded_ref):
+    value = window_product(slots, pl.program_id(0), h_ref, w_ref, listed)
+    term_ref[0] = value
+    rounded_ref[0] = value.astype(bf16)
+
+
+def next_forward_kernel(
+    index, last, listed, rows, slots, coef, h_ref, far, outer, inner, near, before_ref, *rest
+):
+    refs = list(rest)
+    sums_ref = refs.pop(0)
+    if index == 2:
+        sums_ref, first_ref = None, sums_ref
+    if last:
+        density_ref, window, sems = refs
+    else:
+        term_ref, rounded_ref, density_ref, window, sems = refs
+    step = pl.program_id(0)
+
+    @pl.when(step == 0)
+    def _():
+        load_window((far, outer, inner, near), window, sems)
+
+    before = before_ref[0].astype(f32)
+    value = 2.0 * window_product(slots, step, h_ref, window, listed) - before
+    if index == 2:
+        sums = coef[0] * before + coef[1] * first_ref[0]
+    else:
+        sums = sums_ref[0]
+    sums = sums + coef[index] * value
+    if last:
+        density_ref[0, 0] = sums
+    else:
+        term_ref[0] = value
+        rounded_ref[0] = value.astype(bf16)
+        density_ref[0] = sums
+
+
+def push(slots, step, h_ref, adjoint_t, sums, listed):
+    wide = jnp.concatenate([h_ref[0, 0, k] for k in range(listed)], axis=1)
+    product = jnp.dot(adjoint_t, wide, preferred_element_type=f32)
+    width = wide.shape[0]
+    for k in range(listed):
+        slot = slots[step * listed + k]
+        sums[slot] += product[:, k * width : (k + 1) * width]
+
+
+def finish_push(far_ref, near_ref, middle_ref, sums):
+    far_ref[...] = sums[0:4].astype(bf16)
+    near_ref[...] = sums[12:16].astype(bf16)
+    middle_ref[...] = sums[4:12]
+
+
+def first_adjoint_kernel(
+    top, listed, rows, slots, coef, h_ref, cot_ref, cot_t_ref, value_ref, rounded_ref, far_ref, near_ref, middle_ref, sums
+):
+    step = pl.program_id(0)
+
+    @pl.when(step == 0)
+    def _():
+        sums[...] = jnp.zeros_like(sums)
+
+    cot = cot_ref[0, 0].astype(f32)
+    rounded_ref[0] = (coef[top] * cot).astype(bf16)
+    cot_t = jnp.transpose(cot)
+    cot_t_ref[0] = cot_t.astype(bf16)
+    value = coef[top] * cot_t
+    value_ref[0] = value
+    push(slots, step, h_ref, value.astype(bf16), sums, listed)
+
+    @pl.when(step == pl.num_programs(0) - 1)
+    def _():
+        finish_push(far_ref, near_ref, middle_ref, sums)
+
+
+def adjoint_value(index, coef, cot_t_ref, own_ref, came_ref, across_ref):
+    carried = own_ref[0] + came_ref[0].astype(f32) + across_ref[0].astype(f32)
+    return coef[index] * cot_t_ref[0].astype(f32) + 2.0 * carried
+
+
+def next_adjoint_kernel(
+    index, listed, has_older, rows, slots, coef, h_ref, cot_t_ref, own_ref, came_ref, across_ref, *rest
+):
+    refs = list(rest)
+    older_ref = refs.pop(0) if has_older else None
+    value_ref, rounded_ref, far_ref, near_ref, middle_ref, sums = refs
+    step = pl.program_id(0)
+
+    @pl.when(step == 0)
+    def _():
+        sums[...] = jnp.zeros_like(sums)
+
+    value = adjoint_value(index, coef, cot_t_ref, own_ref, came_ref, across_ref)
+    if has_older:
+        value = value - older_ref[0]
+    value_ref[0] = value
+    rounded_ref[0] = jnp.transpose(value).astype(bf16)
+    push(slots, step, h_ref, value.astype(bf16), sums, listed)
+
+    @pl.when(step == pl.num_programs(0) - 1)
+    def _():
+        finish_push(far_ref, near_ref, middle_ref, sums)
+
+
+def gradient_kernel(
+    terms, listed, scale, rows, slots, coef, cot_t_ref, own_ref, came_ref, across_ref, older_ref, *rest
+):
+    refs = list(rest)
+    adjoints = refs[: terms - 2]
+    start = refs[terms - 2]
+    later = refs[terms - 1 : terms - 1 + 4 * (terms - 2)]
+    grad_ref, window, sems = refs[terms - 1 + 4 * (terms - 2) :]
+    step = pl.program_id(0)
+
+    @pl.when(step == 0)
+    def _():
+        copies = [pltpu.make_async_copy(start, window.at[0], sems.at[0])]
+        for t in range(terms - 2):
+            for at in range(4):
+                copies.append(
+                    pltpu.make_async_copy(
+                        later[4 * t + at], window.at[t + 1, pl.ds(4 * at, 4)], sems.at[1 + 4 * t + at]
+                    )
+                )
+        for copy in copies:
+            copy.start()
+        for copy in copies:
+            copy.wait()
+
+    value = adjoint_value(1, coef, cot_t_ref, own_ref, came_ref, across_ref) - older_ref[0]
+    first = jnp.transpose(value).astype(bf16)
+    left = jnp.concatenate([first] + [a[0] * bf16(2.0) for a in adjoints], axis=1)
+    for k in range(listed):
+        slot = slots[step * listed + k]
+        right = jnp.concatenate([window[t, slot] for t in range(terms - 1)], axis=1)
+        total = lax.dot_general(left, right, (((1,), (1,)), ((), ())), preferred_element_type=f32)
+        grad_ref[0, 0, k] = (total * scale).astype(bf16)
+
+
+def pair_shards(hamiltonian, neighbours, probe_seeds, coefficients, cotangent):
+    rows_x, rows_y, listed, width = hamiltonian.shape[:4]
+    probes = cotangent.shape[3]
+    terms = coefficients.shape[0]
+    span_x = rows_x * lax.axis_size("gx")
+    span_y = rows_y * lax.axis_size("gy")
+    odd = lax.axis_index("gx") % 2
+    sign = 1 - 2 * odd
+    four = jnp.arange(4, dtype=jnp.int32)
+    local_row = jnp.where(odd == 0, four - 1, 2 - four)
+    place_x = (lax.axis_index("gx") * rows_x + local_row) % span_x
+    place_y = (lax.axis_index("gy") * rows_y + four) % span_y
+    orbital = jnp.arange(width, dtype=jnp.int32)
+    global_rows = (place_x[:, None] * span_y + place_y).reshape(16)[:, None] * width + orbital
+    start = probe_signs(global_rows, probe_seeds).astype(bf16)
+    rows = jnp.stack([odd, 1 - odd]).astype(jnp.int32)
+    codes = jnp.where(odd == 0, neighbours, neighbours[::-1])
+    window_row = 1 + jnp.arange(2, dtype=jnp.int32)[:, None, None] + sign * (codes // 3 - 1)
+    window_col = (jnp.arange(2, dtype=jnp.int32)[None, :, None] + codes % 3 - 1) % 4
+    slots = (window_row * 4 + window_col).reshape(-1).astype(jnp.int32)
+
+    blocks = rows_x * rows_y
+    whole = lambda *shape: pl.BlockSpec(shape, lambda g, *_: (0,) * len(shape))
+    h_spec = pl.BlockSpec(
+        (1, 1, listed, width, width), lambda g, rows, *_: (rows[g // 2], g % 2, 0, 0, 0)
+    )
+    f_spec = pl.BlockSpec((1, width, probes), lambda g, *_: (g, 0, 0))
+    t_spec = pl.BlockSpec((1, probes, width), lambda g, *_: (g, 0, 0))
+    natural_spec = pl.BlockSpec((1, 1, width, probes), lambda g, rows, *_: (rows[g // 2], g % 2, 0, 0))
+    any_spec = pl.BlockSpec(memory_space=pl.ANY)
+    fields = jax.ShapeDtypeStruct((blocks, width, probes), bf16)
+    fields_f32 = jax.ShapeDtypeStruct((blocks, width, probes), f32)
+    turned = jax.ShapeDtypeStruct((blocks, probes, width), bf16)
+    turned_f32 = jax.ShapeDtypeStruct((blocks, probes, width), f32)
+    apply_flops = 2 * blocks * listed * width * width * probes
+
+    def call(kernel, scalars, in_specs, operands, out_specs, out_shape, scratch, flops, name):
+        return pl.pallas_call(
+            kernel,
+            grid_spec=pltpu.PrefetchScalarGridSpec(
+                num_scalar_prefetch=len(scalars),
+                grid=(blocks,),
+                in_specs=in_specs,
+                out_specs=out_specs,
+                scratch_shapes=scratch,
+            ),
+            out_shape=out_shape,
+            compiler_params=pltpu.CompilerParams(
+                dimension_semantics=("arbitrary",), vmem_limit_bytes=VMEM_BYTES
+            ),
+            cost_estimate=pl.CostEstimate(
+                flops=flops, bytes_accessed=4 * 1024 * 1024, transcendentals=0
+            ),
+            name=name,
+        )(*scalars, *operands)
+
+    window_scratch = [
+        pltpu.VMEM((16, width, probes), bf16),
+        pltpu.SemaphoreType.DMA((4,)),
+    ]
+    sums_scratch = [pltpu.VMEM((16, probes, width), f32)]
+
+    term, rounded = call(
+        functools.partial(first_forward_kernel, listed),
+        (rows, slots), [h_spec, whole(16, width, probes)], (hamiltonian, start),
+        [f_spec, f_spec], [fields_f32, fields], [], apply_flops, "forward_1",
+    )
+    push_specs = [whole(4, probes, width), whole(4, probes, width), whole(8, probes, width)]
+    row_t = jax.ShapeDtypeStruct((4, probes, width), bf16)
+    push_shapes = [row_t, row_t, jax.ShapeDtypeStruct((8, probes, width), f32)]
+    top = terms - 1
+    cot_t, value, adj_rounded, to_far, to_near, middle = call(
+        functools.partial(first_adjoint_kernel, top, listed),
+        (rows, slots, coefficients), [h_spec, natural_spec], (hamiltonian, cotangent),
+        [t_spec, t_spec, f_spec] + push_specs, [turned, turned_f32, fields] + push_shapes,
+        sums_scratch, apply_flops, "adjoint_top",
+    )
+    adjoints = {top: value}
+    adjoints_rounded = {top: adj_rounded}
+    values = {0: start[4:12].reshape(2, 4, width, probes)[:, :2].reshape(4, width, probes), 1: term}
+    windows = []
+    density = None
+    for index in range(2, terms):
+        across = swap_y(rounded)
+        outer = jnp.concatenate([rounded[:2], across[:2]])
+        inner = jnp.concatenate([rounded[2:], across[2:]])
+        near = swap_near(inner)
+        far = swap_far(outer)
+        from_far = swap_far(to_far)
+        from_near = swap_near(to_near)
+        came = jnp.concatenate([from_far, from_near])
+        total = middle + came.astype(f32)
+        to_across = jnp.concatenate([total[2:4], total[6:8]]).astype(bf16)
+        from_across = swap_y(to_across)
+        own = jnp.concatenate([middle[:2], middle[4:6]])
+        came_own = jnp.concatenate([came[:2], came[4:6]])
+
+        windows.append((far, outer, inner, near))
+        last = index == terms - 1
+        sums = values[1] if index == 2 else density
+        out = call(
+            functools.partial(next_forward_kernel, index, last, listed),
+            (rows, slots, coefficients),
+            [h_spec] + [any_spec] * 4 + [f_spec, f_spec],
+            (hamiltonian, far, outer, inner, near, values[index - 2], sums),
+            [natural_spec] if last else [f_spec, f_spec, f_spec],
+            [jax.ShapeDtypeStruct(cotangent.shape, f32)] if last else [fields_f32, fields, fields_f32],
+            window_scratch, apply_flops, "forward_next",
+        )
+        if last:
+            density = out[0]
+        else:
+            values[index], rounded, density = out
+        at = terms - index
+        if at > 1:
+            has_older = at + 2 < terms
+            out = call(
+                functools.partial(next_adjoint_kernel, at, listed, has_older),
+                (rows, slots, coefficients),
+                [h_spec] + [t_spec] * (5 if has_older else 4),
+                (hamiltonian, cot_t, own, came_own, from_across)
+                + ((adjoints[at + 2],) if has_older else ()),
+                [t_spec, f_spec] + push_specs, [turned_f32, fields] + push_shapes,
+                sums_scratch, apply_flops, "adjoint_next",
+            )
+            adjoints[at], adjoints_rounded[at], to_far, to_near, middle = out
+    (gradient,) = call(
+        functools.partial(gradient_kernel, terms, listed, 1.0 / probes),
+        (rows, slots, coefficients),
+        [t_spec] * 5 + [f_spec] * (terms - 2) + [any_spec] * (1 + 4 * (terms - 2)),
+        (cot_t, own, came_own, from_across, adjoints[3])
+        + tuple(adjoints_rounded[t] for t in range(2, terms))
+        + (start,) + tuple(part for window in windows for part in window),
+        [h_spec], [jax.ShapeDtypeStruct(hamiltonian.shape, bf16)],
+        [
+            pltpu.VMEM((terms - 1, 16, width, probes), bf16),
+            pltpu.SemaphoreType.DMA((1 + 4 * (terms - 2),)),
+        ],
+        (terms - 1) * apply_flops, "gradient",
+    )
+    return density, gradient
+
+
+def shards(hamiltonian, neighbours, probe_seeds, coefficients, cotangent):
+    paired = (
+        hamiltonian.shape[:2] == (2, 2)
+        and lax.axis_size("gy") == 2
+        and lax.axis_size("gx") % 2 == 0
+        and hamiltonian.shape[2] % 2 == 0
+        and coefficients.shape[0] > 3
+    )
+    run = pair_shards if paired else any_shards
+    return run(hamiltonian, neighbours, probe_seeds, coefficients, cotangent)
+
+
 def solution(mesh):
     placed = (
         P("gx", "gy", None, None, None),

time: 166 us -> 83.3 us (0.50)
  the two profiles are of different devices: /device:TPU:28 before, /device:TPU:1 now
where the time goes in v1:
time: 83.3 us; the launch traced here: 83 us
  waiting for transfers between devices  25.7 us (31%)
  starting transfers between devices  24 us (29%)
  Pallas kernels  23.2 us (28%)
  local copies, waits for them, and re-layouts  5.22 us (6%)
  other arithmetic  3.79 us (5%)
  between operations  1.06 us (1%)
    pallas_call x8, Pallas kernels, call(): pl.pallas_call(kernel, grid_spec=pltpu.PrefetchScalarGridSpec(num_scalar_...  23.2 us
    ppermute x6, waiting for transfers between devices, swap_y(): return lax.ppermute(value, 'gy', [(0, 1), (1, 0)])  16.1 us
    ppermute x6, starting transfers between devices, swap_near(): return lax.ppermute(value, 'gx', [(i, i ^ 1) for i in range(count)])  10.7 us
    ppermute x6, starting transfers between devices, swap_y(): return lax.ppermute(value, 'gy', [(0, 1), (1, 0)])  9.64 us
    ppermute x6, waiting for transfers between devices, swap_far(): return lax.ppermute(value, 'gx', pairs)  9.58 us
    ppermute x6, starting transfers between devices, swap_far(): return lax.ppermute(value, 'gx', pairs)  3.61 us
    unnamed x14, local copies, waits for them, and re-layouts  2.85 us
    slice x6, local copies, waits for them, and re-layouts, pair_shards(): came_own = jnp.concatenate([came[:2], came[4:6]])  1.87 us
  transfers between devices with their start and end apart: 18, of which 7 were waited for; matrix products, arithmetic and copies ran while one was open for 6% of the time, Pallas kernels for 17%

profile of v1, /device:TPU:1, one launch (start us, length us, event | category | flops | bytes accessed | tf_op | source)
XLA Modules:
  0.0 83.0 jit_solution(7712005285602954559)
XLA Ops:
  4.5 3.1 %adjoint_top.1 = (bf16[4,256,128]{2,1,0:T(8,128)(2,1)S(1)}, f32[4,256,128]{2,1,0:T(8,128)S(1)}, bf16[4,128,256]{2,1,0:T(8,128)(2,1)S(1)}, bf16[4,256,128]{2,1,0:...) custom-call(s32[2]{0:T(128)S(1)} %pad_add_fusion.rows, s32[32]{0:T(128)S(1)} %reshape.94.slots, ...), custom_call_target="tpu_custom_call" | custom-call | flops 268435456 | bytes 4194304 | tf_op jit(solution)/shard_map/adjoint_top/pallas_call | solution.py:362
  7.6 2.6 %collective-permute-start.9 = (bf16[4,256,128]{2,1,0:T(8,128)(2,1)S(1)}, bf16[4,256,128]{2,1,0:T(8,128)(2,1)}, u32[]{:S(2)}, u32[]{:S(2)}) collective-permute-start(bf16[4,256,128]{2,1,0:T(8,128)(2,1)S(1)} %get-tuple-element.33), channel_id=1, source_target_pairs={{0,30},{2,4},{4,2},{6,8},{8,6},{10,12},{12,10},{14,16},{16,14},{18... | collective-permute-start | bytes 786440 | tf_op jit(solution)/shard_map/ppermute | solution.py:160
  11.4 1.6 %forward_1.1 = (f32[4,128,256]{2,1,0:T(8,128)S(1)}, bf16[4,128,256]{2,1,0:T(8,128)(2,1)S(1)}) custom-call(s32[2]{0:T(128)S(1)} %pad_add_fusion.rows, s32[32]{0:T(128)S(1)} %reshape.94.slots, bf16[2,2,8,128,128]{4,3,2,1,0:T(8,128)(2,1)S(1)} %copy-done.1, bf16[16,128,256]{2,1,0:T(8,128)(2,1)S(1)} %fusion.6.w_ref.rest_3_), custom_call_target="tpu_custom_call" | custom-call | flops 268435456 | bytes 4194304 | tf_op jit(solution)/shard_map/forward_1/pallas_call | solution.py:362
  13.0 1.3 %collective-permute-start = (bf16[4,128,256]{2,1,0:T(8,128)(2,1)S(1)}, bf16[4,128,256]{2,1,0:T(8,128)(2,1)S(1)}, u32[]{:S(2)}, u32[]{:S(2)}) collective-permute-start(bf16[4,128,256]{2,1,0:T(8,128)(2,1)S(1)} %get-tuple-element.24), channel_id=1, source_target_pairs={{0,1},{1,0},{2,3},{3,2},{4,5},{5,4},{6,7},{7,6},{8,9},{9,8},{10,11... | collective-permute-start | bytes 786440 | tf_op jit(solution)/shard_map/ppermute | solution.py:149
  14.5 1.9 %collective-permute-done.9 = bf16[4,256,128]{2,1,0:T(8,128)(2,1)} collective-permute-done((bf16[4,256,128]{2,1,0:T(8,128)(2,1)S(1)}, bf16[4,256,128]{2,1,0:T(8,128)(2,1)}, u32[]{:S(2)}, u32[]{:S(2)}) %collective-permute-start.9) | collective-permute-done | bytes 262176 | tf_op jit(solution)/shard_map/ppermute | solution.py:160
  17.5 2.7 %collective-permute-start.11 = (bf16[4,256,128]{2,1,0:T(8,128)(2,1)S(1)}, bf16[4,256,128]{2,1,0:T(8,128)(2,1)S(1)}, u32[]{:S(2)}, u32[]{:S(2)}) collective-permute-start(bf16[4,256,128]{2,1,0:T(8,128)(2,1)S(1)} %pad_maximum_fusion.10), channel_id=1, source_target_pairs={{0,1},{1,0},{2,3},{3,2},{4,5},{5,4},{6,7},{7,6},{8,9},{9,8},{10,11... | collective-permute-start | bytes 786440 | tf_op jit(solution)/shard_map/ppermute | solution.py:149
  20.3 3.8 %collective-permute-start.2 = (bf16[4,128,256]{2,1,0:T(8,128)(2,1)S(1)}, bf16[4,128,256]{2,1,0:T(8,128)(2,1)S(1)}, u32[]{:S(2)}, u32[]{:S(2)}) collective-permute-start(bf16[4,128,256]{2,1,0:T(8,128)(2,1)S(1)} %pad_maximum_fusion.4.inner.rest_6_), channel_id=1, source_target_pairs={{0,2},{2,0},{4,6},{6,4},{8,10},{10,8},{12,14},{14,12},{16,18},{18,... | collective-permute-start | bytes 786440 | tf_op jit(solution)/shard_map/ppermute | solution.py:154
  27.2 2.2 %adjoint_next.2 = (f32[4,256,128]{2,1,0:T(8,128)S(1)}, bf16[4,128,256]{2,1,0:T(8,128)(2,1)S(1)}, bf16[4,256,128]{2,1,0:T(8,128)(2,1)S(1)}, bf16[4,256,128]{2,1,0:T(8,128)(2,1)S(1)}, f32[8,256,128]{2,1,0:T(8,128)S(1)}) custom-call(s32[2]{0:T(128)S(1)} %pad_add_fusion.rows, s32[32]{0:T(128)S(1)} %reshape.94.slots, f32[5]{0:T(128)S(1)} %copy-done.5, ...), custom_call_target="tpu_custom_call" | custom-call | flops 268435456 | bytes 4194304 | tf_op jit(solution)/shard_map/adjoint_next/pallas_call | solution.py:362
  30.2 3.0 %collective-permute-start.13 = (bf16[4,256,128]{2,1,0:T(8,128)(2,1)S(1)}, bf16[4,256,128]{2,1,0:T(8,128)(2,1)S(1)}, u32[]{:S(2)}, u32[]{:S(2)}) collective-permute-start(bf16[4,256,128]{2,1,0:T(8,128)(2,1)S(1)} %get-tuple-element.37), channel_id=1, source_target_pairs={{0,2},{2,0},{4,6},{6,4},{8,10},{10,8},{12,14},{14,12},{16,18},{18,... | collective-permute-start | bytes 786440 | tf_op jit(solution)/shard_map/ppermute | solution.py:154
  33.3 1.7 %forward_next.3 = (f32[4,128,256]{2,1,0:T(8,128)S(1)}, bf16[4,128,256]{2,1,0:T(8,128)(2,1)S(1)}, f32[4,128,256]{2,1,0:T(8,128)S(1)}) custom-call(s32[2]{0:T(128)S(1)} %pad_add_fusion.rows, s32[32]{0:T(128)S(1)} %reshape.94.slots, f32[5]{0:T(128)S(1)} %copy-done.5, bf16[2,2,8,128,128]{4,3,2,1,0:T(8,128)(2,1)S(1)} %copy-done.1, ...), custom_call_target="tpu_custom_call" | custom-call | flops 268435456 | bytes 4194304 | tf_op jit(solution)/shard_map/forward_next/pallas_call | solution.py:362
  35.0 1.3 %collective-permute-start.3 = (bf16[4,128,256]{2,1,0:T(8,128)(2,1)S(1)}, bf16[4,128,256]{2,1,0:T(8,128)(2,1)S(1)}, u32[]{:S(2)}, u32[]{:S(2)}) collective-permute-start(bf16[4,128,256]{2,1,0:T(8,128)(2,1)S(1)} %get-tuple-element.26), channel_id=1, source_target_pairs={{0,1},{1,0},{2,3},{3,2},{4,5},{5,4},{6,7},{7,6},{8,9},{9,8},{10,11... | collective-permute-start | bytes 786440 | tf_op jit(solution)/shard_map/ppermute | solution.py:149
  36.5 1.8 %collective-permute-start.14 = (bf16[4,256,128]{2,1,0:T(8,128)(2,1)S(1)}, bf16[4,256,128]{2,1,0:T(8,128)(2,1)S(1)}, u32[]{:S(2)}, u32[]{:S(2)}) collective-permute-start(bf16[4,256,128]{2,1,0:T(8,128)(2,1)S(1)} %pad_maximum_fusion.12), channel_id=1, source_target_pairs={{0,1},{1,0},{2,3},{3,2},{4,5},{5,4},{6,7},{7,6},{8,9},{9,8},{10,11... | collective-permute-start | bytes 786440 | tf_op jit(solution)/shard_map/ppermute | solution.py:149
  38.3 4.7 %collective-permute-done.3 = bf16[4,128,256]{2,1,0:T(8,128)(2,1)S(1)} collective-permute-done((bf16[4,128,256]{2,1,0:T(8,128)(2,1)S(1)}, bf16[4,128,256]{2,1,0:T(8,128)(2,1)S(1)}, u32[]{:S(2)}, u32[]{:S(2)}) %collective-permute-start.3) | collective-permute-done | bytes 262176 | tf_op jit(solution)/shard_map/ppermute | solution.py:149
  43.1 1.2 %collective-permute-start.5 = (bf16[4,128,256]{2,1,0:T(8,128)(2,1)S(1)}, bf16[4,128,256]{2,1,0:T(8,128)(2,1)S(1)}, u32[]{:S(2)}, u32[]{:S(2)}) collective-permute-start(bf16[4,128,256]{2,1,0:T(8,128)(2,1)S(1)} %pad_maximum_fusion.6.inner.rest_10_), channel_id=1, source_target_pairs={{0,2},{2,0},{4,6},{6,4},{8,10},{10,8},{12,14},{14,12},{16,18},{18,... | collective-permute-start | bytes 786440 | tf_op jit(solution)/shard_map/ppermute | solution.py:154
  44.5 4.1 %collective-permute-done.14.across_ref = bf16[4,256,128]{2,1,0:T(8,128)(2,1)S(1)} collective-permute-done((bf16[4,256,128]{2,1,0:T(8,128)(2,1)S(1)}, bf16[4,256,128]{2,1,0:T(8,128)(2,1)S(1)}, u32[]{:S(2)}, u32[]{:S(2)}) %collective-permute-start.14) | collective-permute-done | bytes 262176 | tf_op jit(solution)/shard_map/ppermute | solution.py:149
  48.6 3.2 %adjoint_next.3 = (f32[4,256,128]{2,1,0:T(8,128)}, bf16[4,128,256]{2,1,0:T(8,128)(2,1)S(1)}, bf16[4,256,128]{2,1,0:T(8,128)(2,1)S(1)}, bf16[4,256,128]{2,1,0:T(8,128)(2,1)S(1)}, f32[8,256,128]{2,1,0:T(8,128)S(1)}) custom-call(s32[2]{0:T(128)S(1)} %pad_add_fusion.rows, s32[32]{0:T(128)S(1)} %reshape.94.slots, f32[5]{0:T(128)S(1)} %copy-done.5, ...), custom_call_target="tpu_custom_call" | custom-call | flops 268435456 | bytes 4194304 | tf_op jit(solution)/shard_map/adjoint_next/pallas_call | solution.py:362
  51.8 1.8 %collective-permute-start.16 = (bf16[4,256,128]{2,1,0:T(8,128)(2,1)S(1)}, bf16[4,256,128]{2,1,0:T(8,128)(2,1)S(1)}, u32[]{:S(2)}, u32[]{:S(2)}) collective-permute-start(bf16[4,256,128]{2,1,0:T(8,128)(2,1)S(1)} %get-tuple-element.41), channel_id=1, source_target_pairs={{0,2},{2,0},{4,6},{6,4},{8,10},{10,8},{12,14},{14,12},{16,18},{18,... | collective-permute-start | bytes 786440 | tf_op jit(solution)/shard_map/ppermute | solution.py:154
  53.6 2.8 %forward_next.4 = (f32[4,128,256]{2,1,0:T(8,128)}, bf16[4,128,256]{2,1,0:T(8,128)(2,1)S(1)}, f32[4,128,256]{2,1,0:T(8,128)S(1)}) custom-call(s32[2]{0:T(128)S(1)} %pad_add_fusion.rows, s32[32]{0:T(128)S(1)} %reshape.94.slots, f32[5]{0:T(128)S(1)} %copy-done.5, bf16[2,2,8,128,128]{4,3,2,1,0:T(8,128)(2,1)S(1)} %copy-done.1, ...), custom_call_target="tpu_custom_call" | custom-call | flops 268435456 | bytes 4194304 | tf_op jit(solution)/shard_map/forward_next/pallas_call | solution.py:362
  56.3 1.3 %collective-permute-start.6 = (bf16[4,128,256]{2,1,0:T(8,128)(2,1)S(1)}, bf16[4,128,256]{2,1,0:T(8,128)(2,1)S(1)}, u32[]{:S(2)}, u32[]{:S(2)}) collective-permute-start(bf16[4,128,256]{2,1,0:T(8,128)(2,1)S(1)} %get-tuple-element.28), channel_id=1, source_target_pairs={{0,1},{1,0},{2,3},{3,2},{4,5},{5,4},{6,7},{7,6},{8,9},{9,8},{10,11... | collective-permute-start | bytes 786440 | tf_op jit(solution)/shard_map/ppermute | solution.py:149
  58.0 6.3 %collective-permute-done.6 = bf16[4,128,256]{2,1,0:T(8,128)(2,1)S(1)} collective-permute-done((bf16[4,128,256]{2,1,0:T(8,128)(2,1)S(1)}, bf16[4,128,256]{2,1,0:T(8,128)(2,1)S(1)}, u32[]{:S(2)}, u32[]{:S(2)}) %collective-permute-start.6) | collective-permute-done | bytes 262176 | tf_op jit(solution)/shard_map/ppermute | solution.py:149
  65.4 1.3 %collective-permute-start.17 = (bf16[4,256,128]{2,1,0:T(8,128)(2,1)S(1)}, bf16[4,256,128]{2,1,0:T(8,128)(2,1)S(1)}, u32[]{:S(2)}, u32[]{:S(2)}) collective-permute-start(bf16[4,256,128]{2,1,0:T(8,128)(2,1)S(1)} %pad_maximum_fusion.14), channel_id=1, source_target_pairs={{0,1},{1,0},{2,3},{3,2},{4,5},{5,4},{6,7},{7,6},{8,9},{9,8},{10,11... | collective-permute-start | bytes 786440 | tf_op jit(solution)/shard_map/ppermute | solution.py:149
  66.8 7.5 %collective-permute-done.7.far.rest_12_ = bf16[4,128,256]{2,1,0:T(8,128)(2,1)S(1)} collective-permute-done((bf16[4,128,256]{2,1,0:T(8,128)(2,1)S(1)}, bf16[4,128,256]{2,1,0:T(8,128)(2,1)S(1)}, u32[]{:S(2)}, u32[]{:S(2)}) %collective-permute-start.7) | collective-permute-done | bytes 262176 | tf_op jit(solution)/shard_map/ppermute | solution.py:160
  74.2 2.8 %forward_next.5 = f32[2,2,128,256]{3,2,1,0:T(8,128)} custom-call(s32[2]{0:T(128)S(1)} %pad_add_fusion.rows, s32[32]{0:T(128)S(1)} %reshape.94.slots, f32[5]{0:T(128)S(1)} %copy-done.5, bf16[2,2,8,128,128]{4,3,2,1,0:T(8,128)(2,1)S(1)} %copy-done.1, bf16[4,128,256]{2,1,0:T(8,128)(2,1)S(1)} %collective-permute-done.7.far.rest_12_, ...), custom_call_target="tpu_custom_call" | custom-call | flops 268435456 | bytes 4194304 | tf_op jit(solution)/shard_map/forward_next/pallas_call | solution.py:362
  77.1 5.9 %gradient.1 = bf16[2,2,8,128,128]{4,3,2,1,0:T(8,128)(2,1)} custom-call(s32[2]{0:T(128)S(1)} %pad_add_fusion.rows, s32[32]{0:T(128)S(1)} %reshape.94.slots, f32[5]{0:T(128)S(1)} %copy-done.5, bf16[4,256,128]{2,1,0:T(8,128)(2,1)S(1)} %get-tuple-element.31.cot_t_ref, f32[4,256,128]{2,1,0:T(8,128)S(1)} %pad_maximum_fusion.2.own_ref, ...), custom_call_target="tpu_custom_call" | custom-call | flops 1073741824 | bytes 4194304 | tf_op jit(solution)/shard_map/gradient/pallas_call | solution.py:362
  (81 shorter events, 12.3 us)
Async XLA Ops:
  0.6 9.8 %copy-start.6 = (s32[256]{0:T(256)S(1)}, s32[256]{0:T(256)}, u32[]{:S(2)}) copy-start(s32[256]{0:T(256)} %param.7) | copy-start | bytes 3076
  1.7 1.2 %copy-start = (bf16[2,2,8,128,128]{4,3,2,1,0:T(8,128)(2,1)S(1)}, bf16[2,2,8,128,128]{4,3,2,1,0:T(8,128)(2,1)}, u32[]{:S(2)}) copy-start(bf16[2,2,8,128,128]{4,3,2,1,0:T(8,128)(2,1)} %h_ref.13) | copy-start | bytes 3145732
  2.9 0.9 %copy-start.3 = (bf16[2,2,128,256]{3,2,1,0:T(8,128)(2,1)S(1)}, bf16[2,2,128,256]{3,2,1,0:T(8,128)(2,1)}, u32[]{:S(2)}) copy-start(bf16[2,2,128,256]{3,2,1,0:T(8,128)(2,1)} %cot_ref.1) | copy-start | bytes 786436
  4.5 6.9 %copy-start.1 = (bf16[2,2,8,128,128]{4,3,2,1,0:T(8,128)(2,1)S(1)}, bf16[2,2,8,128,128]{4,3,2,1,0:T(8,128)(2,1)}, u32[]{:S(2)}) copy-start(bf16[2,2,8,128,128]{4,3,2,1,0:T(8,128)(2,1)} %h_ref.13) | copy-start | bytes 3145732
  7.6 6.9 %collective-permute-start.10 = (bf16[4,256,128]{2,1,0:T(8,128)(2,1)}, bf16[4,256,128]{2,1,0:T(8,128)(2,1)}, u32[]{:S(2)}, u32[]{:S(2)}) collective-permute-start(bf16[4,256,128]{2,1,0:T(8,128)(2,1)} %get-tuple-element.34), channel_id=1, source_target_pairs={{0,2},{2,0},{4,6},{6,4},{8,10},{10,8},{12,14},{14,12},{16,18},{18,... | collective-permute-start | bytes 786440 | tf_op jit(solution)/shard_map/ppermute | solution.py:154
  7.6 8.7 %collective-permute-start.9 = (bf16[4,256,128]{2,1,0:T(8,128)(2,1)S(1)}, bf16[4,256,128]{2,1,0:T(8,128)(2,1)}, u32[]{:S(2)}, u32[]{:S(2)}) collective-permute-start(bf16[4,256,128]{2,1,0:T(8,128)(2,1)S(1)} %get-tuple-element.33), channel_id=1, source_target_pairs={{0,30},{2,4},{4,2},{6,8},{8,6},{10,12},{12,10},{14,16},{16,14},{18... | collective-permute-start | bytes 786440 | tf_op jit(solution)/shard_map/ppermute | solution.py:160
  11.4 2.9 %copy-start.2 = (bf16[16,128,256]{2,1,0:T(8,128)(2,1)}, bf16[16,128,256]{2,1,0:T(8,128)(2,1)S(1)}, u32[]{:S(2)}) copy-start(bf16[16,128,256]{2,1,0:T(8,128)(2,1)S(1)} %fusion.6.w_ref.rest_3_) | copy-start | bytes 3145732
  13.0 7.3 %collective-permute-start = (bf16[4,128,256]{2,1,0:T(8,128)(2,1)S(1)}, bf16[4,128,256]{2,1,0:T(8,128)(2,1)S(1)}, u32[]{:S(2)}, u32[]{:S(2)}) collective-permute-start(bf16[4,128,256]{2,1,0:T(8,128)(2,1)S(1)} %get-tuple-element.24), channel_id=1, source_target_pairs={{0,1},{1,0},{2,3},{3,2},{4,5},{5,4},{6,7},{7,6},{8,9},{9,8},{10,11... | collective-permute-start | bytes 786440 | tf_op jit(solution)/shard_map/ppermute | solution.py:149
  17.5 9.7 %collective-permute-start.11 = (bf16[4,256,128]{2,1,0:T(8,128)(2,1)S(1)}, bf16[4,256,128]{2,1,0:T(8,128)(2,1)S(1)}, u32[]{:S(2)}, u32[]{:S(2)}) collective-permute-start(bf16[4,256,128]{2,1,0:T(8,128)(2,1)S(1)} %pad_maximum_fusion.10), channel_id=1, source_target_pairs={{0,1},{1,0},{2,3},{3,2},{4,5},{5,4},{6,7},{7,6},{8,9},{9,8},{10,11... | collective-permute-start | bytes 786440 | tf_op jit(solution)/shard_map/ppermute | solution.py:149
  20.3 12.9 %collective-permute-start.2 = (bf16[4,128,256]{2,1,0:T(8,128)(2,1)S(1)}, bf16[4,128,256]{2,1,0:T(8,128)(2,1)S(1)}, u32[]{:S(2)}, u32[]{:S(2)}) collective-permute-start(bf16[4,128,256]{2,1,0:T(8,128)(2,1)S(1)} %pad_maximum_fusion.4.inner.rest_6_), channel_id=1, source_target_pairs={{0,2},{2,0},{4,6},{6,4},{8,10},{10,8},{12,14},{14,12},{16,18},{18,... | collective-permute-start | bytes 786440 | tf_op jit(solution)/shard_map/ppermute | solution.py:154
  24.1 9.1 %collective-permute-start.1 = (bf16[4,128,256]{2,1,0:T(8,128)(2,1)S(1)}, bf16[4,128,256]{2,1,0:T(8,128)(2,1)S(1)}, u32[]{:S(2)}, u32[]{:S(2)}) collective-permute-start(bf16[4,128,256]{2,1,0:T(8,128)(2,1)S(1)} %pad_maximum_fusion.3.outer.rest_5_), channel_id=1, source_target_pairs={{0,30},{2,4},{4,2},{6,8},{8,6},{10,12},{12,10},{14,16},{16,14},{18... | collective-permute-start | bytes 786440 | tf_op jit(solution)/shard_map/ppermute | solution.py:160
  24.2 3.0 %copy-start.5 = (f32[5]{0:T(128)S(1)}, f32[5]{0:T(128)}, u32[]{:S(2)}) copy-start(f32[5]{0:T(128)} %coef.13) | copy-start | bytes 64
  29.4 6.9 %collective-permute-start.12 = (bf16[4,256,128]{2,1,0:T(8,128)(2,1)S(1)}, bf16[4,256,128]{2,1,0:T(8,128)(2,1)S(1)}, u32[]{:S(2)}, u32[]{:S(2)}) collective-permute-start(bf16[4,256,128]{2,1,0:T(8,128)(2,1)S(1)} %get-tuple-element.36), channel_id=1, source_target_pairs={{0,30},{2,4},{4,2},{6,8},{8,6},{10,12},{12,10},{14,16},{16,14},{18... | collective-permute-start | bytes 786440 | tf_op jit(solution)/shard_map/ppermute | solution.py:160
  30.2 6.1 %collective-permute-start.13 = (bf16[4,256,128]{2,1,0:T(8,128)(2,1)S(1)}, bf16[4,256,128]{2,1,0:T(8,128)(2,1)S(1)}, u32[]{:S(2)}, u32[]{:S(2)}) collective-permute-start(bf16[4,256,128]{2,1,0:T(8,128)(2,1)S(1)} %get-tuple-element.37), channel_id=1, source_target_pairs={{0,2},{2,0},{4,6},{6,4},{8,10},{10,8},{12,14},{14,12},{16,18},{18,... | collective-permute-start | bytes 786440 | tf_op jit(solution)/shard_map/ppermute | solution.py:154
  35.0 8.0 %collective-permute-start.3 = (bf16[4,128,256]{2,1,0:T(8,128)(2,1)S(1)}, bf16[4,128,256]{2,1,0:T(8,128)(2,1)S(1)}, u32[]{:S(2)}, u32[]{:S(2)}) collective-permute-start(bf16[4,128,256]{2,1,0:T(8,128)(2,1)S(1)} %get-tuple-element.26), channel_id=1, source_target_pairs={{0,1},{1,0},{2,3},{3,2},{4,5},{5,4},{6,7},{7,6},{8,9},{9,8},{10,11... | collective-permute-start | bytes 786440 | tf_op jit(solution)/shard_map/ppermute | solution.py:149
  36.5 12.1 %collective-permute-start.14 = (bf16[4,256,128]{2,1,0:T(8,128)(2,1)S(1)}, bf16[4,256,128]{2,1,0:T(8,128)(2,1)S(1)}, u32[]{:S(2)}, u32[]{:S(2)}) collective-permute-start(bf16[4,256,128]{2,1,0:T(8,128)(2,1)S(1)} %pad_maximum_fusion.12), channel_id=1, source_target_pairs={{0,1},{1,0},{2,3},{3,2},{4,5},{5,4},{6,7},{7,6},{8,9},{9,8},{10,11... | collective-permute-start | bytes 786440 | tf_op jit(solution)/shard_map/ppermute | solution.py:149
  43.1 10.5 %collective-permute-start.5 = (bf16[4,128,256]{2,1,0:T(8,128)(2,1)S(1)}, bf16[4,128,256]{2,1,0:T(8,128)(2,1)S(1)}, u32[]{:S(2)}, u32[]{:S(2)}) collective-permute-start(bf16[4,128,256]{2,1,0:T(8,128)(2,1)S(1)} %pad_maximum_fusion.6.inner.rest_10_), channel_id=1, source_target_pairs={{0,2},{2,0},{4,6},{6,4},{8,10},{10,8},{12,14},{14,12},{16,18},{18,... | collective-permute-start | bytes 786440 | tf_op jit(solution)/shard_map/ppermute | solution.py:154
  44.3 9.2 %collective-permute-start.4 = (bf16[4,128,256]{2,1,0:T(8,128)(2,1)S(1)}, bf16[4,128,256]{2,1,0:T(8,128)(2,1)S(1)}, u32[]{:S(2)}, u32[]{:S(2)}) collective-permute-start(bf16[4,128,256]{2,1,0:T(8,128)(2,1)S(1)} %pad_maximum_fusion.5.outer.rest_9_), channel_id=1, source_target_pairs={{0,30},{2,4},{4,2},{6,8},{8,6},{10,12},{12,10},{14,16},{16,14},{18... | collective-permute-start | bytes 786440 | tf_op jit(solution)/shard_map/ppermute | solution.py:160
  51.8 6.1 %collective-permute-start.15 = (bf16[4,256,128]{2,1,0:T(8,128)(2,1)S(1)}, bf16[4,256,128]{2,1,0:T(8,128)(2,1)S(1)}, u32[]{:S(2)}, u32[]{:S(2)}) collective-permute-start(bf16[4,256,128]{2,1,0:T(8,128)(2,1)S(1)} %get-tuple-element.40), channel_id=1, source_target_pairs={{0,30},{2,4},{4,2},{6,8},{8,6},{10,12},{12,10},{14,16},{16,14},{18... | collective-permute-start | bytes 786440 | tf_op jit(solution)/shard_map/ppermute | solution.py:160
  51.8 6.1 %collective-permute-start.16 = (bf16[4,256,128]{2,1,0:T(8,128)(2,1)S(1)}, bf16[4,256,128]{2,1,0:T(8,128)(2,1)S(1)}, u32[]{:S(2)}, u32[]{:S(2)}) collective-permute-start(bf16[4,256,128]{2,1,0:T(8,128)(2,1)S(1)} %get-tuple-element.41), channel_id=1, source_target_pairs={{0,2},{2,0},{4,6},{6,4},{8,10},{10,8},{12,14},{14,12},{16,18},{18,... | collective-permute-start | bytes 786440 | tf_op jit(solution)/shard_map/ppermute | solution.py:154
  56.3 8.0 %collective-permute-start.6 = (bf16[4,128,256]{2,1,0:T(8,128)(2,1)S(1)}, bf16[4,128,256]{2,1,0:T(8,128)(2,1)S(1)}, u32[]{:S(2)}, u32[]{:S(2)}) collective-permute-start(bf16[4,128,256]{2,1,0:T(8,128)(2,1)S(1)} %get-tuple-element.28), channel_id=1, source_target_pairs={{0,1},{1,0},{2,3},{3,2},{4,5},{5,4},{6,7},{7,6},{8,9},{9,8},{10,11... | collective-permute-start | bytes 786440 | tf_op jit(solution)/shard_map/ppermute | solution.py:149
  64.4 2.4 %collective-permute-start.8 = (bf16[4,128,256]{2,1,0:T(8,128)(2,1)S(1)}, bf16[4,128,256]{2,1,0:T(8,128)(2,1)S(1)}, u32[]{:S(2)}, u32[]{:S(2)}) collective-permute-start(bf16[4,128,256]{2,1,0:T(8,128)(2,1)S(1)} %pad_maximum_fusion.8.inner.rest_14_), channel_id=1, source_target_pairs={{0,2},{2,0},{4,6},{6,4},{8,10},{10,8},{12,14},{14,12},{16,18},{18,... | collective-permute-start | bytes 786440 | tf_op jit(solution)/shard_map/ppermute | solution.py:154
  65.3 9.0 %collective-permute-start.7 = (bf16[4,128,256]{2,1,0:T(8,128)(2,1)S(1)}, bf16[4,128,256]{2,1,0:T(8,128)(2,1)S(1)}, u32[]{:S(2)}, u32[]{:S(2)}) collective-permute-start(bf16[4,128,256]{2,1,0:T(8,128)(2,1)S(1)} %pad_maximum_fusion.7.outer.rest_13_), channel_id=1, source_target_pairs={{0,30},{2,4},{4,2},{6,8},{8,6},{10,12},{12,10},{14,16},{16,14},{18... | collective-permute-start | bytes 786440 | tf_op jit(solution)/shard_map/ppermute | solution.py:160
  65.4 11.7 %collective-permute-start.17 = (bf16[4,256,128]{2,1,0:T(8,128)(2,1)S(1)}, bf16[4,256,128]{2,1,0:T(8,128)(2,1)S(1)}, u32[]{:S(2)}, u32[]{:S(2)}) collective-permute-start(bf16[4,256,128]{2,1,0:T(8,128)(2,1)S(1)} %pad_maximum_fusion.14), channel_id=1, source_target_pairs={{0,1},{1,0},{2,3},{3,2},{4,5},{5,4},{6,7},{7,6},{8,9},{9,8},{10,11... | collective-permute-start | bytes 786440 | tf_op jit(solution)/shard_map/ppermute | solution.py:149
  (1 other events, 0.7 us)

commit v2 on v0

--- a/solution.py
+++ b/solution.py
@@ -1,6 +1,10 @@
+import functools
+
 import jax
 import jax.numpy as jnp
 from jax import lax
+from jax.experimental import pallas as pl
+from jax.experimental.pallas import tpu as pltpu
 from jax.sharding import PartitionSpec as P
 
 offset_table = tuple(((offset_code // 3 - 1, offset_code % 3 - 1) for offset_code in range(9)))
@@ -81,7 +85,7 @@
     return middle[:, 1 : rows_y + 1]
 
 
-def shards(hamiltonian, neighbours, probe_seeds, coefficients, cotangent):
+def any_shards(hamiltonian, neighbours, probe_seeds, coefficients, cotangent):
     rows_x, rows_y = (hamiltonian.shape[0], hamiltonian.shape[1])
     width = hamiltonian.shape[3]
     probes = cotangent.shape[3]
@@ -136,6 +140,308 @@
     return (density, (gradient * (1.0 / probes)).astype(jnp.bfloat16))
 
 
+bf16 = jnp.bfloat16
+f32 = jnp.float32
+VMEM_BYTES = 40 * 1024 * 1024
+OWN = (4, 5, 8, 9)
+ACROSS = (6, 7, 10, 11)
+
+
+def swap_y(value):
+    return lax.ppermute(value, "gy", [(0, 1), (1, 0)])
+
+
+def swap_near(value):
+    count = lax.axis_size("gx")
+    return lax.ppermute(value, "gx", [(i, i ^ 1) for i in range(count)])
+
+
+def swap_far(value):
+    count = lax.axis_size("gx")
+    pairs = [(i, (i + 1) % count if i % 2 else (i - 1) % count) for i in range(count)]
+    return lax.ppermute(value, "gx", pairs)
+
+
+def start_signs(rows_from, seeds, width):
+    shape = (width, seeds.shape[1])
+    hashed = (rows_from + lax.broadcasted_iota(jnp.int32, shape, 0)) * jnp.int32(-1640531535)
+    hashed = hashed ^ seeds
+    hashed = hashed ^ hashed >> 15
+    hashed = hashed * jnp.int32(739982445)
+    hashed = hashed ^ hashed >> 12
+    return (1 - 2 * (hashed >> 7 & 1)).astype(f32).astype(bf16)
+
+
+def listed_blocks(h_ref, rows, at):
+    return [h_ref[rows[at // 2], at % 2, k] for k in range(h_ref.shape[2])]
+
+
+def window_product(slots, rows, at, h_ref, window):
+    listed = h_ref.shape[2]
+    left = jnp.concatenate(listed_blocks(h_ref, rows, at), axis=1)
+    right = jnp.concatenate([window[slots[at * listed + k]] for k in range(listed)], axis=0)
+    return jnp.dot(left, right, preferred_element_type=f32)
+
+
+def push(slots, rows, at, h_ref, adjoint_t, sums):
+    listed, width = h_ref.shape[2:4]
+    wide = jnp.concatenate(listed_blocks(h_ref, rows, at), axis=1)
+    product = jnp.dot(adjoint_t, wide, preferred_element_type=f32)
+    for k in range(listed):
+        sums[slots[at * listed + k]] += product[:, k * width : (k + 1) * width]
+
+
+def finish_push(sums, far_ref, near_ref, own_ref, across_ref):
+    far_ref[...] = sums[0:4].astype(bf16)
+    near_ref[...] = sums[12:16].astype(bf16)
+    for at in range(4):
+        own_ref[at] = sums[OWN[at]]
+        across_ref[at] = sums[ACROSS[at]]
+
+
+def first_kernel(
+    top, rows, slots, place, coef, seeds_ref, h_hbm, cot_hbm,
+    start_ref, term_ref, rounded_ref, cot_t_ref, adjoint_ref, far_ref, near_ref, own_ref, across_ref,
+    h_ref, cot_ref, sums, h_sem, cot_sem,
+):
+    copies = []
+    for at in range(4):
+        source = (rows[at // 2], at % 2)
+        copies.append(
+            (
+                pltpu.make_async_copy(h_hbm.at[source], h_ref.at[source], h_sem.at[at]),
+                pltpu.make_async_copy(cot_hbm.at[source], cot_ref.at[at], cot_sem.at[at]),
+            )
+        )
+    for pair in copies:
+        for copy in pair:
+            copy.start()
+    for slot in range(16):
+        start_ref[slot] = start_signs(place[slot], seeds_ref[...], h_ref.shape[3])
+    sums[...] = jnp.zeros_like(sums)
+    for at in range(4):
+        copies[at][0].wait()
+        value = window_product(slots, rows, at, h_ref, start_ref)
+        term_ref[at] = value
+        rounded_ref[at] = value.astype(bf16)
+    for at in range(4):
+        copies[at][1].wait()
+        cot = cot_ref[at].astype(f32)
+        cot_t = jnp.transpose(cot)
+        cot_t_ref[at] = cot_t.astype(bf16)
+        adjoint_ref[at] = (coef[top] * cot).astype(bf16)
+        push(slots, rows, at, h_ref, (coef[top] * cot_t).astype(bf16), sums)
+    finish_push(sums, far_ref, near_ref, own_ref, across_ref)
+
+
+def forward_kernel(index, rows, slots, coef, h_ref, window, before_ref, sums_ref, term_ref, rounded_ref, density_ref):
+    for at in range(4):
+        before = (before_ref[OWN[at]] if index == 2 else before_ref[at]).astype(f32)
+        value = 2.0 * window_product(slots, rows, at, h_ref, window) - before
+        sums = coef[0] * before + coef[1] * sums_ref[at] if index == 2 else sums_ref[at]
+        term_ref[at] = value
+        rounded_ref[at] = value.astype(bf16)
+        density_ref[at] = sums + coef[index] * value
+
+
+def adjoint_value(at, index, coef, cot_t_ref, own_ref, far_ref, near_ref, across_ref):
+    came = far_ref[at] if at < 2 else near_ref[at - 2]
+    carried = own_ref[at] + came.astype(f32) + across_ref[at].astype(f32)
+    return coef[index] * cot_t_ref[at].astype(f32) + 2.0 * carried
+
+
+def adjoint_kernel(
+    index, top, rows, slots, coef, h_ref, cot_t_ref, own_in, far_in, near_in, across_in,
+    value_ref, rounded_ref, far_ref, near_ref, own_ref, across_ref, sums,
+):
+    sums[...] = jnp.zeros_like(sums)
+    for at in range(4):
+        value = adjoint_value(at, index, coef, cot_t_ref, own_in, far_in, near_in, across_in)
+        if index + 2 == top:
+            value = value - coef[top] * cot_t_ref[at].astype(f32)
+        value_ref[at] = value
+        push(slots, rows, at, h_ref, value.astype(bf16), sums)
+        rounded_ref[at] = jnp.transpose(value).astype(bf16)
+    finish_push(sums, far_ref, near_ref, own_ref, across_ref)
+
+
+def block_gradients(slots, at, left, windows, listed, store):
+    for k in range(listed):
+        slot = slots[at * listed + k]
+        right = jnp.concatenate([window[slot] for window in windows], axis=1)
+        store(k, lax.dot_general(left, right, (((1,), (1,)), ((), ())), preferred_element_type=f32))
+
+
+def early_gradient_kernel(terms, rows, slots, coef, cot_t_ref, own_ref, far_ref, near_ref, across_ref, older_ref, *rest):
+    adjoints, windows, sums_ref = rest[: terms - 3], rest[terms - 3 : -1], rest[-1]
+    listed = sums_ref.shape[1]
+    for at in range(4):
+        value = adjoint_value(at, 1, coef, cot_t_ref, own_ref, far_ref, near_ref, across_ref) - older_ref[at]
+        left = [jnp.transpose(value).astype(bf16)] + [a[at] * bf16(2.0) for a in adjoints]
+
+        def store(k, total, at=at):
+            sums_ref[at, k] = total
+
+        block_gradients(slots, at, jnp.concatenate(left, axis=1), windows, listed, store)
+
+
+def last_kernel(
+    index, scale, rows, slots, coef, h_ref, window, before_ref, sums_ref, adjoint_ref, early_ref,
+    density_hbm, grad_hbm, density, grad, density_sem, grad_sem,
+):
+    listed = h_ref.shape[2]
+    copies = []
+    for at in range(4):
+        place = (rows[at // 2], at % 2)
+        value = 2.0 * window_product(slots, rows, at, h_ref, window) - before_ref[at]
+        density[at] = sums_ref[at] + coef[index] * value
+        copies.append(pltpu.make_async_copy(density.at[at], density_hbm.at[place], density_sem.at[at]))
+        copies[-1].start()
+
+        def store(k, total, at=at):
+            grad[at, k] = ((early_ref[at, k] + total) * scale).astype(bf16)
+
+        block_gradients(slots, at, adjoint_ref[at] * bf16(2.0), (window,), listed, store)
+        copies.append(pltpu.make_async_copy(grad.at[at], grad_hbm.at[place], grad_sem.at[at]))
+        copies[-1].start()
+    for copy in copies:
+        copy.wait()
+
+
+def pair_shards(hamiltonian, neighbours, probe_seeds, coefficients, cotangent):
+    rows_x, rows_y, listed, width = hamiltonian.shape[:4]
+    probes = cotangent.shape[3]
+    terms = coefficients.shape[0]
+    top = terms - 1
+    blocks = rows_x * rows_y
+    span_x = rows_x * lax.axis_size("gx")
+    span_y = rows_y * lax.axis_size("gy")
+    odd = lax.axis_index("gx") % 2
+    four = jnp.arange(4, dtype=jnp.int32)
+    local_row = jnp.where(odd == 0, four - 1, 2 - four)
+    place_x = (lax.axis_index("gx") * rows_x + local_row) % span_x
+    place_y = (lax.axis_index("gy") * rows_y + four) % span_y
+    place = ((place_x[:, None] * span_y + place_y) * width).reshape(-1).astype(jnp.int32)
+    rows = jnp.stack([odd, 1 - odd]).astype(jnp.int32)
+    codes = jnp.where(odd == 0, neighbours, neighbours[::-1])
+    window_row = 1 + jnp.arange(2, dtype=jnp.int32)[:, None, None] + (1 - 2 * odd) * (codes // 3 - 1)
+    window_col = (jnp.arange(2, dtype=jnp.int32)[None, :, None] + codes % 3 - 1) % 4
+    slots = (window_row * 4 + window_col).reshape(-1).astype(jnp.int32)
+
+    vmem = pl.BlockSpec(memory_space=pltpu.VMEM)
+    smem = pl.BlockSpec(memory_space=pltpu.SMEM)
+    outside = pl.BlockSpec(memory_space=pl.ANY)
+
+    def field(count, dtype):
+        return jax.ShapeDtypeStruct((count, width, probes), dtype)
+
+    def turned(count, dtype):
+        return jax.ShapeDtypeStruct((count, probes, width), dtype)
+
+    apply_flops = 2 * blocks * listed * width * width * probes
+    pushed = [turned(4, bf16), turned(4, bf16), turned(4, f32), turned(4, f32)]
+    sums_scratch = pltpu.VMEM((16, probes, width), f32)
+
+    def call(name, kernel, scalars, operands, out_shape, scratch=(), flops=apply_flops, out_specs=None, in_specs=None):
+        return pl.pallas_call(
+            kernel,
+            in_specs=[smem] * len(scalars) + (in_specs or [vmem] * len(operands)),
+            out_specs=out_specs or [vmem] * len(out_shape),
+            out_shape=out_shape,
+            scratch_shapes=list(scratch),
+            compiler_params=pltpu.CompilerParams(vmem_limit_bytes=VMEM_BYTES),
+            cost_estimate=pl.CostEstimate(flops=flops, bytes_accessed=2 * 1024 * 1024, transcendentals=0),
+            name=name,
+        )(*scalars, *operands)
+
+    scalars = (rows, slots, coefficients)
+    start, term, rounded, cot_t, adjoint, *sent = call(
+        "first",
+        functools.partial(first_kernel, top),
+        (rows, slots, place, coefficients),
+        (probe_seeds.reshape(1, probes), hamiltonian, cotangent),
+        [field(16, bf16), field(4, f32), field(4, bf16), turned(4, bf16), field(4, bf16)] + pushed,
+        scratch=(
+            pltpu.VMEM(hamiltonian.shape, bf16),
+            pltpu.VMEM((4, width, probes), bf16),
+            sums_scratch,
+            pltpu.SemaphoreType.DMA((4,)),
+            pltpu.SemaphoreType.DMA((4,)),
+        ),
+        flops=2 * apply_flops,
+        in_specs=[vmem, outside, outside],
+    )
+    adjoints = {top: adjoint}
+    values = {}
+    windows = [start]
+    before, sums = start, term
+    for index in range(2, terms):
+        across = swap_y(rounded)
+        outer = jnp.concatenate([rounded[:2], across[:2]])
+        inner = jnp.concatenate([rounded[2:], across[2:]])
+        window = jnp.concatenate([swap_far(outer), outer, inner, swap_near(inner)])
+        to_far, to_near, own, to_across = sent
+        far, near = swap_far(to_far), swap_near(to_near)
+        to_across = to_across + jnp.concatenate([far[2:], near[2:]]).astype(f32)
+        arrived = (cot_t, own, far, near, swap_y(to_across.astype(bf16)))
+
+        windows.append(window)
+        at = terms - index
+        if index < top:
+            following, rounded, density = call(
+                "forward",
+                functools.partial(forward_kernel, index),
+                scalars, (hamiltonian, window, before, sums),
+                [field(4, f32), field(4, bf16), field(4, f32)],
+            )
+            before, sums, term = term, density, following
+            values[at], adjoints[at], *sent = call(
+                "adjoint",
+                functools.partial(adjoint_kernel, at, top),
+                scalars, (hamiltonian,) + arrived,
+                [turned(4, f32), field(4, bf16)] + pushed,
+                scratch=(sums_scratch,),
+            )
+    early = call(
+        "early_gradient",
+        functools.partial(early_gradient_kernel, terms),
+        scalars,
+        arrived + (values[3],) + tuple(adjoints[t] for t in range(2, top)) + tuple(windows[: top - 1]),
+        [jax.ShapeDtypeStruct((blocks, listed, width, width), f32)],
+        flops=(terms - 2) * apply_flops,
+    )[0]
+    density, gradient = call(
+        "last",
+        functools.partial(last_kernel, top, 1.0 / probes),
+        scalars, (hamiltonian, windows[top - 1], before, sums, adjoints[top], early),
+        [
+            jax.ShapeDtypeStruct(cotangent.shape, f32),
+            jax.ShapeDtypeStruct(hamiltonian.shape, bf16),
+        ],
+        scratch=(
+            pltpu.VMEM((4, width, probes), f32),
+            pltpu.VMEM((blocks, listed, width, width), bf16),
+            pltpu.SemaphoreType.DMA((4,)),
+            pltpu.SemaphoreType.DMA((4,)),
+        ),
+        flops=2 * apply_flops,
+        out_specs=[outside, outside],
+    )
+    return density, gradient
+
+
+def shards(hamiltonian, neighbours, probe_seeds, coefficients, cotangent):
+    paired = (
+        hamiltonian.shape[:2] == (2, 2)
+        and lax.axis_size("gy") == 2
+        and lax.axis_size("gx") % 2 == 0
+        and hamiltonian.shape[2] % 2 == 0
+        and coefficients.shape[0] == 5
+    )
+    run = pair_shards if paired else any_shards
+    return run(hamiltonian, neighbours, probe_seeds, coefficients, cotangent)
+
+
 def solution(mesh):
     placed = (
         P("gx", "gy", None, None, None),

time: 166 us -> 80.7 us (0.49)
  the two profiles are of different devices: /device:TPU:28 before, /device:TPU:1 now
where the time goes in v2:
time: 80.7 us; the launch traced here: 80.2 us
  waiting for transfers between devices  31.3 us (39%)
  starting transfers between devices  26.1 us (32%)
  Pallas kernels  16.3 us (20%)
  local copies, waits for them, and re-layouts  4.09 us (5%)
  other arithmetic  1.33 us (2%)
  between operations  1 us (1%)
    ppermute x6, waiting for transfers between devices, swap_y(): return lax.ppermute(value, 'gy', [(0, 1), (1, 0)])  19.9 us
    pallas_call x7, Pallas kernels, call(): pl.pallas_call(kernel, in_specs=[smem] * len(scalars) + (in_specs or [vme...  16.3 us
    ppermute x6, starting transfers between devices, swap_far(): return lax.ppermute(value, 'gx', pairs)  9.75 us
    ppermute x6, starting transfers between devices, swap_near(): return lax.ppermute(value, 'gx', [(i, i ^ 1) for i in range(count)])  8.94 us
    ppermute x6, waiting for transfers between devices, swap_far(): return lax.ppermute(value, 'gx', pairs)  7.42 us
    ppermute x6, starting transfers between devices, swap_y(): return lax.ppermute(value, 'gy', [(0, 1), (1, 0)])  7.42 us
    ppermute x6, waiting for transfers between devices, swap_near(): return lax.ppermute(value, 'gx', [(i, i ^ 1) for i in range(count)])  4.04 us
    unnamed x19, local copies, waits for them, and re-layouts  3.63 us
  transfers between devices with their start and end apart: 18, of which 11 were waited for; matrix products, arithmetic and copies ran while one was open for 1% of the time, Pallas kernels for 9%

profile of v2, /device:TPU:1, one launch (start us, length us, event | category | flops | bytes accessed | tf_op | source)
XLA Modules:
  0.0 80.2 jit_solution(8720430840714661253)
XLA Ops:
  5.3 4.8 %first.1 = (bf16[16,128,256]{2,1,0:T(8,128)(2,1)S(1)}, f32[4,128,256]{2,1,0:T(8,128)S(1)}, bf16[4,128,256]{2,1,0:T(8,128)(2,1)S(1)}, bf16[4,256,128]{2,1,0:T(8,1...) custom-call(s32[2]{0:T(128)S(1)} %pad_add_fusion.rows, ...), custom_call_target="tpu_custom_call" | custom-call | flops 536870912 | bytes 2097152 | tf_op jit(solution)/shard_map/first/pallas_call | solution.py:346
  10.2 2.1 %collective-permute-start = (bf16[4,128,256]{2,1,0:T(8,128)(2,1)S(1)}, bf16[4,128,256]{2,1,0:T(8,128)(2,1)S(1)}, u32[]{:S(2)}, u32[]{:S(2)}) collective-permute-start(bf16[4,128,256]{2,1,0:T(8,128)(2,1)S(1)} %get-tuple-element.27), channel_id=1, source_target_pairs={{0,1},{1,0},{2,3},{3,2},{4,5},{5,4},{6,7},{7,6},{8,9},{9,8},{10,11... | collective-permute-start | bytes 786440 | tf_op jit(solution)/shard_map/ppermute | solution.py:151
  12.3 2.1 %collective-permute-start.9 = (bf16[4,256,128]{2,1,0:T(8,128)(2,1)S(1)}, bf16[4,256,128]{2,1,0:T(8,128)(2,1)S(1)}, u32[]{:S(2)}, u32[]{:S(2)}) collective-permute-start(bf16[4,256,128]{2,1,0:T(8,128)(2,1)S(1)} %get-tuple-element.38), channel_id=1, source_target_pairs={{0,30},{2,4},{4,2},{6,8},{8,6},{10,12},{12,10},{14,16},{16,14},{18... | collective-permute-start | bytes 786440 | tf_op jit(solution)/shard_map/ppermute | solution.py:162
  14.3 2.6 %collective-permute-start.10 = (bf16[4,256,128]{2,1,0:T(8,128)(2,1)S(1)}, bf16[4,256,128]{2,1,0:T(8,128)(2,1)S(1)}, u32[]{:S(2)}, u32[]{:S(2)}) collective-permute-start(bf16[4,256,128]{2,1,0:T(8,128)(2,1)S(1)} %get-tuple-element.39), channel_id=1, source_target_pairs={{0,2},{2,0},{4,6},{6,4},{8,10},{10,8},{12,14},{14,12},{16,18},{18,... | collective-permute-start | bytes 786440 | tf_op jit(solution)/shard_map/ppermute | solution.py:156
  17.0 1.3 %collective-permute-done = bf16[4,128,256]{2,1,0:T(8,128)(2,1)S(1)} collective-permute-done((bf16[4,128,256]{2,1,0:T(8,128)(2,1)S(1)}, bf16[4,128,256]{2,1,0:T(8,128)(2,1)S(1)}, u32[]{:S(2)}, u32[]{:S(2)}) %collective-permute-start) | collective-permute-done | bytes 262176 | tf_op jit(solution)/shard_map/ppermute | solution.py:151
  18.3 2.7 %collective-permute-start.1 = (bf16[4,128,256]{2,1,0:T(8,128)(2,1)S(1)}, bf16[4,128,256]{2,1,0:T(8,128)(2,1)S(1)}, u32[]{:S(2)}, u32[]{:S(2)}) collective-permute-start(bf16[4,128,256]{2,1,0:T(8,128)(2,1)S(1)} %pad_maximum_fusion), channel_id=1, source_target_pairs={{0,30},{2,4},{4,2},{6,8},{8,6},{10,12},{12,10},{14,16},{16,14},{18... | collective-permute-start | bytes 786440 | tf_op jit(solution)/shard_map/ppermute | solution.py:162
  22.4 5.8 %collective-permute-done.1 = bf16[4,128,256]{2,1,0:T(8,128)(2,1)S(1)} collective-permute-done((bf16[4,128,256]{2,1,0:T(8,128)(2,1)S(1)}, bf16[4,128,256]{2,1,0:T(8,128)(2,1)S(1)}, u32[]{:S(2)}, u32[]{:S(2)}) %collective-permute-start.1) | collective-permute-done | bytes 262176 | tf_op jit(solution)/shard_map/ppermute | solution.py:162
  28.2 1.6 %adjoint.2 = (f32[4,256,128]{2,1,0:T(8,128)S(1)}, bf16[4,128,256]{2,1,0:T(8,128)(2,1)S(1)}, bf16[4,256,128]{2,1,0:T(8,128)(2,1)S(1)}, bf16[4,256,128]{2,1,0:T(8,...) custom-call(s32[2]{0:T(128)S(1)} %pad_add_fusion.rows, s32[32]{0:T(128)S(1)} %reshape.57.slots, ...), custom_call_target="tpu_custom_call" | custom-call | flops 268435456 | bytes 2097152 | tf_op jit(solution)/shard_map/adjoint/pallas_call | solution.py:346
  29.8 2.9 %collective-permute-start.12 = (bf16[4,256,128]{2,1,0:T(8,128)(2,1)S(1)}, bf16[4,256,128]{2,1,0:T(8,128)(2,1)S(1)}, u32[]{:S(2)}, u32[]{:S(2)}) collective-permute-start(bf16[4,256,128]{2,1,0:T(8,128)(2,1)S(1)} %get-tuple-element.42), channel_id=1, source_target_pairs={{0,30},{2,4},{4,2},{6,8},{8,6},{10,12},{12,10},{14,16},{16,14},{18... | collective-permute-start | bytes 786440 | tf_op jit(solution)/shard_map/ppermute | solution.py:162
  32.7 1.5 %collective-permute-start.13 = (bf16[4,256,128]{2,1,0:T(8,128)(2,1)S(1)}, bf16[4,256,128]{2,1,0:T(8,128)(2,1)S(1)}, u32[]{:S(2)}, u32[]{:S(2)}) collective-permute-start(bf16[4,256,128]{2,1,0:T(8,128)(2,1)S(1)} %get-tuple-element.43), channel_id=1, source_target_pairs={{0,2},{2,0},{4,6},{6,4},{8,10},{10,8},{12,14},{14,12},{16,18},{18,... | collective-permute-start | bytes 786440 | tf_op jit(solution)/shard_map/ppermute | solution.py:156
  34.4 1.5 %collective-permute-done.2 = bf16[4,128,256]{2,1,0:T(8,128)(2,1)S(1)} collective-permute-done((bf16[4,128,256]{2,1,0:T(8,128)(2,1)S(1)}, bf16[4,128,256]{2,1,0:T(8,128)(2,1)S(1)}, u32[]{:S(2)}, u32[]{:S(2)}) %collective-permute-start.2) | collective-permute-done | bytes 262176 | tf_op jit(solution)/shard_map/ppermute | solution.py:156
  38.8 2.4 %collective-permute-start.14 = (bf16[4,256,128]{2,1,0:T(8,128)(2,1)S(1)}, bf16[4,256,128]{2,1,0:T(8,128)(2,1)S(1)}, u32[]{:S(2)}, u32[]{:S(2)}) collective-permute-start(bf16[4,256,128]{2,1,0:T(8,128)(2,1)S(1)} %add_convert_fusion.1), channel_id=1, source_target_pairs={{0,1},{1,0},{2,3},{3,2},{4,5},{5,4},{6,7},{7,6},{8,9},{9,8},{10,11... | collective-permute-start | bytes 786440 | tf_op jit(solution)/shard_map/ppermute | solution.py:151
  41.2 3.5 %collective-permute-done.3 = bf16[4,128,256]{2,1,0:T(8,128)(2,1)S(1)} collective-permute-done((bf16[4,128,256]{2,1,0:T(8,128)(2,1)S(1)}, bf16[4,128,256]{2,1,0:T(8,128)(2,1)S(1)}, u32[]{:S(2)}, u32[]{:S(2)}) %collective-permute-start.3) | collective-permute-done | bytes 262176 | tf_op jit(solution)/shard_map/ppermute | solution.py:151
  45.2 5.1 %collective-permute-done.14.across_in = bf16[4,256,128]{2,1,0:T(8,128)(2,1)S(1)} collective-permute-done((bf16[4,256,128]{2,1,0:T(8,128)(2,1)S(1)}, bf16[4,256,128]{2,1,0:T(8,128)(2,1)S(1)}, u32[]{:S(2)}, u32[]{:S(2)}) %collective-permute-start.14) | collective-permute-done | bytes 262176 | tf_op jit(solution)/shard_map/ppermute | solution.py:151
  50.3 2.3 %adjoint.3 = (f32[4,256,128]{2,1,0:T(8,128)}, bf16[4,128,256]{2,1,0:T(8,128)(2,1)S(1)}, bf16[4,256,128]{2,1,0:T(8,128)(2,1)S(1)}, bf16[4,256,128]{2,1,0:T(8,128)...) custom-call(s32[2]{0:T(128)S(1)} %pad_add_fusion.rows, s32[32]{0:T(128)S(1)} %reshape.57.slots, ...), custom_call_target="tpu_custom_call" | custom-call | flops 268435456 | bytes 2097152 | tf_op jit(solution)/shard_map/adjoint/pallas_call | solution.py:346
  52.6 2.3 %collective-permute-start.16 = (bf16[4,256,128]{2,1,0:T(8,128)(2,1)S(1)}, bf16[4,256,128]{2,1,0:T(8,128)(2,1)S(1)}, u32[]{:S(2)}, u32[]{:S(2)}) collective-permute-start(bf16[4,256,128]{2,1,0:T(8,128)(2,1)S(1)} %get-tuple-element.47), channel_id=1, source_target_pairs={{0,2},{2,0},{4,6},{6,4},{8,10},{10,8},{12,14},{14,12},{16,18},{18,... | collective-permute-start | bytes 786440 | tf_op jit(solution)/shard_map/ppermute | solution.py:156
  55.3 1.4 %collective-permute-done.5 = bf16[4,128,256]{2,1,0:T(8,128)(2,1)S(1)} collective-permute-done((bf16[4,128,256]{2,1,0:T(8,128)(2,1)S(1)}, bf16[4,128,256]{2,1,0:T(8,128)(2,1)S(1)}, u32[]{:S(2)}, u32[]{:S(2)}) %collective-permute-start.5) | collective-permute-done | bytes 262176 | tf_op jit(solution)/shard_map/ppermute | solution.py:156
  56.7 1.8 %forward.3 = (f32[4,128,256]{2,1,0:T(8,128)}, bf16[4,128,256]{2,1,0:T(8,128)(2,1)S(1)}, f32[4,128,256]{2,1,0:T(8,128)S(1)}) custom-call(s32[2]{0:T(128)S(1)} %pad_add_fusion.rows, s32[32]{0:T(128)S(1)} %reshape.57.slots, f32[5]{0:T(128)S(1)} %copy-done.2, bf16[2,2,8,128,128]{4,3,2,1,0:T(8,128)(2,1)S(1)} %copy-done.1, ...), custom_call_target="tpu_custom_call" | custom-call | flops 268435456 | bytes 2097152 | tf_op jit(solution)/shard_map/forward/pallas_call | solution.py:346
  60.2 6.1 %collective-permute-done.6 = bf16[4,128,256]{2,1,0:T(8,128)(2,1)S(1)} collective-permute-done((bf16[4,128,256]{2,1,0:T(8,128)(2,1)S(1)}, bf16[4,128,256]{2,1,0:T(8,128)(2,1)S(1)}, u32[]{:S(2)}, u32[]{:S(2)}) %collective-permute-start.6) | collective-permute-done | bytes 262176 | tf_op jit(solution)/shard_map/ppermute | solution.py:151
  66.3 1.7 %collective-permute-start.7 = (bf16[4,128,256]{2,1,0:T(8,128)(2,1)S(1)}, bf16[4,128,256]{2,1,0:T(8,128)(2,1)S(1)}, u32[]{:S(2)}, u32[]{:S(2)}) collective-permute-start(bf16[4,128,256]{2,1,0:T(8,128)(2,1)S(1)} %pad_maximum_fusion.4), channel_id=1, source_target_pairs={{0,30},{2,4},{4,2},{6,8},{8,6},{10,12},{12,10},{14,16},{16,14},{18... | collective-permute-start | bytes 786440 | tf_op jit(solution)/shard_map/ppermute | solution.py:162
  68.0 3.9 %collective-permute-done.17.across_ref = bf16[4,256,128]{2,1,0:T(8,128)(2,1)S(1)} collective-permute-done((bf16[4,256,128]{2,1,0:T(8,128)(2,1)S(1)}, bf16[4,256,128]{2,1,0:T(8,128)(2,1)S(1)}, u32[]{:S(2)}, u32[]{:S(2)}) %collective-permute-start.17) | collective-permute-done | bytes 262176 | tf_op jit(solution)/shard_map/ppermute | solution.py:151
  71.9 2.4 %early_gradient.1.early_ref = f32[4,8,128,128]{3,2,1,0:T(8,128)S(1)} custom-call(s32[2]{0:T(128)S(1)} %pad_add_fusion.rows, s32[32]{0:T(128)S(1)} %reshape.57.slots, f32[5]{0:T(128)S(1)} %copy-done.2, bf16[4,256,128]{2,1,0:T(8,128)(2,1)S(1)} %get-tuple-element.36.cot_t_ref, f32[4,256,128]{2,1,0:T(8,128)S(1)} %get-tuple-element.45.own_ref, ...), custom_call_target="tpu_custom_call" | custom-call | flops 805306368 | bytes 2097152 | tf_op jit(solution)/shard_map/early_gradient/pallas_call | solution.py:346
  74.4 2.2 %collective-permute-start.8 = (bf16[4,128,256]{2,1,0:T(8,128)(2,1)S(1)}, bf16[4,128,256]{2,1,0:T(8,128)(2,1)S(1)}, u32[]{:S(2)}, u32[]{:S(2)}) collective-permute-start(bf16[4,128,256]{2,1,0:T(8,128)(2,1)S(1)} %pad_maximum_fusion.5), channel_id=1, source_target_pairs={{0,2},{2,0},{4,6},{6,4},{8,10},{10,8},{12,14},{14,12},{16,18},{18,... | collective-permute-start | bytes 786440 | tf_op jit(solution)/shard_map/ppermute | solution.py:156
  77.8 2.3 %last.1 = (f32[2,2,128,256]{3,2,1,0:T(8,128)}, bf16[2,2,8,128,128]{4,3,2,1,0:T(8,128)(2,1)}) custom-call(s32[2]{0:T(128)S(1)} %pad_add_fusion.rows, s32[32]{0:T(128)S(1)} %reshape.57.slots, f32[5]{0:T(128)S(1)} %copy-done.2, bf16[2,2,8,128,128]{4,3,2,1,0:T(8,128)(2,1)S(1)} %copy-done.1, ...), custom_call_target="tpu_custom_call" | custom-call | flops 536870912 | bytes 2097152 | tf_op jit(solution)/shard_map/last/pallas_call | solution.py:346
  (75 shorter events, 12.8 us)
Async XLA Ops:
  1.8 1.2 %copy-start = (bf16[2,2,8,128,128]{4,3,2,1,0:T(8,128)(2,1)S(1)}, bf16[2,2,8,128,128]{4,3,2,1,0:T(8,128)(2,1)}, u32[]{:S(2)}) copy-start(bf16[2,2,8,128,128]{4,3,2,1,0:T(8,128)(2,1)} %h_ref.9) | copy-start | bytes 3145732
  3.1 0.7 copy-start.2
  3.7 0.9 %copy-start.3 = (bf16[2,2,128,256]{3,2,1,0:T(8,128)(2,1)S(1)}, bf16[2,2,128,256]{3,2,1,0:T(8,128)(2,1)}, u32[]{:S(2)}) copy-start(bf16[2,2,128,256]{3,2,1,0:T(8,128)(2,1)} %cot_hbm.1) | copy-start | bytes 786436
  4.7 0.7 copy-start.4
  10.1 18.1 %copy-start.1 = (bf16[2,2,8,128,128]{4,3,2,1,0:T(8,128)(2,1)S(1)}, bf16[2,2,8,128,128]{4,3,2,1,0:T(8,128)(2,1)}, u32[]{:S(2)}) copy-start(bf16[2,2,8,128,128]{4,3,2,1,0:T(8,128)(2,1)} %h_ref.9) | copy-start | bytes 3145732
  10.2 8.1 %collective-permute-start = (bf16[4,128,256]{2,1,0:T(8,128)(2,1)S(1)}, bf16[4,128,256]{2,1,0:T(8,128)(2,1)S(1)}, u32[]{:S(2)}, u32[]{:S(2)}) collective-permute-start(bf16[4,128,256]{2,1,0:T(8,128)(2,1)S(1)} %get-tuple-element.27), channel_id=1, source_target_pairs={{0,1},{1,0},{2,3},{3,2},{4,5},{5,4},{6,7},{7,6},{8,9},{9,8},{10,11... | collective-permute-start | bytes 786440 | tf_op jit(solution)/shard_map/ppermute | solution.py:151
  12.3 9.1 %collective-permute-start.9 = (bf16[4,256,128]{2,1,0:T(8,128)(2,1)S(1)}, bf16[4,256,128]{2,1,0:T(8,128)(2,1)S(1)}, u32[]{:S(2)}, u32[]{:S(2)}) collective-permute-start(bf16[4,256,128]{2,1,0:T(8,128)(2,1)S(1)} %get-tuple-element.38), channel_id=1, source_target_pairs={{0,30},{2,4},{4,2},{6,8},{8,6},{10,12},{12,10},{14,16},{16,14},{18... | collective-permute-start | bytes 786440 | tf_op jit(solution)/shard_map/ppermute | solution.py:162
  14.3 7.0 %collective-permute-start.10 = (bf16[4,256,128]{2,1,0:T(8,128)(2,1)S(1)}, bf16[4,256,128]{2,1,0:T(8,128)(2,1)S(1)}, u32[]{:S(2)}, u32[]{:S(2)}) collective-permute-start(bf16[4,256,128]{2,1,0:T(8,128)(2,1)S(1)} %get-tuple-element.39), channel_id=1, source_target_pairs={{0,2},{2,0},{4,6},{6,4},{8,10},{10,8},{12,14},{14,12},{16,18},{18,... | collective-permute-start | bytes 786440 | tf_op jit(solution)/shard_map/ppermute | solution.py:156
  18.3 9.8 %collective-permute-start.1 = (bf16[4,128,256]{2,1,0:T(8,128)(2,1)S(1)}, bf16[4,128,256]{2,1,0:T(8,128)(2,1)S(1)}, u32[]{:S(2)}, u32[]{:S(2)}) collective-permute-start(bf16[4,128,256]{2,1,0:T(8,128)(2,1)S(1)} %pad_maximum_fusion), channel_id=1, source_target_pairs={{0,30},{2,4},{4,2},{6,8},{8,6},{10,12},{12,10},{14,16},{16,14},{18... | collective-permute-start | bytes 786440 | tf_op jit(solution)/shard_map/ppermute | solution.py:162
  21.4 6.8 %collective-permute-start.11 = (bf16[4,256,128]{2,1,0:T(8,128)(2,1)S(1)}, bf16[4,256,128]{2,1,0:T(8,128)(2,1)S(1)}, u32[]{:S(2)}, u32[]{:S(2)}) collective-permute-start(bf16[4,256,128]{2,1,0:T(8,128)(2,1)S(1)} %add_convert_fusion.2), channel_id=1, source_target_pairs={{0,1},{1,0},{2,3},{3,2},{4,5},{5,4},{6,7},{7,6},{8,9},{9,8},{10,11... | collective-permute-start | bytes 786440 | tf_op jit(solution)/shard_map/ppermute | solution.py:151
  29.8 8.9 %collective-permute-start.12 = (bf16[4,256,128]{2,1,0:T(8,128)(2,1)S(1)}, bf16[4,256,128]{2,1,0:T(8,128)(2,1)S(1)}, u32[]{:S(2)}, u32[]{:S(2)}) collective-permute-start(bf16[4,256,128]{2,1,0:T(8,128)(2,1)S(1)} %get-tuple-element.42), channel_id=1, source_target_pairs={{0,30},{2,4},{4,2},{6,8},{8,6},{10,12},{12,10},{14,16},{16,14},{18... | collective-permute-start | bytes 786440 | tf_op jit(solution)/shard_map/ppermute | solution.py:162
  32.7 6.0 %collective-permute-start.13 = (bf16[4,256,128]{2,1,0:T(8,128)(2,1)S(1)}, bf16[4,256,128]{2,1,0:T(8,128)(2,1)S(1)}, u32[]{:S(2)}, u32[]{:S(2)}) collective-permute-start(bf16[4,256,128]{2,1,0:T(8,128)(2,1)S(1)} %get-tuple-element.43), channel_id=1, source_target_pairs={{0,2},{2,0},{4,6},{6,4},{8,10},{10,8},{12,14},{14,12},{16,18},{18,... | collective-permute-start | bytes 786440 | tf_op jit(solution)/shard_map/ppermute | solution.py:156
  34.3 1.6 %collective-permute-start.2 = (bf16[4,128,256]{2,1,0:T(8,128)(2,1)S(1)}, bf16[4,128,256]{2,1,0:T(8,128)(2,1)S(1)}, u32[]{:S(2)}, u32[]{:S(2)}) collective-permute-start(bf16[4,128,256]{2,1,0:T(8,128)(2,1)S(1)} %pad_maximum_fusion.1), channel_id=1, source_target_pairs={{0,2},{2,0},{4,6},{6,4},{8,10},{10,8},{12,14},{14,12},{16,18},{18,... | collective-permute-start | bytes 786440 | tf_op jit(solution)/shard_map/ppermute | solution.py:156
  37.0 7.7 %collective-permute-start.3 = (bf16[4,128,256]{2,1,0:T(8,128)(2,1)S(1)}, bf16[4,128,256]{2,1,0:T(8,128)(2,1)S(1)}, u32[]{:S(2)}, u32[]{:S(2)}) collective-permute-start(bf16[4,128,256]{2,1,0:T(8,128)(2,1)S(1)} %get-tuple-element.30), channel_id=1, source_target_pairs={{0,1},{1,0},{2,3},{3,2},{4,5},{5,4},{6,7},{7,6},{8,9},{9,8},{10,11... | collective-permute-start | bytes 786440 | tf_op jit(solution)/shard_map/ppermute | solution.py:151
  38.8 11.5 %collective-permute-start.14 = (bf16[4,256,128]{2,1,0:T(8,128)(2,1)S(1)}, bf16[4,256,128]{2,1,0:T(8,128)(2,1)S(1)}, u32[]{:S(2)}, u32[]{:S(2)}) collective-permute-start(bf16[4,256,128]{2,1,0:T(8,128)(2,1)S(1)} %add_convert_fusion.1), channel_id=1, source_target_pairs={{0,1},{1,0},{2,3},{3,2},{4,5},{5,4},{6,7},{7,6},{8,9},{9,8},{10,11... | collective-permute-start | bytes 786440 | tf_op jit(solution)/shard_map/ppermute | solution.py:151
  44.8 10.2 %collective-permute-start.4 = (bf16[4,128,256]{2,1,0:T(8,128)(2,1)S(1)}, bf16[4,128,256]{2,1,0:T(8,128)(2,1)S(1)}, u32[]{:S(2)}, u32[]{:S(2)}) collective-permute-start(bf16[4,128,256]{2,1,0:T(8,128)(2,1)S(1)} %pad_maximum_fusion.2), channel_id=1, source_target_pairs={{0,30},{2,4},{4,2},{6,8},{8,6},{10,12},{12,10},{14,16},{16,14},{18... | collective-permute-start | bytes 786440 | tf_op jit(solution)/shard_map/ppermute | solution.py:162
  52.6 6.8 %collective-permute-start.15 = (bf16[4,256,128]{2,1,0:T(8,128)(2,1)S(1)}, bf16[4,256,128]{2,1,0:T(8,128)(2,1)S(1)}, u32[]{:S(2)}, u32[]{:S(2)}) collective-permute-start(bf16[4,256,128]{2,1,0:T(8,128)(2,1)S(1)} %get-tuple-element.46), channel_id=1, source_target_pairs={{0,30},{2,4},{4,2},{6,8},{8,6},{10,12},{12,10},{14,16},{16,14},{18... | collective-permute-start | bytes 786440 | tf_op jit(solution)/shard_map/ppermute | solution.py:162
  52.6 6.9 %collective-permute-start.16 = (bf16[4,256,128]{2,1,0:T(8,128)(2,1)S(1)}, bf16[4,256,128]{2,1,0:T(8,128)(2,1)S(1)}, u32[]{:S(2)}, u32[]{:S(2)}) collective-permute-start(bf16[4,256,128]{2,1,0:T(8,128)(2,1)S(1)} %get-tuple-element.47), channel_id=1, source_target_pairs={{0,2},{2,0},{4,6},{6,4},{8,10},{10,8},{12,14},{14,12},{16,18},{18,... | collective-permute-start | bytes 786440 | tf_op jit(solution)/shard_map/ppermute | solution.py:156
  55.1 1.6 %collective-permute-start.5 = (bf16[4,128,256]{2,1,0:T(8,128)(2,1)S(1)}, bf16[4,128,256]{2,1,0:T(8,128)(2,1)S(1)}, u32[]{:S(2)}, u32[]{:S(2)}) collective-permute-start(bf16[4,128,256]{2,1,0:T(8,128)(2,1)S(1)} %pad_maximum_fusion.3), channel_id=1, source_target_pairs={{0,2},{2,0},{4,6},{6,4},{8,10},{10,8},{12,14},{14,12},{16,18},{18,... | collective-permute-start | bytes 786440 | tf_op jit(solution)/shard_map/ppermute | solution.py:156
  58.5 7.7 %collective-permute-start.6 = (bf16[4,128,256]{2,1,0:T(8,128)(2,1)S(1)}, bf16[4,128,256]{2,1,0:T(8,128)(2,1)S(1)}, u32[]{:S(2)}, u32[]{:S(2)}) collective-permute-start(bf16[4,128,256]{2,1,0:T(8,128)(2,1)S(1)} %get-tuple-element.32), channel_id=1, source_target_pairs={{0,1},{1,0},{2,3},{3,2},{4,5},{5,4},{6,7},{7,6},{8,9},{9,8},{10,11... | collective-permute-start | bytes 786440 | tf_op jit(solution)/shard_map/ppermute | solution.py:151
  59.5 12.3 %collective-permute-start.17 = (bf16[4,256,128]{2,1,0:T(8,128)(2,1)S(1)}, bf16[4,256,128]{2,1,0:T(8,128)(2,1)S(1)}, u32[]{:S(2)}, u32[]{:S(2)}) collective-permute-start(bf16[4,256,128]{2,1,0:T(8,128)(2,1)S(1)} %add_convert_fusion), channel_id=1, source_target_pairs={{0,1},{1,0},{2,3},{3,2},{4,5},{5,4},{6,7},{7,6},{8,9},{9,8},{10,11... | collective-permute-start | bytes 786440 | tf_op jit(solution)/shard_map/ppermute | solution.py:151
  66.3 8.0 %collective-permute-start.7 = (bf16[4,128,256]{2,1,0:T(8,128)(2,1)S(1)}, bf16[4,128,256]{2,1,0:T(8,128)(2,1)S(1)}, u32[]{:S(2)}, u32[]{:S(2)}) collective-permute-start(bf16[4,128,256]{2,1,0:T(8,128)(2,1)S(1)} %pad_maximum_fusion.4), channel_id=1, source_target_pairs={{0,30},{2,4},{4,2},{6,8},{8,6},{10,12},{12,10},{14,16},{16,14},{18... | collective-permute-start | bytes 786440 | tf_op jit(solution)/shard_map/ppermute | solution.py:162
  74.4 3.4 %collective-permute-start.8 = (bf16[4,128,256]{2,1,0:T(8,128)(2,1)S(1)}, bf16[4,128,256]{2,1,0:T(8,128)(2,1)S(1)}, u32[]{:S(2)}, u32[]{:S(2)}) collective-permute-start(bf16[4,128,256]{2,1,0:T(8,128)(2,1)S(1)} %pad_maximum_fusion.5), channel_id=1, source_target_pairs={{0,2},{2,0},{4,6},{6,4},{8,10},{10,8},{12,14},{14,12},{16,18},{18,... | collective-permute-start | bytes 786440 | tf_op jit(solution)/shard_map/ppermute | solution.py:156

commit v3 on v2

--- a/solution.py
+++ b/solution.py
@@ -142,7 +142,7 @@
 
 bf16 = jnp.bfloat16
 f32 = jnp.float32
-VMEM_BYTES = 40 * 1024 * 1024
+VMEM_BYTES = 16 * 1024 * 1024
 OWN = (4, 5, 8, 9)
 ACROSS = (6, 7, 10, 11)
 
@@ -199,33 +199,71 @@
         across_ref[at] = sums[ACROSS[at]]
 
 
+def fill_window(parts, window):
+    for at, part in enumerate(parts):
+        window[4 * at : 4 * at + 4] = part[...]
+
+
+def pack_rows_kernel(own_ref, across_ref, outer_ref, inner_ref):
+    outer_ref[0:2] = own_ref[0:2]
+    outer_ref[2:4] = across_ref[0:2]
+    inner_ref[0:2] = own_ref[2:4]
+    inner_ref[2:4] = across_ref[2:4]
+
+
+def pack_across_kernel(across_ref, far_ref, near_ref, packed_ref):
+    packed_ref[0:2] = (across_ref[0:2] + far_ref[2:4].astype(f32)).astype(bf16)
+    packed_ref[2:4] = (across_ref[2:4] + near_ref[2:4].astype(f32)).astype(bf16)
+
+
 def first_kernel(
-    top, rows, slots, place, coef, seeds_ref, h_hbm, cot_hbm,
+    top, span_x, span_y, position, seeds_hbm, coef_hbm, codes_hbm, h_hbm, cot_hbm,
     start_ref, term_ref, rounded_ref, cot_t_ref, adjoint_ref, far_ref, near_ref, own_ref, across_ref,
-    h_ref, cot_ref, sums, h_sem, cot_sem,
+    rows_out, slots_out, seeds_ref, coef, codes, h_ref, cot_ref, sums, small_sem, h_sem, cot_sem,
 ):
-    copies = []
+    gx, gy = position[0], position[1]
+    odd = lax.rem(gx, 2)
+    rows = (odd, 1 - odd)
+    small = [
+        pltpu.make_async_copy(source, target, small_sem.at[at])
+        for at, (source, target) in enumerate(((seeds_hbm, seeds_ref), (codes_hbm, codes), (coef_hbm, coef)))
+    ]
+    for copy in small:
+        copy.start()
+    h_copies, cot_copies = [], []
     for at in range(4):
         source = (rows[at // 2], at % 2)
-        copies.append(
-            (
-                pltpu.make_async_copy(h_hbm.at[source], h_ref.at[source], h_sem.at[at]),
-                pltpu.make_async_copy(cot_hbm.at[source], cot_ref.at[at], cot_sem.at[at]),
-            )
-        )
-    for pair in copies:
-        for copy in pair:
-            copy.start()
+        h_copies.append(pltpu.make_async_copy(h_hbm.at[source], h_ref.at[source], h_sem.at[at]))
+        cot_copies.append(pltpu.make_async_copy(cot_hbm.at[source], cot_ref.at[at], cot_sem.at[at]))
+    for copy in h_copies + cot_copies:
+        copy.start()
+    sums[...] = jnp.zeros_like(sums)
+    for copy in small:
+        copy.wait()
+    listed, width = h_ref.shape[2:4]
     for slot in range(16):
-        start_ref[slot] = start_signs(place[slot], seeds_ref[...], h_ref.shape[3])
-    sums[...] = jnp.zeros_like(sums)
-    for at in range(4):
-        copies[at][0].wait()
+        local = jnp.where(odd == 0, slot // 4 - 1, 2 - slot // 4)
+        place_x = lax.rem(gx * 2 + local + span_x, span_x)
+        place_y = lax.rem(gy * 2 + slot % 4, span_y)
+        start_ref[slot] = start_signs((place_x * span_y + place_y) * width, seeds_ref[...], width)
+    slots = []
+    for at in range(4):
+        for k in range(listed):
+            code = codes[rows[at // 2], at % 2, k]
+            step_x = jnp.where(code >= 6, 1, jnp.where(code >= 3, 0, -1))
+            step_y = code - 3 * step_x - 4
+            slots.append((1 + at // 2 + (1 - 2 * odd) * step_x) * 4 + lax.rem(at % 2 + step_y + 4, 4))
+    for at in range(2):
+        rows_out[at] = rows[at]
+    for at in range(4 * listed):
+        slots_out[at] = slots[at]
+    for at in range(4):
+        h_copies[at].wait()
         value = window_product(slots, rows, at, h_ref, start_ref)
         term_ref[at] = value
         rounded_ref[at] = value.astype(bf16)
     for at in range(4):
-        copies[at][1].wait()
+        cot_copies[at].wait()
         cot = cot_ref[at].astype(f32)
         cot_t = jnp.transpose(cot)
         cot_t_ref[at] = cot_t.astype(bf16)
@@ -234,14 +272,19 @@
     finish_push(sums, far_ref, near_ref, own_ref, across_ref)
 
 
-def forward_kernel(index, rows, slots, coef, h_ref, window, before_ref, sums_ref, term_ref, rounded_ref, density_ref):
+def forward_kernel(
+    index, rows, slots, coef, h_ref, far, outer, inner, near, before_ref, sums_ref, rounded_ref, density_ref, *rest
+):
+    term_ref, window = rest[:-1], rest[-1]
+    fill_window((far, outer, inner, near), window)
     for at in range(4):
         before = (before_ref[OWN[at]] if index == 2 else before_ref[at]).astype(f32)
         value = 2.0 * window_product(slots, rows, at, h_ref, window) - before
         sums = coef[0] * before + coef[1] * sums_ref[at] if index == 2 else sums_ref[at]
-        term_ref[at] = value
         rounded_ref[at] = value.astype(bf16)
         density_ref[at] = sums + coef[index] * value
+        for ref in term_ref:
+            ref[at] = value
 
 
 def adjoint_value(at, index, coef, cot_t_ref, own_ref, far_ref, near_ref, across_ref):
@@ -252,14 +295,16 @@
 
 def adjoint_kernel(
     index, top, rows, slots, coef, h_ref, cot_t_ref, own_in, far_in, near_in, across_in,
-    value_ref, rounded_ref, far_ref, near_ref, own_ref, across_ref, sums,
+    rounded_ref, far_ref, near_ref, own_ref, across_ref, *rest,
 ):
+    value_refs, sums = rest[:-1], rest[-1]
     sums[...] = jnp.zeros_like(sums)
     for at in range(4):
         value = adjoint_value(at, index, coef, cot_t_ref, own_in, far_in, near_in, across_in)
         if index + 2 == top:
             value = value - coef[top] * cot_t_ref[at].astype(f32)
-        value_ref[at] = value
+        for ref in value_refs:
+            ref[at] = value
         push(slots, rows, at, h_ref, value.astype(bf16), sums)
         rounded_ref[at] = jnp.transpose(value).astype(bf16)
     finish_push(sums, far_ref, near_ref, own_ref, across_ref)
@@ -272,23 +317,38 @@
         store(k, lax.dot_general(left, right, (((1,), (1,)), ((), ())), preferred_element_type=f32))
 
 
-def early_gradient_kernel(terms, rows, slots, coef, cot_t_ref, own_ref, far_ref, near_ref, across_ref, older_ref, *rest):
-    adjoints, windows, sums_ref = rest[: terms - 3], rest[terms - 3 : -1], rest[-1]
+def middle_gradient_kernel(count, slots, *refs):
+    adjoints, parts, (sums_ref, windows) = refs[:count], refs[count : 5 * count], refs[5 * count :]
     listed = sums_ref.shape[1]
-    for at in range(4):
-        value = adjoint_value(at, 1, coef, cot_t_ref, own_ref, far_ref, near_ref, across_ref) - older_ref[at]
-        left = [jnp.transpose(value).astype(bf16)] + [a[at] * bf16(2.0) for a in adjoints]
+    for t in range(count):
+        fill_window(parts[4 * t : 4 * t + 4], windows.at[t])
+    for at in range(4):
+        left = jnp.concatenate([a[at] * bf16(2.0) for a in adjoints], axis=1)
 
         def store(k, total, at=at):
             sums_ref[at, k] = total
 
-        block_gradients(slots, at, jnp.concatenate(left, axis=1), windows, listed, store)
+        block_gradients(slots, at, left, [windows.at[t] for t in range(count)], listed, store)
+
+
+def first_gradient_kernel(
+    slots, coef, cot_t_ref, own_ref, far_ref, near_ref, across_ref, older_ref, start_ref, before_ref, sums_ref
+):
+    listed = sums_ref.shape[1]
+    for at in range(4):
+        value = adjoint_value(at, 1, coef, cot_t_ref, own_ref, far_ref, near_ref, across_ref) - older_ref[at]
+
+        def store(k, total, at=at):
+            sums_ref[at, k] = before_ref[at, k] + total
+
+        block_gradients(slots, at, jnp.transpose(value).astype(bf16), (start_ref,), listed, store)
 
 
 def last_kernel(
-    index, scale, rows, slots, coef, h_ref, window, before_ref, sums_ref, adjoint_ref, early_ref,
-    density_hbm, grad_hbm, density, grad, density_sem, grad_sem,
+    index, scale, rows, slots, coef, h_ref, far, outer, inner, near, before_ref, sums_ref, adjoint_ref, early_ref,
+    density_hbm, grad_hbm, density, grad, window, density_sem, grad_sem,
 ):
+    fill_window((far, outer, inner, near), window)
     listed = h_ref.shape[2]
     copies = []
     for at in range(4):
@@ -316,21 +376,9 @@
     blocks = rows_x * rows_y
     span_x = rows_x * lax.axis_size("gx")
     span_y = rows_y * lax.axis_size("gy")
-    odd = lax.axis_index("gx") % 2
-    four = jnp.arange(4, dtype=jnp.int32)
-    local_row = jnp.where(odd == 0, four - 1, 2 - four)
-    place_x = (lax.axis_index("gx") * rows_x + local_row) % span_x
-    place_y = (lax.axis_index("gy") * rows_y + four) % span_y
-    place = ((place_x[:, None] * span_y + place_y) * width).reshape(-1).astype(jnp.int32)
-    rows = jnp.stack([odd, 1 - odd]).astype(jnp.int32)
-    codes = jnp.where(odd == 0, neighbours, neighbours[::-1])
-    window_row = 1 + jnp.arange(2, dtype=jnp.int32)[:, None, None] + (1 - 2 * odd) * (codes // 3 - 1)
-    window_col = (jnp.arange(2, dtype=jnp.int32)[None, :, None] + codes % 3 - 1) % 4
-    slots = (window_row * 4 + window_col).reshape(-1).astype(jnp.int32)
-
     vmem = pl.BlockSpec(memory_space=pltpu.VMEM)
     smem = pl.BlockSpec(memory_space=pltpu.SMEM)
-    outside = pl.BlockSpec(memory_space=pl.ANY)
+    hbm = pl.BlockSpec(memory_space=pltpu.HBM)
 
     def field(count, dtype):
         return jax.ShapeDtypeStruct((count, width, probes), dtype)
@@ -341,6 +389,11 @@
     apply_flops = 2 * blocks * listed * width * width * probes
     pushed = [turned(4, bf16), turned(4, bf16), turned(4, f32), turned(4, f32)]
     sums_scratch = pltpu.VMEM((16, probes, width), f32)
+
+    window_scratch = pltpu.VMEM((16, width, probes), bf16)
+
+    def kept(values):
+        return tuple(pltpu.with_memory_space_constraint(value, pltpu.VMEM) for value in values)
 
     def call(name, kernel, scalars, operands, out_shape, scratch=(), flops=apply_flops, out_specs=None, in_specs=None):
         return pl.pallas_call(
@@ -354,66 +407,91 @@
             name=name,
         )(*scalars, *operands)
 
-    scalars = (rows, slots, coefficients)
-    start, term, rounded, cot_t, adjoint, *sent = call(
+    start, term, rounded, cot_t, adjoint, *sent, rows, slots = call(
         "first",
-        functools.partial(first_kernel, top),
-        (rows, slots, place, coefficients),
-        (probe_seeds.reshape(1, probes), hamiltonian, cotangent),
-        [field(16, bf16), field(4, f32), field(4, bf16), turned(4, bf16), field(4, bf16)] + pushed,
+        functools.partial(first_kernel, top, span_x, span_y),
+        (jnp.stack([lax.axis_index("gx"), lax.axis_index("gy")]).astype(jnp.int32),),
+        tuple(
+            pltpu.with_memory_space_constraint(value, pltpu.HBM)
+            for value in (probe_seeds.reshape(1, probes), coefficients, neighbours, hamiltonian, cotangent)
+        ),
+        [field(16, bf16), field(4, f32), field(4, bf16), turned(4, bf16), field(4, bf16)]
+        + pushed
+        + [jax.ShapeDtypeStruct((2,), jnp.int32), jax.ShapeDtypeStruct((blocks * listed,), jnp.int32)],
+        out_specs=[vmem] * 9 + [smem] * 2,
         scratch=(
+            pltpu.VMEM((1, probes), jnp.int32),
+            pltpu.SMEM(coefficients.shape, f32),
+            pltpu.SMEM(neighbours.shape, jnp.int32),
             pltpu.VMEM(hamiltonian.shape, bf16),
             pltpu.VMEM((4, width, probes), bf16),
             sums_scratch,
+            pltpu.SemaphoreType.DMA((3,)),
             pltpu.SemaphoreType.DMA((4,)),
             pltpu.SemaphoreType.DMA((4,)),
         ),
         flops=2 * apply_flops,
-        in_specs=[vmem, outside, outside],
-    )
+        in_specs=[hbm] * 5,
+    )
+    scalars = (rows, slots, coefficients)
     adjoints = {top: adjoint}
-    values = {}
-    windows = [start]
+    windows = [(start,)]
     before, sums = start, term
     for index in range(2, terms):
-        across = swap_y(rounded)
-        outer = jnp.concatenate([rounded[:2], across[:2]])
-        inner = jnp.concatenate([rounded[2:], across[2:]])
-        window = jnp.concatenate([swap_far(outer), outer, inner, swap_near(inner)])
+        at = terms - index
+        outer, inner = call(
+            "pack_rows", pack_rows_kernel, (), kept((rounded, swap_y(rounded))), [field(4, bf16)] * 2, flops=0
+        )
+        far, near = swap_far(outer), swap_near(inner)
         to_far, to_near, own, to_across = sent
-        far, near = swap_far(to_far), swap_near(to_near)
-        to_across = to_across + jnp.concatenate([far[2:], near[2:]]).astype(f32)
-        arrived = (cot_t, own, far, near, swap_y(to_across.astype(bf16)))
-
+        from_far, from_near = swap_far(to_far), swap_near(to_near)
+        (to_across,) = call(
+            "pack_across", pack_across_kernel, (), kept((to_across, from_far, from_near)), [turned(4, bf16)], flops=0
+        )
+        from_across, _ = lax.optimization_barrier((swap_y(to_across), near))
+        arrived = kept((cot_t, own, from_far, from_near, from_across))
+        window = kept((far, outer, inner, near))
         windows.append(window)
-        at = terms - index
-        if index < top:
-            following, rounded, density = call(
-                "forward",
-                functools.partial(forward_kernel, index),
-                scalars, (hamiltonian, window, before, sums),
-                [field(4, f32), field(4, bf16), field(4, f32)],
-            )
-            before, sums, term = term, density, following
-            values[at], adjoints[at], *sent = call(
-                "adjoint",
-                functools.partial(adjoint_kernel, at, top),
-                scalars, (hamiltonian,) + arrived,
-                [turned(4, f32), field(4, bf16)] + pushed,
-                scratch=(sums_scratch,),
-            )
+        if index == top:
+            break
+        rounded, density, *following = call(
+            "forward",
+            functools.partial(forward_kernel, index),
+            scalars, (hamiltonian,) + window + kept((before, sums)),
+            [field(4, bf16), field(4, f32)] + [field(4, f32)] * (index + 2 <= top),
+            scratch=(window_scratch,),
+        )
+        before, sums = term, density
+        if following:
+            term = following[0]
+        adjoints[at], *sent = call(
+            "adjoint",
+            functools.partial(adjoint_kernel, at, top),
+            scalars, (hamiltonian,) + arrived,
+            [field(4, bf16)] + pushed + [turned(4, f32)] * (at == 3),
+            scratch=(sums_scratch,),
+        )
+        if at == 3:
+            older = sent.pop()
+    gradient_sums = jax.ShapeDtypeStruct((blocks, listed, width, width), f32)
+    middle = call(
+        "middle_gradient",
+        functools.partial(middle_gradient_kernel, terms - 3),
+        (slots,), tuple(adjoints[t] for t in range(2, top)) + windows[1] + windows[2],
+        [gradient_sums],
+        scratch=(pltpu.VMEM((terms - 3, 16, width, probes), bf16),),
+        flops=(terms - 3) * apply_flops,
+    )[0]
     early = call(
-        "early_gradient",
-        functools.partial(early_gradient_kernel, terms),
-        scalars,
-        arrived + (values[3],) + tuple(adjoints[t] for t in range(2, top)) + tuple(windows[: top - 1]),
-        [jax.ShapeDtypeStruct((blocks, listed, width, width), f32)],
-        flops=(terms - 2) * apply_flops,
+        "first_gradient",
+        first_gradient_kernel,
+        (slots, coefficients), arrived + (older, start, middle),
+        [gradient_sums],
     )[0]
     density, gradient = call(
         "last",
         functools.partial(last_kernel, top, 1.0 / probes),
-        scalars, (hamiltonian, windows[top - 1], before, sums, adjoints[top], early),
+        scalars, (hamiltonian,) + windows[top - 1] + kept((before, sums, adjoints[top], early)),
         [
             jax.ShapeDtypeStruct(cotangent.shape, f32),
             jax.ShapeDtypeStruct(hamiltonian.shape, bf16),
@@ -421,11 +499,12 @@
         scratch=(
             pltpu.VMEM((4, width, probes), f32),
             pltpu.VMEM((blocks, listed, width, width), bf16),
+            window_scratch,
             pltpu.SemaphoreType.DMA((4,)),
             pltpu.SemaphoreType.DMA((4,)),
         ),
         flops=2 * apply_flops,
-        out_specs=[outside, outside],
+        out_specs=[hbm, hbm],
     )
     return density, gradient
 

time: 80.7 us -> 70.9 us (0.88)
  local copies, waits for them, and re-layouts: 4.09 us -> 0.01 us
  waiting for transfers between devices: 31.3 us -> 28.1 us
  starting transfers between devices: 26.1 us -> 24.7 us
  other arithmetic: 1.33 us -> 0.08 us
    ppermute x6, starting transfers between devices: 9.75 us -> 3.46 us  [swap_far(): return lax.ppermute(value, 'gx', pairs)]
    ppermute x6, starting transfers between devices: 7.42 us -> 12.1 us  [swap_y(): return lax.ppermute(value, 'gy', [(0, 1), (1, 0)])]
    ppermute x6, waiting for transfers between devices: 4.04 us -> 0.02 us  [swap_near(): return lax.ppermute(value, 'gx', [(i, i ^ 1) for i in range(count)])]
    unnamed x19 -> x4, local copies, waits for them, and re-layouts: 3.63 us -> 0.01 us
    ppermute x6, waiting for transfers between devices: 7.42 us -> 10.1 us  [swap_far(): return lax.ppermute(value, 'gx', pairs)]
    ppermute x6, waiting for transfers between devices: 19.9 us -> 18 us  [swap_y(): return lax.ppermute(value, 'gy', [(0, 1), (1, 0)])]
    add x2 -> x0, other arithmetic: 0.84 us -> none  [the longest x1 0.83 us: pair_shards(): slots = (window_row * 4 + window_col).reshape(-1).astype(jnp.int32)]
    pallas_call x7 -> x14, Pallas kernels: 16.3 us -> 17.1 us  [call(): pl.pallas_call(kernel, in_specs=[smem] * len(scalars) + (in_specs or [vme...]
  transfers between devices with their start and end apart: 18 -> 18, of which waited for: 11 -> 9; matrix products, arithmetic and copies ran while one was open for 1% -> 0% of each run, Pallas kernels for 9% -> 13%
where the time goes in v3:
time: 70.9 us; the launch traced here: 70.8 us
  waiting for transfers between devices  28.1 us (40%)
  starting transfers between devices  24.7 us (35%)
  Pallas kernels  17.1 us (24%)
  between operations  0.76 us (1%)
    ppermute x6, waiting for transfers between devices, swap_y(): return lax.ppermute(value, 'gy', [(0, 1), (1, 0)])  18 us
    pallas_call x14, Pallas kernels, call(): pl.pallas_call(kernel, in_specs=[smem] * len(scalars) + (in_specs or [vme...  17.1 us
    ppermute x6, starting transfers between devices, swap_y(): return lax.ppermute(value, 'gy', [(0, 1), (1, 0)])  12.1 us
    ppermute x6, waiting for transfers between devices, swap_far(): return lax.ppermute(value, 'gx', pairs)  10.1 us
    ppermute x6, starting transfers between devices, swap_near(): return lax.ppermute(value, 'gx', [(i, i ^ 1) for i in range(count)])  9.14 us
    ppermute x6, starting transfers between devices, swap_far(): return lax.ppermute(value, 'gx', pairs)  3.46 us
  transfers between devices with their start and end apart: 18, of which 9 were waited for; matrix products, arithmetic and copies ran while one was open for 0% of the time, Pallas kernels for 13%

profile of v3, /device:TPU:1, one launch (start us, length us, event | category | flops | bytes accessed | tf_op | source)
XLA Modules:
  0.0 70.8 jit_solution(8468618295101744931)
XLA Ops:
  0.7 5.6 %first.1 = (bf16[16,128,256]{2,1,0:T(8,128)(2,1)S(1)}, f32[4,128,256]{2,1,0:T(8,128)S(1)}, bf16[4,128,256]{2,1,0:T(8,128)(2,1)S(1)}, bf16[4,256,128]{2,1,0:T(8,1...) custom-call(s32[2]{0:T(128)S(1)} %pad_add_fusion.position, ...), custom_call_target="tpu_custom_call" | custom-call | flops 536870912 | bytes 2097152 | tf_op jit(solution)/shard_map/first/pallas_call | solution.py:399
  6.5 2.7 %collective-permute-start.9 = (bf16[4,256,128]{2,1,0:T(8,128)(2,1)S(1)}, bf16[4,256,128]{2,1,0:T(8,128)(2,1)S(1)}, u32[]{:S(2)}, u32[]{:S(2)}) collective-permute-start(bf16[4,256,128]{2,1,0:T(8,128)(2,1)S(1)} %get-tuple-element.57), channel_id=1, source_target_pairs={{0,30},{2,4},{4,2},{6,8},{8,6},{10,12},{12,10},{14,16},{16,14},{18... | collective-permute-start | bytes 786440 | tf_op jit(solution)/shard_map/ppermute | solution.py:162
  9.1 1.2 %collective-permute-start = (bf16[4,128,256]{2,1,0:T(8,128)(2,1)S(1)}, bf16[4,128,256]{2,1,0:T(8,128)(2,1)S(1)}, u32[]{:S(2)}, u32[]{:S(2)}) collective-permute-start(bf16[4,128,256]{2,1,0:T(8,128)(2,1)S(1)} %get-tuple-element.40.own_ref), channel_id=1, source_target_pairs={{0,1},{1,0},{2,3},{3,2},{4,5},{5,4},{6,7},{7,6},{8,9},{9,8},{10,11... | collective-permute-start | bytes 786440 | tf_op jit(solution)/shard_map/ppermute | solution.py:151
  10.3 4.9 %collective-permute-done.9.far_ref.far_in = bf16[4,256,128]{2,1,0:T(8,128)(2,1)S(1)} collective-permute-done((bf16[4,256,128]{2,1,0:T(8,128)(2,1)S(1)}, bf16[4,256,128]{2,1,0:T(8,128)(2,1)S(1)}, u32[]{:S(2)}, u32[]{:S(2)}) %collective-permute-start.9) | collective-permute-done | bytes 262176 | tf_op jit(solution)/shard_map/ppermute | solution.py:162
  15.3 2.8 %collective-permute-start.11 = (bf16[4,256,128]{2,1,0:T(8,128)(2,1)S(1)}, bf16[4,256,128]{2,1,0:T(8,128)(2,1)S(1)}, u32[]{:S(2)}, u32[]{:S(2)}) collective-permute-start(bf16[4,256,128]{2,1,0:T(8,128)(2,1)S(1)} %pack_across.3), channel_id=1, source_target_pairs={{0,1},{1,0},{2,3},{3,2},{4,5},{5,4},{6,7},{7,6},{8,9},{9,8},{10,11... | collective-permute-start | bytes 786440 | tf_op jit(solution)/shard_map/ppermute | solution.py:151
  19.5 5.0 %collective-permute-done.11.across_in = bf16[4,256,128]{2,1,0:T(8,128)(2,1)S(1)} collective-permute-done((bf16[4,256,128]{2,1,0:T(8,128)(2,1)S(1)}, bf16[4,256,128]{2,1,0:T(8,128)(2,1)S(1)}, u32[]{:S(2)}, u32[]{:S(2)}) %collective-permute-start.11) | collective-permute-done | bytes 262176 | tf_op jit(solution)/shard_map/ppermute | solution.py:151
  24.5 1.6 %adjoint.2 = (bf16[4,128,256]{2,1,0:T(8,128)(2,1)S(1)}, bf16[4,256,128]{2,1,0:T(8,128)(2,1)S(1)}, bf16[4,256,128]{2,1,0:T(8,128)(2,1)S(1)}, f32[4,256,128]{2,1,0...) custom-call(s32[2]{0:T(128)S(1)} %get-tuple-element.38.rows, s32[32]{0:T(128)S(1)} %get-tuple-element.39.slots, ...), custom_call_target="tpu_custom_call" | custom-call | flops 268435456 | bytes 2097152 | tf_op jit(solution)/shard_map/adjoint/pallas_call | solution.py:399
  26.4 3.8 %collective-permute-start.13 = (bf16[4,256,128]{2,1,0:T(8,128)(2,1)S(1)}, bf16[4,256,128]{2,1,0:T(8,128)(2,1)S(1)}, u32[]{:S(2)}, u32[]{:S(2)}) collective-permute-start(bf16[4,256,128]{2,1,0:T(8,128)(2,1)S(1)} %get-tuple-element.63), channel_id=1, source_target_pairs={{0,2},{2,0},{4,6},{6,4},{8,10},{10,8},{12,14},{14,12},{16,18},{18,... | collective-permute-start | bytes 786440 | tf_op jit(solution)/shard_map/ppermute | solution.py:156
  31.3 1.3 %collective-permute-start.3 = (bf16[4,128,256]{2,1,0:T(8,128)(2,1)S(1)}, bf16[4,128,256]{2,1,0:T(8,128)(2,1)S(1)}, u32[]{:S(2)}, u32[]{:S(2)}) collective-permute-start(bf16[4,128,256]{2,1,0:T(8,128)(2,1)S(1)} %get-tuple-element.45.own_ref), channel_id=1, source_target_pairs={{0,1},{1,0},{2,3},{3,2},{4,5},{5,4},{6,7},{7,6},{8,9},{9,8},{10,11... | collective-permute-start | bytes 786440 | tf_op jit(solution)/shard_map/ppermute | solution.py:151
  32.7 4.2 %collective-permute-start.14 = (bf16[4,256,128]{2,1,0:T(8,128)(2,1)S(1)}, bf16[4,256,128]{2,1,0:T(8,128)(2,1)S(1)}, u32[]{:S(2)}, u32[]{:S(2)}) collective-permute-start(bf16[4,256,128]{2,1,0:T(8,128)(2,1)S(1)} %pack_across.4), channel_id=1, source_target_pairs={{0,1},{1,0},{2,3},{3,2},{4,5},{5,4},{6,7},{7,6},{8,9},{9,8},{10,11... | collective-permute-start | bytes 786440 | tf_op jit(solution)/shard_map/ppermute | solution.py:151
  36.9 2.4 %collective-permute-done.3.across_ref = bf16[4,128,256]{2,1,0:T(8,128)(2,1)S(1)} collective-permute-done((bf16[4,128,256]{2,1,0:T(8,128)(2,1)S(1)}, bf16[4,128,256]{2,1,0:T(8,128)(2,1)S(1)}, u32[]{:S(2)}, u32[]{:S(2)}) %collective-permute-start.3) | collective-permute-done | bytes 262176 | tf_op jit(solution)/shard_map/ppermute | solution.py:151
  39.4 1.2 %collective-permute-start.5 = (bf16[4,128,256]{2,1,0:T(8,128)(2,1)S(1)}, bf16[4,128,256]{2,1,0:T(8,128)(2,1)S(1)}, u32[]{:S(2)}, u32[]{:S(2)}) collective-permute-start(bf16[4,128,256]{2,1,0:T(8,128)(2,1)S(1)} %get-tuple-element.47.inner.refs_8_), channel_id=1, source_target_pairs={{0,2},{2,0},{4,6},{6,4},{8,10},{10,8},{12,14},{14,12},{16,18},{18,... | collective-permute-start | bytes 786440 | tf_op jit(solution)/shard_map/ppermute | solution.py:156
  40.6 4.3 %collective-permute-done.14.across_in = bf16[4,256,128]{2,1,0:T(8,128)(2,1)S(1)} collective-permute-done((bf16[4,256,128]{2,1,0:T(8,128)(2,1)S(1)}, bf16[4,256,128]{2,1,0:T(8,128)(2,1)S(1)}, u32[]{:S(2)}, u32[]{:S(2)}) %collective-permute-start.14) | collective-permute-done | bytes 262176 | tf_op jit(solution)/shard_map/ppermute | solution.py:151
  45.0 1.7 %adjoint.3 = (bf16[4,128,256]{2,1,0:T(8,128)(2,1)S(1)}, bf16[4,256,128]{2,1,0:T(8,128)(2,1)S(1)}, bf16[4,256,128]{2,1,0:T(8,128)(2,1)S(1)}, f32[4,256,128]{2,1,0:T(8,128)S(1)}, f32[4,256,128]{2,1,0:T(8,128)S(1)}) custom-call(s32[2]{0:T(128)S(1)} %get-tuple-element.38.rows, s32[32]{0:T(128)S(1)} %get-tuple-element.39.slots, f32[5]{0:T(128)S(1)} %copy-done.1, ...), custom_call_target="tpu_custom_call" | custom-call | flops 268435456 | bytes 2097152 | tf_op jit(solution)/shard_map/adjoint/pallas_call | solution.py:399
  46.7 1.7 %collective-permute-start.16 = (bf16[4,256,128]{2,1,0:T(8,128)(2,1)S(1)}, bf16[4,256,128]{2,1,0:T(8,128)(2,1)S(1)}, u32[]{:S(2)}, u32[]{:S(2)}) collective-permute-start(bf16[4,256,128]{2,1,0:T(8,128)(2,1)S(1)} %get-tuple-element.68), channel_id=1, source_target_pairs={{0,2},{2,0},{4,6},{6,4},{8,10},{10,8},{12,14},{14,12},{16,18},{18,... | collective-permute-start | bytes 786440 | tf_op jit(solution)/shard_map/ppermute | solution.py:156
  50.3 1.3 %collective-permute-start.6 = (bf16[4,128,256]{2,1,0:T(8,128)(2,1)S(1)}, bf16[4,128,256]{2,1,0:T(8,128)(2,1)S(1)}, u32[]{:S(2)}, u32[]{:S(2)}) collective-permute-start(bf16[4,128,256]{2,1,0:T(8,128)(2,1)S(1)} %get-tuple-element.49.own_ref), channel_id=1, source_target_pairs={{0,1},{1,0},{2,3},{3,2},{4,5},{5,4},{6,7},{7,6},{8,9},{9,8},{10,11... | collective-permute-start | bytes 786440 | tf_op jit(solution)/shard_map/ppermute | solution.py:151
  52.8 1.3 %collective-permute-start.17 = (bf16[4,256,128]{2,1,0:T(8,128)(2,1)S(1)}, bf16[4,256,128]{2,1,0:T(8,128)(2,1)S(1)}, u32[]{:S(2)}, u32[]{:S(2)}) collective-permute-start(bf16[4,256,128]{2,1,0:T(8,128)(2,1)S(1)} %pack_across.5), channel_id=1, source_target_pairs={{0,1},{1,0},{2,3},{3,2},{4,5},{5,4},{6,7},{7,6},{8,9},{9,8},{10,11... | collective-permute-start | bytes 786440 | tf_op jit(solution)/shard_map/ppermute | solution.py:151
  54.1 4.1 %collective-permute-done.6.across_ref = bf16[4,128,256]{2,1,0:T(8,128)(2,1)S(1)} collective-permute-done((bf16[4,128,256]{2,1,0:T(8,128)(2,1)S(1)}, bf16[4,128,256]{2,1,0:T(8,128)(2,1)S(1)}, u32[]{:S(2)}, u32[]{:S(2)}) %collective-permute-start.6) | collective-permute-done | bytes 262176 | tf_op jit(solution)/shard_map/ppermute | solution.py:151
  58.3 1.4 %collective-permute-start.8 = (bf16[4,128,256]{2,1,0:T(8,128)(2,1)S(1)}, bf16[4,128,256]{2,1,0:T(8,128)(2,1)S(1)}, u32[]{:S(2)}, u32[]{:S(2)}) collective-permute-start(bf16[4,128,256]{2,1,0:T(8,128)(2,1)S(1)} %get-tuple-element.51.inner), channel_id=1, source_target_pairs={{0,2},{2,0},{4,6},{6,4},{8,10},{10,8},{12,14},{14,12},{16,18},{18,... | collective-permute-start | bytes 786440 | tf_op jit(solution)/shard_map/ppermute | solution.py:156
  59.7 1.9 %middle_gradient.1.before_ref = f32[4,8,128,128]{3,2,1,0:T(8,128)S(1)} custom-call(s32[32]{0:T(128)S(1)} %get-tuple-element.39.slots, bf16[4,128,256]{2,1,0:T(8,128)(2,1)S(1)} %get-tuple-element.72.refs_0_, bf16[4,128,256]{2,1,0:T(8,128)(2,1)S(1)} %get-tuple-element.73.refs_1_, bf16[4,128,256]{2,1,0:T(8,128)(2,1)S(1)} %collective-permute-done.1.far.refs_2_, ...), custom_call_target="tpu_custom_call" | custom-call | flops 536870912 | bytes 2097152 | tf_op jit(solution)/shard_map/middle_gradient/pallas_call | solution.py:399
  61.6 2.1 %collective-permute-done.17.across_ref = bf16[4,256,128]{2,1,0:T(8,128)(2,1)S(1)} collective-permute-done((bf16[4,256,128]{2,1,0:T(8,128)(2,1)S(1)}, bf16[4,256,128]{2,1,0:T(8,128)(2,1)S(1)}, u32[]{:S(2)}, u32[]{:S(2)}) %collective-permute-start.17) | collective-permute-done | bytes 262176 | tf_op jit(solution)/shard_map/ppermute | solution.py:151
  63.7 1.4 %first_gradient.1.early_ref = f32[4,8,128,128]{3,2,1,0:T(8,128)S(1)} custom-call(s32[32]{0:T(128)S(1)} %get-tuple-element.39.slots, f32[5]{0:T(128)S(1)} %copy-done.1, bf16[4,256,128]{2,1,0:T(8,128)(2,1)S(1)} %get-tuple-element.55.cot_t_ref, f32[4,256,128]{2,1,0:T(8,128)S(1)} %get-tuple-element.66.own_ref, ...), custom_call_target="tpu_custom_call" | custom-call | flops 268435456 | bytes 2097152 | tf_op jit(solution)/shard_map/first_gradient/pallas_call | solution.py:399
  65.1 3.2 %collective-permute-done.7.far = bf16[4,128,256]{2,1,0:T(8,128)(2,1)S(1)} collective-permute-done((bf16[4,128,256]{2,1,0:T(8,128)(2,1)S(1)}, bf16[4,128,256]{2,1,0:T(8,128)(2,1)S(1)}, u32[]{:S(2)}, u32[]{:S(2)}) %collective-permute-start.7) | collective-permute-done | bytes 262176 | tf_op jit(solution)/shard_map/ppermute | solution.py:162
  68.3 2.5 %last.1 = (f32[2,2,128,256]{3,2,1,0:T(8,128)}, bf16[2,2,8,128,128]{4,3,2,1,0:T(8,128)(2,1)}) custom-call(s32[2]{0:T(128)S(1)} %get-tuple-element.38.rows, s32[32]{0:T(128)S(1)} %get-tuple-element.39.slots, f32[5]{0:T(128)S(1)} %copy-done.1, bf16[2,2,8,128,128]{4,3,2,1,0:T(8,128)(2,1)S(1)} %copy-done, bf16[4,128,256]{2,1,0:T(8,128)(2,1)S(1)} %collective-permute-done.7.far, ...), custom_call_target="tpu_custom_call" | custom-call | flops 536870912 | bytes 2097152 | tf_op jit(solution)/shard_map/last/pallas_call | solution.py:399
  (31 shorter events, 6.4 us)
Async XLA Ops:
  0.6 23.9 %copy-start = (bf16[2,2,8,128,128]{4,3,2,1,0:T(8,128)(2,1)S(1)}, bf16[2,2,8,128,128]{4,3,2,1,0:T(8,128)(2,1)}, u32[]{:S(2)}) copy-start(bf16[2,2,8,128,128]{4,3,2,1,0:T(8,128)(2,1)} %h_ref.9) | copy-start | bytes 3145732
  0.6 23.9 %copy-start.1 = (f32[5]{0:T(128)S(1)}, f32[5]{0:T(128)}, u32[]{:S(2)}) copy-start(f32[5]{0:T(128)} %coef.11) | copy-start | bytes 64
  6.3 4.0 %collective-permute-start.10 = (bf16[4,256,128]{2,1,0:T(8,128)(2,1)S(1)}, bf16[4,256,128]{2,1,0:T(8,128)(2,1)S(1)}, u32[]{:S(2)}, u32[]{:S(2)}) collective-permute-start(bf16[4,256,128]{2,1,0:T(8,128)(2,1)S(1)} %get-tuple-element.58), channel_id=1, source_target_pairs={{0,2},{2,0},{4,6},{6,4},{8,10},{10,8},{12,14},{14,12},{16,18},{18,... | collective-permute-start | bytes 786440 | tf_op jit(solution)/shard_map/ppermute | solution.py:156
  6.5 8.8 %collective-permute-start.9 = (bf16[4,256,128]{2,1,0:T(8,128)(2,1)S(1)}, bf16[4,256,128]{2,1,0:T(8,128)(2,1)S(1)}, u32[]{:S(2)}, u32[]{:S(2)}) collective-permute-start(bf16[4,256,128]{2,1,0:T(8,128)(2,1)S(1)} %get-tuple-element.57), channel_id=1, source_target_pairs={{0,30},{2,4},{4,2},{6,8},{8,6},{10,12},{12,10},{14,16},{16,14},{18... | collective-permute-start | bytes 786440 | tf_op jit(solution)/shard_map/ppermute | solution.py:162
  9.1 9.0 %collective-permute-start = (bf16[4,128,256]{2,1,0:T(8,128)(2,1)S(1)}, bf16[4,128,256]{2,1,0:T(8,128)(2,1)S(1)}, u32[]{:S(2)}, u32[]{:S(2)}) collective-permute-start(bf16[4,128,256]{2,1,0:T(8,128)(2,1)S(1)} %get-tuple-element.40.own_ref), channel_id=1, source_target_pairs={{0,1},{1,0},{2,3},{3,2},{4,5},{5,4},{6,7},{7,6},{8,9},{9,8},{10,11... | collective-permute-start | bytes 786440 | tf_op jit(solution)/shard_map/ppermute | solution.py:151
  15.3 9.2 %collective-permute-start.11 = (bf16[4,256,128]{2,1,0:T(8,128)(2,1)S(1)}, bf16[4,256,128]{2,1,0:T(8,128)(2,1)S(1)}, u32[]{:S(2)}, u32[]{:S(2)}) collective-permute-start(bf16[4,256,128]{2,1,0:T(8,128)(2,1)S(1)} %pack_across.3), channel_id=1, source_target_pairs={{0,1},{1,0},{2,3},{3,2},{4,5},{5,4},{6,7},{7,6},{8,9},{9,8},{10,11... | collective-permute-start | bytes 786440 | tf_op jit(solution)/shard_map/ppermute | solution.py:151
  18.2 6.3 %collective-permute-start.2 = (bf16[4,128,256]{2,1,0:T(8,128)(2,1)S(1)}, bf16[4,128,256]{2,1,0:T(8,128)(2,1)S(1)}, u32[]{:S(2)}, u32[]{:S(2)}) collective-permute-start(bf16[4,128,256]{2,1,0:T(8,128)(2,1)S(1)} %get-tuple-element.42.inner.refs_4_), channel_id=1, source_target_pairs={{0,2},{2,0},{4,6},{6,4},{8,10},{10,8},{12,14},{14,12},{16,18},{18,... | collective-permute-start | bytes 786440 | tf_op jit(solution)/shard_map/ppermute | solution.py:156
  19.0 11.2 %collective-permute-start.1 = (bf16[4,128,256]{2,1,0:T(8,128)(2,1)S(1)}, bf16[4,128,256]{2,1,0:T(8,128)(2,1)S(1)}, u32[]{:S(2)}, u32[]{:S(2)}) collective-permute-start(bf16[4,128,256]{2,1,0:T(8,128)(2,1)S(1)} %get-tuple-element.41.outer.refs_3_), channel_id=1, source_target_pairs={{0,30},{2,4},{4,2},{6,8},{8,6},{10,12},{12,10},{14,16},{16,14},{18... | collective-permute-start | bytes 786440 | tf_op jit(solution)/shard_map/ppermute | solution.py:162
  26.1 6.5 %collective-permute-start.12 = (bf16[4,256,128]{2,1,0:T(8,128)(2,1)S(1)}, bf16[4,256,128]{2,1,0:T(8,128)(2,1)S(1)}, u32[]{:S(2)}, u32[]{:S(2)}) collective-permute-start(bf16[4,256,128]{2,1,0:T(8,128)(2,1)S(1)} %get-tuple-element.62), channel_id=1, source_target_pairs={{0,30},{2,4},{4,2},{6,8},{8,6},{10,12},{12,10},{14,16},{16,14},{18... | collective-permute-start | bytes 786440 | tf_op jit(solution)/shard_map/ppermute | solution.py:162
  26.4 6.2 %collective-permute-start.13 = (bf16[4,256,128]{2,1,0:T(8,128)(2,1)S(1)}, bf16[4,256,128]{2,1,0:T(8,128)(2,1)S(1)}, u32[]{:S(2)}, u32[]{:S(2)}) collective-permute-start(bf16[4,256,128]{2,1,0:T(8,128)(2,1)S(1)} %get-tuple-element.63), channel_id=1, source_target_pairs={{0,2},{2,0},{4,6},{6,4},{8,10},{10,8},{12,14},{14,12},{16,18},{18,... | collective-permute-start | bytes 786440 | tf_op jit(solution)/shard_map/ppermute | solution.py:156
  31.3 8.0 %collective-permute-start.3 = (bf16[4,128,256]{2,1,0:T(8,128)(2,1)S(1)}, bf16[4,128,256]{2,1,0:T(8,128)(2,1)S(1)}, u32[]{:S(2)}, u32[]{:S(2)}) collective-permute-start(bf16[4,128,256]{2,1,0:T(8,128)(2,1)S(1)} %get-tuple-element.45.own_ref), channel_id=1, source_target_pairs={{0,1},{1,0},{2,3},{3,2},{4,5},{5,4},{6,7},{7,6},{8,9},{9,8},{10,11... | collective-permute-start | bytes 786440 | tf_op jit(solution)/shard_map/ppermute | solution.py:151
  32.7 12.3 %collective-permute-start.14 = (bf16[4,256,128]{2,1,0:T(8,128)(2,1)S(1)}, bf16[4,256,128]{2,1,0:T(8,128)(2,1)S(1)}, u32[]{:S(2)}, u32[]{:S(2)}) collective-permute-start(bf16[4,256,128]{2,1,0:T(8,128)(2,1)S(1)} %pack_across.4), channel_id=1, source_target_pairs={{0,1},{1,0},{2,3},{3,2},{4,5},{5,4},{6,7},{7,6},{8,9},{9,8},{10,11... | collective-permute-start | bytes 786440 | tf_op jit(solution)/shard_map/ppermute | solution.py:151
  39.4 5.6 %collective-permute-start.5 = (bf16[4,128,256]{2,1,0:T(8,128)(2,1)S(1)}, bf16[4,128,256]{2,1,0:T(8,128)(2,1)S(1)}, u32[]{:S(2)}, u32[]{:S(2)}) collective-permute-start(bf16[4,128,256]{2,1,0:T(8,128)(2,1)S(1)} %get-tuple-element.47.inner.refs_8_), channel_id=1, source_target_pairs={{0,2},{2,0},{4,6},{6,4},{8,10},{10,8},{12,14},{14,12},{16,18},{18,... | collective-permute-start | bytes 786440 | tf_op jit(solution)/shard_map/ppermute | solution.py:156
  40.6 8.6 %collective-permute-start.4 = (bf16[4,128,256]{2,1,0:T(8,128)(2,1)S(1)}, bf16[4,128,256]{2,1,0:T(8,128)(2,1)S(1)}, u32[]{:S(2)}, u32[]{:S(2)}) collective-permute-start(bf16[4,128,256]{2,1,0:T(8,128)(2,1)S(1)} %get-tuple-element.46.outer.refs_7_), channel_id=1, source_target_pairs={{0,30},{2,4},{4,2},{6,8},{8,6},{10,12},{12,10},{14,16},{16,14},{18... | collective-permute-start | bytes 786440 | tf_op jit(solution)/shard_map/ppermute | solution.py:162
  46.6 6.2 %collective-permute-start.15 = (bf16[4,256,128]{2,1,0:T(8,128)(2,1)S(1)}, bf16[4,256,128]{2,1,0:T(8,128)(2,1)S(1)}, u32[]{:S(2)}, u32[]{:S(2)}) collective-permute-start(bf16[4,256,128]{2,1,0:T(8,128)(2,1)S(1)} %get-tuple-element.67), channel_id=1, source_target_pairs={{0,30},{2,4},{4,2},{6,8},{8,6},{10,12},{12,10},{14,16},{16,14},{18... | collective-permute-start | bytes 786440 | tf_op jit(solution)/shard_map/ppermute | solution.py:162
  46.7 6.1 %collective-permute-start.16 = (bf16[4,256,128]{2,1,0:T(8,128)(2,1)S(1)}, bf16[4,256,128]{2,1,0:T(8,128)(2,1)S(1)}, u32[]{:S(2)}, u32[]{:S(2)}) collective-permute-start(bf16[4,256,128]{2,1,0:T(8,128)(2,1)S(1)} %get-tuple-element.68), channel_id=1, source_target_pairs={{0,2},{2,0},{4,6},{6,4},{8,10},{10,8},{12,14},{14,12},{16,18},{18,... | collective-permute-start | bytes 786440 | tf_op jit(solution)/shard_map/ppermute | solution.py:156
  50.3 7.9 %collective-permute-start.6 = (bf16[4,128,256]{2,1,0:T(8,128)(2,1)S(1)}, bf16[4,128,256]{2,1,0:T(8,128)(2,1)S(1)}, u32[]{:S(2)}, u32[]{:S(2)}) collective-permute-start(bf16[4,128,256]{2,1,0:T(8,128)(2,1)S(1)} %get-tuple-element.49.own_ref), channel_id=1, source_target_pairs={{0,1},{1,0},{2,3},{3,2},{4,5},{5,4},{6,7},{7,6},{8,9},{9,8},{10,11... | collective-permute-start | bytes 786440 | tf_op jit(solution)/shard_map/ppermute | solution.py:151
  52.8 10.9 %collective-permute-start.17 = (bf16[4,256,128]{2,1,0:T(8,128)(2,1)S(1)}, bf16[4,256,128]{2,1,0:T(8,128)(2,1)S(1)}, u32[]{:S(2)}, u32[]{:S(2)}) collective-permute-start(bf16[4,256,128]{2,1,0:T(8,128)(2,1)S(1)} %pack_across.5), channel_id=1, source_target_pairs={{0,1},{1,0},{2,3},{3,2},{4,5},{5,4},{6,7},{7,6},{8,9},{9,8},{10,11... | collective-permute-start | bytes 786440 | tf_op jit(solution)/shard_map/ppermute | solution.py:151
  58.3 5.4 %collective-permute-start.8 = (bf16[4,128,256]{2,1,0:T(8,128)(2,1)S(1)}, bf16[4,128,256]{2,1,0:T(8,128)(2,1)S(1)}, u32[]{:S(2)}, u32[]{:S(2)}) collective-permute-start(bf16[4,128,256]{2,1,0:T(8,128)(2,1)S(1)} %get-tuple-element.51.inner), channel_id=1, source_target_pairs={{0,2},{2,0},{4,6},{6,4},{8,10},{10,8},{12,14},{14,12},{16,18},{18,... | collective-permute-start | bytes 786440 | tf_op jit(solution)/shard_map/ppermute | solution.py:156
  59.7 8.6 %collective-permute-start.7 = (bf16[4,128,256]{2,1,0:T(8,128)(2,1)S(1)}, bf16[4,128,256]{2,1,0:T(8,128)(2,1)S(1)}, u32[]{:S(2)}, u32[]{:S(2)}) collective-permute-start(bf16[4,128,256]{2,1,0:T(8,128)(2,1)S(1)} %get-tuple-element.50.outer), channel_id=1, source_target_pairs={{0,30},{2,4},{4,2},{6,8},{8,6},{10,12},{12,10},{14,16},{16,14},{18... | collective-permute-start | bytes 786440 | tf_op jit(solution)/shard_map/ppermute | solution.py:162

commit v4 on v3

--- a/solution.py
+++ b/solution.py
@@ -144,7 +144,6 @@
 f32 = jnp.float32
 VMEM_BYTES = 16 * 1024 * 1024
 OWN = (4, 5, 8, 9)
-ACROSS = (6, 7, 10, 11)
 
 
 def swap_y(value):
@@ -169,39 +168,50 @@
     hashed = hashed ^ hashed >> 15
     hashed = hashed * jnp.int32(739982445)
     hashed = hashed ^ hashed >> 12
-    return (1 - 2 * (hashed >> 7 & 1)).astype(f32).astype(bf16)
-
-
-def listed_blocks(h_ref, rows, at):
-    return [h_ref[rows[at // 2], at % 2, k] for k in range(h_ref.shape[2])]
-
-
-def window_product(slots, rows, at, h_ref, window):
-    listed = h_ref.shape[2]
-    left = jnp.concatenate(listed_blocks(h_ref, rows, at), axis=1)
-    right = jnp.concatenate([window[slots[at * listed + k]] for k in range(listed)], axis=0)
-    return jnp.dot(left, right, preferred_element_type=f32)
-
-
-def push(slots, rows, at, h_ref, adjoint_t, sums):
-    listed, width = h_ref.shape[2:4]
-    wide = jnp.concatenate(listed_blocks(h_ref, rows, at), axis=1)
-    product = jnp.dot(adjoint_t, wide, preferred_element_type=f32)
-    for k in range(listed):
-        sums[slots[at * listed + k]] += product[:, k * width : (k + 1) * width]
-
-
-def finish_push(sums, far_ref, near_ref, own_ref, across_ref):
-    far_ref[...] = sums[0:4].astype(bf16)
-    near_ref[...] = sums[12:16].astype(bf16)
-    for at in range(4):
-        own_ref[at] = sums[OWN[at]]
-        across_ref[at] = sums[ACROSS[at]]
+    return jnp.where((hashed & 128) == 0, f32(1.0), f32(-1.0)).astype(bf16)
+
+
+def step_of(code):
+    return code // 3 - 1, code % 3 - 1
+
+
+def window_product(at, coded, rows_of_blocks):
+    right = []
+    for code in range(9):
+        step_x, step_y = step_of(code)
+        right.append(rows_of_blocks[1 + at // 2 + step_x][(at % 2 + step_y) % 4])
+    left = jnp.concatenate([coded[at, code] for code in range(9)], axis=1)
+    return jnp.dot(left, jnp.concatenate(right, axis=0), preferred_element_type=f32)
+
+
+def push(coded, fields, near_ref, own_ref, across_ref, far_ref):
+    for col in range(4):
+        sources = [(b, (col - b + 1) % 4 - 1) for b in range(2) if (col - b + 1) % 4 < 3]
+
+        def blocks(row, *steps):
+            return [
+                jnp.concatenate([coded[2 * row + b, 3 * (step_x + 1) + step_y + 1] for step_x in steps], axis=1)
+                for b, step_y in sources
+            ]
+
+        def total(rows, right):
+            left = jnp.concatenate([fields[2 * row + b] for row in rows for b, _ in sources], axis=1)
+            return jnp.dot(left, jnp.concatenate(right, axis=0), preferred_element_type=f32)
+
+        far_ref[col] = total((0,), blocks(0, -1)).astype(bf16)
+        near_ref[col] = total((1,), blocks(1, 1)).astype(bf16)
+        middle = total((0, 1), blocks(0, 0, 1) + blocks(1, -1, 0))
+        width = middle.shape[1] // 2
+        ref = own_ref if col < 2 else across_ref
+        ref[col % 2] = middle[:, :width]
+        ref[2 + col % 2] = middle[:, width:]
 
 
 def fill_window(parts, window):
-    for at, part in enumerate(parts):
-        window[4 * at : 4 * at + 4] = part[...]
+    first = 0
+    for part in parts:
+        window[first : first + part.shape[0]] = part[...]
+        first += part.shape[0]
 
 
 def pack_rows_kernel(own_ref, across_ref, outer_ref, inner_ref):
@@ -211,103 +221,97 @@
     inner_ref[2:4] = across_ref[2:4]
 
 
-def pack_across_kernel(across_ref, far_ref, near_ref, packed_ref):
+def pack_across_kernel(across_ref, near_ref, far_ref, packed_ref):
     packed_ref[0:2] = (across_ref[0:2] + far_ref[2:4].astype(f32)).astype(bf16)
     packed_ref[2:4] = (across_ref[2:4] + near_ref[2:4].astype(f32)).astype(bf16)
 
 
 def first_kernel(
     top, span_x, span_y, position, seeds_hbm, coef_hbm, codes_hbm, h_hbm, cot_hbm,
-    start_ref, term_ref, rounded_ref, cot_t_ref, adjoint_ref, far_ref, near_ref, own_ref, across_ref,
-    rows_out, slots_out, seeds_ref, coef, codes, h_ref, cot_ref, sums, small_sem, h_sem, cot_sem,
+    rows_out, slots_out, coded, start_ref, term_ref, cot_t_ref, adjoint_ref, rounded_ref, *rest,
 ):
+    sent_refs, (seeds_ref, coef, codes, h_ref, cot_ref, small_sem, h_sem, cot_sem) = rest[:-8], rest[-8:]
     gx, gy = position[0], position[1]
     odd = lax.rem(gx, 2)
     rows = (odd, 1 - odd)
-    small = [
+    copies = [
         pltpu.make_async_copy(source, target, small_sem.at[at])
         for at, (source, target) in enumerate(((seeds_hbm, seeds_ref), (codes_hbm, codes), (coef_hbm, coef)))
     ]
-    for copy in small:
+    for at in range(4):
+        source = (rows[at // 2], at % 2)
+        copies.append(pltpu.make_async_copy(h_hbm.at[source], h_ref.at[at], h_sem.at[at]))
+        copies.append(pltpu.make_async_copy(cot_hbm.at[source], cot_ref.at[at], cot_sem.at[at]))
+    for copy in copies:
         copy.start()
-    h_copies, cot_copies = [], []
-    for at in range(4):
-        source = (rows[at // 2], at % 2)
-        h_copies.append(pltpu.make_async_copy(h_hbm.at[source], h_ref.at[source], h_sem.at[at]))
-        cot_copies.append(pltpu.make_async_copy(cot_hbm.at[source], cot_ref.at[at], cot_sem.at[at]))
-    for copy in h_copies + cot_copies:
-        copy.start()
-    sums[...] = jnp.zeros_like(sums)
-    for copy in small:
+    coded[...] = jnp.zeros_like(coded)
+    for copy in copies[:3]:
         copy.wait()
-    listed, width = h_ref.shape[2:4]
+    listed, width = h_ref.shape[1:3]
+    places = []
+    for at in range(4):
+        for k in range(listed):
+            code = codes[rows[at // 2], at % 2, k]
+            step_x = jnp.where(code >= 6, 1, jnp.where(code >= 3, 0, -1))
+            step_y = code - 3 * step_x - 4
+            step_x = (1 - 2 * odd) * step_x
+            places.append(3 * step_x + step_y + 4)
+            slots_out[at * listed + k] = (1 + at // 2 + step_x) * 4 + lax.rem(at % 2 + step_y + 4, 4)
+    for at in range(2):
+        rows_out[at] = rows[at]
+    for copy in copies[3:]:
+        copy.wait()
+    for at in range(4):
+        for k in range(listed):
+            coded[at, places[at * listed + k]] = h_ref[at, k]
+    fields = []
+    for at in range(4):
+        cot = cot_ref[at].astype(f32)
+        cot_t = jnp.transpose(cot)
+        cot_t_ref[at] = cot_t.astype(bf16)
+        adjoint_ref[at] = (coef[top] * cot).astype(bf16)
+        fields.append((coef[top] * cot_t).astype(bf16))
     for slot in range(16):
         local = jnp.where(odd == 0, slot // 4 - 1, 2 - slot // 4)
         place_x = lax.rem(gx * 2 + local + span_x, span_x)
         place_y = lax.rem(gy * 2 + slot % 4, span_y)
         start_ref[slot] = start_signs((place_x * span_y + place_y) * width, seeds_ref[...], width)
-    slots = []
-    for at in range(4):
-        for k in range(listed):
-            code = codes[rows[at // 2], at % 2, k]
-            step_x = jnp.where(code >= 6, 1, jnp.where(code >= 3, 0, -1))
-            step_y = code - 3 * step_x - 4
-            slots.append((1 + at // 2 + (1 - 2 * odd) * step_x) * 4 + lax.rem(at % 2 + step_y + 4, 4))
-    for at in range(2):
-        rows_out[at] = rows[at]
-    for at in range(4 * listed):
-        slots_out[at] = slots[at]
-    for at in range(4):
-        h_copies[at].wait()
-        value = window_product(slots, rows, at, h_ref, start_ref)
+    push(coded, fields, *sent_refs)
+    for at in range(4):
+        value = window_product(at, coded, [start_ref.at[pl.ds(4 * row, 4)] for row in range(4)])
         term_ref[at] = value
         rounded_ref[at] = value.astype(bf16)
-    for at in range(4):
-        cot_copies[at].wait()
-        cot = cot_ref[at].astype(f32)
-        cot_t = jnp.transpose(cot)
-        cot_t_ref[at] = cot_t.astype(bf16)
-        adjoint_ref[at] = (coef[top] * cot).astype(bf16)
-        push(slots, rows, at, h_ref, (coef[top] * cot_t).astype(bf16), sums)
-    finish_push(sums, far_ref, near_ref, own_ref, across_ref)
-
-
-def forward_kernel(
-    index, rows, slots, coef, h_ref, far, outer, inner, near, before_ref, sums_ref, rounded_ref, density_ref, *rest
-):
-    term_ref, window = rest[:-1], rest[-1]
-    fill_window((far, outer, inner, near), window)
+
+
+def forward_kernel(index, has_term, coef, coded, far, outer, inner, near, before_ref, sums_ref, density_ref, rounded_ref, *term_ref):
     for at in range(4):
         before = (before_ref[OWN[at]] if index == 2 else before_ref[at]).astype(f32)
-        value = 2.0 * window_product(slots, rows, at, h_ref, window) - before
+        value = 2.0 * window_product(at, coded, (far, outer, inner, near)) - before
         sums = coef[0] * before + coef[1] * sums_ref[at] if index == 2 else sums_ref[at]
         rounded_ref[at] = value.astype(bf16)
         density_ref[at] = sums + coef[index] * value
-        for ref in term_ref:
-            ref[at] = value
-
-
-def adjoint_value(at, index, coef, cot_t_ref, own_ref, far_ref, near_ref, across_ref):
-    came = far_ref[at] if at < 2 else near_ref[at - 2]
-    carried = own_ref[at] + came.astype(f32) + across_ref[at].astype(f32)
+        if has_term:
+            term_ref[0][at] = value
+
+
+def adjoint_value(at, index, coef, cot_t_ref, own_ref, across_ref, near_ref, far_ref):
+    came = (far_ref if at < 2 else near_ref)[at % 2]
+    carried = own_ref[at] + across_ref[at].astype(f32) + came.astype(f32)
     return coef[index] * cot_t_ref[at].astype(f32) + 2.0 * carried
 
 
-def adjoint_kernel(
-    index, top, rows, slots, coef, h_ref, cot_t_ref, own_in, far_in, near_in, across_in,
-    rounded_ref, far_ref, near_ref, own_ref, across_ref, *rest,
-):
-    value_refs, sums = rest[:-1], rest[-1]
-    sums[...] = jnp.zeros_like(sums)
-    for at in range(4):
-        value = adjoint_value(at, index, coef, cot_t_ref, own_in, far_in, near_in, across_in)
+def adjoint_kernel(index, top, coef, coded, *refs):
+    arrived, rounded_ref, sent_refs, value_refs = refs[:5], refs[5], refs[6:10], refs[10:]
+    fields = []
+    for at in range(4):
+        value = adjoint_value(at, index, coef, *arrived)
         if index + 2 == top:
-            value = value - coef[top] * cot_t_ref[at].astype(f32)
+            value = value - coef[top] * arrived[0][at].astype(f32)
         for ref in value_refs:
             ref[at] = value
-        push(slots, rows, at, h_ref, value.astype(bf16), sums)
-        rounded_ref[at] = jnp.transpose(value).astype(bf16)
-    finish_push(sums, far_ref, near_ref, own_ref, across_ref)
+        fields.append(value.astype(bf16))
+        rounded_ref[at] = fields[-1]
+    push(coded, fields, *sent_refs)
 
 
 def block_gradients(slots, at, left, windows, listed, store):
@@ -317,26 +321,28 @@
         store(k, lax.dot_general(left, right, (((1,), (1,)), ((), ())), preferred_element_type=f32))
 
 
-def middle_gradient_kernel(count, slots, *refs):
-    adjoints, parts, (sums_ref, windows) = refs[:count], refs[count : 5 * count], refs[5 * count :]
+def middle_gradient_kernel(parts, slots, *refs):
+    count = len(parts)
+    adjoints, (sums_ref, windows) = refs[:count], refs[-2:]
     listed = sums_ref.shape[1]
+    first = count
     for t in range(count):
-        fill_window(parts[4 * t : 4 * t + 4], windows.at[t])
-    for at in range(4):
-        left = jnp.concatenate([a[at] * bf16(2.0) for a in adjoints], axis=1)
+        fill_window(refs[first : first + parts[t]], windows.at[t])
+        first += parts[t]
+    for at in range(4):
+        left = [jnp.transpose(2.0 * a[at].astype(f32)).astype(bf16) for a in adjoints]
 
         def store(k, total, at=at):
             sums_ref[at, k] = total
 
-        block_gradients(slots, at, left, [windows.at[t] for t in range(count)], listed, store)
-
-
-def first_gradient_kernel(
-    slots, coef, cot_t_ref, own_ref, far_ref, near_ref, across_ref, older_ref, start_ref, before_ref, sums_ref
-):
+        block_gradients(slots, at, jnp.concatenate(left, axis=1), [windows.at[t] for t in range(count)], listed, store)
+
+
+def first_gradient_kernel(slots, coef, older_ref, start_ref, before_ref, *refs):
+    arrived, sums_ref = refs[:-1], refs[-1]
     listed = sums_ref.shape[1]
     for at in range(4):
-        value = adjoint_value(at, 1, coef, cot_t_ref, own_ref, far_ref, near_ref, across_ref) - older_ref[at]
+        value = adjoint_value(at, 1, coef, *arrived) - older_ref[at]
 
         def store(k, total, at=at):
             sums_ref[at, k] = before_ref[at, k] + total
@@ -344,16 +350,14 @@
         block_gradients(slots, at, jnp.transpose(value).astype(bf16), (start_ref,), listed, store)
 
 
-def last_kernel(
-    index, scale, rows, slots, coef, h_ref, far, outer, inner, near, before_ref, sums_ref, adjoint_ref, early_ref,
-    density_hbm, grad_hbm, density, grad, window, density_sem, grad_sem,
-):
-    fill_window((far, outer, inner, near), window)
-    listed = h_ref.shape[2]
+def last_kernel(index, scale, rows, slots, coef, coded, *refs):
+    before_ref, sums_ref, adjoint_ref, early_ref, density_hbm, grad_hbm, density, grad, window, density_sem, grad_sem = refs[4:]
+    fill_window(refs[:4], window)
+    listed = early_ref.shape[1]
     copies = []
     for at in range(4):
         place = (rows[at // 2], at % 2)
-        value = 2.0 * window_product(slots, rows, at, h_ref, window) - before_ref[at]
+        value = 2.0 * window_product(at, coded, refs[:4]) - before_ref[at]
         density[at] = sums_ref[at] + coef[index] * value
         copies.append(pltpu.make_async_copy(density.at[at], density_hbm.at[place], density_sem.at[at]))
         copies[-1].start()
@@ -387,9 +391,7 @@
         return jax.ShapeDtypeStruct((count, probes, width), dtype)
 
     apply_flops = 2 * blocks * listed * width * width * probes
-    pushed = [turned(4, bf16), turned(4, bf16), turned(4, f32), turned(4, f32)]
-    sums_scratch = pltpu.VMEM((16, probes, width), f32)
-
+    sent_shapes = [turned(4, bf16), turned(4, f32), turned(4, f32), turned(4, bf16)]
     window_scratch = pltpu.VMEM((16, width, probes), bf16)
 
     def kept(values):
@@ -403,11 +405,15 @@
             out_shape=out_shape,
             scratch_shapes=list(scratch),
             compiler_params=pltpu.CompilerParams(vmem_limit_bytes=VMEM_BYTES),
-            cost_estimate=pl.CostEstimate(flops=flops, bytes_accessed=2 * 1024 * 1024, transcendentals=0),
+            cost_estimate=pl.CostEstimate(flops=flops, bytes_accessed=1024 * 1024, transcendentals=0),
             name=name,
         )(*scalars, *operands)
 
-    start, term, rounded, cot_t, adjoint, *sent, rows, slots = call(
+    gradient_sums = jax.ShapeDtypeStruct((blocks, listed, width, width), f32)
+    shapes = [jax.ShapeDtypeStruct((2,), jnp.int32), jax.ShapeDtypeStruct((blocks * listed,), jnp.int32)]
+    shapes += [jax.ShapeDtypeStruct((blocks, 9, width, width), bf16), field(16, bf16), field(4, f32)]
+    shapes += [turned(4, bf16), field(4, bf16), field(4, bf16)] + sent_shapes
+    rows, slots, coded, start, term, cot_t, adjoint, rounded, to_near, own, to_across, to_far = call(
         "first",
         functools.partial(first_kernel, top, span_x, span_y),
         (jnp.stack([lax.axis_index("gx"), lax.axis_index("gy")]).astype(jnp.int32),),
@@ -415,17 +421,14 @@
             pltpu.with_memory_space_constraint(value, pltpu.HBM)
             for value in (probe_seeds.reshape(1, probes), coefficients, neighbours, hamiltonian, cotangent)
         ),
-        [field(16, bf16), field(4, f32), field(4, bf16), turned(4, bf16), field(4, bf16)]
-        + pushed
-        + [jax.ShapeDtypeStruct((2,), jnp.int32), jax.ShapeDtypeStruct((blocks * listed,), jnp.int32)],
-        out_specs=[vmem] * 9 + [smem] * 2,
+        shapes,
+        out_specs=[smem] * 2 + [vmem] * (len(shapes) - 2),
         scratch=(
             pltpu.VMEM((1, probes), jnp.int32),
             pltpu.SMEM(coefficients.shape, f32),
             pltpu.SMEM(neighbours.shape, jnp.int32),
-            pltpu.VMEM(hamiltonian.shape, bf16),
-            pltpu.VMEM((4, width, probes), bf16),
-            sums_scratch,
+            pltpu.VMEM((blocks, listed, width, width), bf16),
+            pltpu.VMEM((blocks, width, probes), bf16),
             pltpu.SemaphoreType.DMA((3,)),
             pltpu.SemaphoreType.DMA((4,)),
             pltpu.SemaphoreType.DMA((4,)),
@@ -433,65 +436,64 @@
         flops=2 * apply_flops,
         in_specs=[hbm] * 5,
     )
-    scalars = (rows, slots, coefficients)
+    (coded,) = kept((coded,))
     adjoints = {top: adjoint}
-    windows = [(start,)]
+    windows = []
     before, sums = start, term
     for index in range(2, terms):
         at = terms - index
         outer, inner = call(
             "pack_rows", pack_rows_kernel, (), kept((rounded, swap_y(rounded))), [field(4, bf16)] * 2, flops=0
         )
-        far, near = swap_far(outer), swap_near(inner)
-        to_far, to_near, own, to_across = sent
-        from_far, from_near = swap_far(to_far), swap_near(to_near)
+        near = swap_near(inner)
+        window = kept((swap_far(outer), outer, inner, near))
+        from_near, from_far = swap_near(to_near), swap_far(to_far)
+        if index == top:
+            middle = call(
+                "middle_gradient",
+                functools.partial(middle_gradient_kernel, (4,) * len(windows)),
+                (slots,),
+                kept(tuple(adjoints[t] for t in range(2, top)) + tuple(part for shown in windows for part in shown)),
+                [gradient_sums],
+                scratch=(pltpu.VMEM((terms - 3, 16, width, probes), bf16),),
+                flops=(terms - 3) * apply_flops,
+            )[0]
+            from_near, middle = lax.optimization_barrier((from_near, middle))
         (to_across,) = call(
-            "pack_across", pack_across_kernel, (), kept((to_across, from_far, from_near)), [turned(4, bf16)], flops=0
-        )
-        from_across, _ = lax.optimization_barrier((swap_y(to_across), near))
-        arrived = kept((cot_t, own, from_far, from_near, from_across))
-        window = kept((far, outer, inner, near))
-        windows.append(window)
+            "pack_across", pack_across_kernel, (), kept((to_across, from_near, from_far)), [turned(4, bf16)], flops=0
+        )
+        arrived = kept((cot_t, own, swap_y(to_across), from_near, from_far))
         if index == top:
             break
-        rounded, density, *following = call(
+        windows.append(window)
+        has_term = index + 2 <= top
+        density, rounded, *following = call(
             "forward",
-            functools.partial(forward_kernel, index),
-            scalars, (hamiltonian,) + window + kept((before, sums)),
-            [field(4, bf16), field(4, f32)] + [field(4, f32)] * (index + 2 <= top),
-            scratch=(window_scratch,),
+            functools.partial(forward_kernel, index, has_term),
+            (coefficients,), (coded,) + window + kept((before, sums)),
+            [field(4, f32), field(4, bf16)] + [field(4, f32)] * has_term,
         )
         before, sums = term, density
-        if following:
-            term = following[0]
-        adjoints[at], *sent = call(
+        term = following[0] if has_term else None
+        has_value = at == 3
+        adjoints[at], to_near, own, to_across, to_far, *rest = call(
             "adjoint",
             functools.partial(adjoint_kernel, at, top),
-            scalars, (hamiltonian,) + arrived,
-            [field(4, bf16)] + pushed + [turned(4, f32)] * (at == 3),
-            scratch=(sums_scratch,),
-        )
-        if at == 3:
-            older = sent.pop()
-    gradient_sums = jax.ShapeDtypeStruct((blocks, listed, width, width), f32)
-    middle = call(
-        "middle_gradient",
-        functools.partial(middle_gradient_kernel, terms - 3),
-        (slots,), tuple(adjoints[t] for t in range(2, top)) + windows[1] + windows[2],
-        [gradient_sums],
-        scratch=(pltpu.VMEM((terms - 3, 16, width, probes), bf16),),
-        flops=(terms - 3) * apply_flops,
-    )[0]
+            (coefficients,), (coded,) + arrived,
+            [turned(4, bf16)] + sent_shapes + [turned(4, f32)] * has_value,
+        )
+        if has_value:
+            older = rest[0]
     early = call(
         "first_gradient",
         first_gradient_kernel,
-        (slots, coefficients), arrived + (older, start, middle),
+        (slots, coefficients), kept((older, start, middle)) + arrived,
         [gradient_sums],
     )[0]
     density, gradient = call(
         "last",
         functools.partial(last_kernel, top, 1.0 / probes),
-        scalars, (hamiltonian,) + windows[top - 1] + kept((before, sums, adjoints[top], early)),
+        (rows, slots, coefficients), (coded,) + window + kept((before, sums, adjoints[top], early)),
         [
             jax.ShapeDtypeStruct(cotangent.shape, f32),
             jax.ShapeDtypeStruct(hamiltonian.shape, bf16),

time: 70.9 us -> 65.8 us (0.928)
  Pallas kernels: 17.1 us -> 14.4 us
  waiting for transfers between devices: 28.1 us -> 26.4 us
  starting transfers between devices: 24.7 us -> 23.9 us
    ppermute x6, waiting for transfers between devices: 18 us -> 10.1 us  [swap_y(): return lax.ppermute(value, 'gy', [(0, 1), (1, 0)])]
    ppermute x6, waiting for transfers between devices: 10.1 us -> 16.3 us  [swap_far(): return lax.ppermute(value, 'gx', pairs)]
    ppermute x6, starting transfers between devices: 3.46 us -> 6.63 us  [swap_far(): return lax.ppermute(value, 'gx', pairs)]
    pallas_call x14, Pallas kernels: 17.1 us -> 14.4 us  [call(): pl.pallas_call(kernel, in_specs=[smem] * len(scalars) + (in_specs or [vme...]
    ppermute x6, starting transfers between devices: 12.1 us -> 10.1 us  [swap_y(): return lax.ppermute(value, 'gy', [(0, 1), (1, 0)])]
    ppermute x6, starting transfers between devices: 9.14 us -> 7.21 us  [swap_near(): return lax.ppermute(value, 'gx', [(i, i ^ 1) for i in range(count)])]
  transfers between devices with their start and end apart: 18 -> 18, of which waited for: 9 -> 8; matrix products, arithmetic and copies ran while one was open for 0% -> 0% of each run, Pallas kernels for 13% -> 12%
where the time goes in v4:
time: 65.8 us; the launch traced here: 65.6 us
  waiting for transfers between devices  26.4 us (40%)
  starting transfers between devices  23.9 us (36%)
  Pallas kernels  14.4 us (22%)
  between operations  0.74 us (1%)
    ppermute x6, waiting for transfers between devices, swap_far(): return lax.ppermute(value, 'gx', pairs)  16.3 us
    pallas_call x14, Pallas kernels, call(): pl.pallas_call(kernel, in_specs=[smem] * len(scalars) + (in_specs or [vme...  14.4 us
    ppermute x6, waiting for transfers between devices, swap_y(): return lax.ppermute(value, 'gy', [(0, 1), (1, 0)])  10.1 us
    ppermute x6, starting transfers between devices, swap_y(): return lax.ppermute(value, 'gy', [(0, 1), (1, 0)])  10.1 us
    ppermute x6, starting transfers between devices, swap_near(): return lax.ppermute(value, 'gx', [(i, i ^ 1) for i in range(count)])  7.21 us
    ppermute x6, starting transfers between devices, swap_far(): return lax.ppermute(value, 'gx', pairs)  6.63 us
  transfers between devices with their start and end apart: 18, of which 8 were waited for; matrix products, arithmetic and copies ran while one was open for 0% of the time, Pallas kernels for 12%

profile of v4, /device:TPU:1, one launch (start us, length us, event | category | flops | bytes accessed | tf_op | source)
XLA Modules:
  0.0 65.6 jit_solution(14737356718013436009)
XLA Ops:
  0.7 3.8 %first.1 = (s32[2]{0:T(128)S(1)}, s32[32]{0:T(128)S(1)}, bf16[4,9,128,128]{3,2,1,0:T(8,128)(2,1)S(1)}, bf16[16,128,256]{2,1,0:T(8,128)(2,1)S(1)}, f32[4,128,256]...) custom-call(s32[2]{0:T(128)S(1)} %pad_add_fusion.position, ...), custom_call_target="tpu_custom_call" | custom-call | flops 536870912 | bytes 1048576 | tf_op jit(solution)/shard_map/first/pallas_call | solution.py:401
  4.7 2.7 %collective-permute-start.10 = (bf16[4,256,128]{2,1,0:T(8,128)(2,1)S(1)}, bf16[4,256,128]{2,1,0:T(8,128)(2,1)S(1)}, u32[]{:S(2)}, u32[]{:S(2)}) collective-permute-start(bf16[4,256,128]{2,1,0:T(8,128)(2,1)S(1)} %get-tuple-element.60), channel_id=1, source_target_pairs={{0,30},{2,4},{4,2},{6,8},{8,6},{10,12},{12,10},{14,16},{16,14},{18... | collective-permute-start | bytes 786440 | tf_op jit(solution)/shard_map/ppermute | solution.py:161
  7.3 1.2 %collective-permute-start = (bf16[4,128,256]{2,1,0:T(8,128)(2,1)S(1)}, bf16[4,128,256]{2,1,0:T(8,128)(2,1)S(1)}, u32[]{:S(2)}, u32[]{:S(2)}) collective-permute-start(bf16[4,128,256]{2,1,0:T(8,128)(2,1)S(1)} %get-tuple-element.41.own_ref), channel_id=1, source_target_pairs={{0,1},{1,0},{2,3},{3,2},{4,5},{5,4},{6,7},{7,6},{8,9},{9,8},{10,11... | collective-permute-start | bytes 786440 | tf_op jit(solution)/shard_map/ppermute | solution.py:150
  8.6 4.9 %collective-permute-done.10.far_ref.refs_4_ = bf16[4,256,128]{2,1,0:T(8,128)(2,1)S(1)} collective-permute-done((bf16[4,256,128]{2,1,0:T(8,128)(2,1)S(1)}, bf16[4,256,128]{2,1,0:T(8,128)(2,1)S(1)}, u32[]{:S(2)}, u32[]{:S(2)}) %collective-permute-start.10) | collective-permute-done | bytes 262176 | tf_op jit(solution)/shard_map/ppermute | solution.py:161
  13.5 2.8 %collective-permute-start.11 = (bf16[4,256,128]{2,1,0:T(8,128)(2,1)S(1)}, bf16[4,256,128]{2,1,0:T(8,128)(2,1)S(1)}, u32[]{:S(2)}, u32[]{:S(2)}) collective-permute-start(bf16[4,256,128]{2,1,0:T(8,128)(2,1)S(1)} %pack_across.3), channel_id=1, source_target_pairs={{0,1},{1,0},{2,3},{3,2},{4,5},{5,4},{6,7},{7,6},{8,9},{9,8},{10,11... | collective-permute-start | bytes 786440 | tf_op jit(solution)/shard_map/ppermute | solution.py:150
  16.4 1.3 %collective-permute-start.1 = (bf16[4,128,256]{2,1,0:T(8,128)(2,1)S(1)}, bf16[4,128,256]{2,1,0:T(8,128)(2,1)S(1)}, u32[]{:S(2)}, u32[]{:S(2)}) collective-permute-start(bf16[4,128,256]{2,1,0:T(8,128)(2,1)S(1)} %get-tuple-element.42.outer.refs_3_), channel_id=1, source_target_pairs={{0,30},{2,4},{4,2},{6,8},{8,6},{10,12},{12,10},{14,16},{16,14},{18... | collective-permute-start | bytes 786440 | tf_op jit(solution)/shard_map/ppermute | solution.py:161
  17.7 3.1 %collective-permute-start.2 = (bf16[4,128,256]{2,1,0:T(8,128)(2,1)S(1)}, bf16[4,128,256]{2,1,0:T(8,128)(2,1)S(1)}, u32[]{:S(2)}, u32[]{:S(2)}) collective-permute-start(bf16[4,128,256]{2,1,0:T(8,128)(2,1)S(1)} %get-tuple-element.43.inner.refs_4_), channel_id=1, source_target_pairs={{0,2},{2,0},{4,6},{6,4},{8,10},{10,8},{12,14},{14,12},{16,18},{18,... | collective-permute-start | bytes 786440 | tf_op jit(solution)/shard_map/ppermute | solution.py:155
  20.8 2.0 %collective-permute-done.11.refs_2_ = bf16[4,256,128]{2,1,0:T(8,128)(2,1)S(1)} collective-permute-done((bf16[4,256,128]{2,1,0:T(8,128)(2,1)S(1)}, bf16[4,256,128]{2,1,0:T(8,128)(2,1)S(1)}, u32[]{:S(2)}, u32[]{:S(2)}) %collective-permute-start.11) | collective-permute-done | bytes 262176 | tf_op jit(solution)/shard_map/ppermute | solution.py:150
  22.7 1.1 %adjoint.2 = (bf16[4,256,128]{2,1,0:T(8,128)(2,1)S(1)}, bf16[4,256,128]{2,1,0:T(8,128)(2,1)S(1)}, f32[4,256,128]{2,1,0:T(8,128)S(1)}, f32[4,256,128]{2,1,0:T(8,1...) custom-call(f32[5]{0:T(128)S(1)} %copy-done, ...), custom_call_target="tpu_custom_call" | custom-call | flops 268435456 | bytes 1048576 | tf_op jit(solution)/shard_map/adjoint/pallas_call | solution.py:401
  26.0 1.5 %collective-permute-start.3 = (bf16[4,128,256]{2,1,0:T(8,128)(2,1)S(1)}, bf16[4,128,256]{2,1,0:T(8,128)(2,1)S(1)}, u32[]{:S(2)}, u32[]{:S(2)}) collective-permute-start(bf16[4,128,256]{2,1,0:T(8,128)(2,1)S(1)} %get-tuple-element.46.own_ref), channel_id=1, source_target_pairs={{0,1},{1,0},{2,3},{3,2},{4,5},{5,4},{6,7},{7,6},{8,9},{9,8},{10,11... | collective-permute-start | bytes 786440 | tf_op jit(solution)/shard_map/ppermute | solution.py:150
  27.5 6.3 %collective-permute-done.13.far_ref.refs_4_ = bf16[4,256,128]{2,1,0:T(8,128)(2,1)S(1)} collective-permute-done((bf16[4,256,128]{2,1,0:T(8,128)(2,1)S(1)}, bf16[4,256,128]{2,1,0:T(8,128)(2,1)S(1)}, u32[]{:S(2)}, u32[]{:S(2)}) %collective-permute-start.13) | collective-permute-done | bytes 262176 | tf_op jit(solution)/shard_map/ppermute | solution.py:161
  33.8 1.5 %collective-permute-start.14 = (bf16[4,256,128]{2,1,0:T(8,128)(2,1)S(1)}, bf16[4,256,128]{2,1,0:T(8,128)(2,1)S(1)}, u32[]{:S(2)}, u32[]{:S(2)}) collective-permute-start(bf16[4,256,128]{2,1,0:T(8,128)(2,1)S(1)} %pack_across.4), channel_id=1, source_target_pairs={{0,1},{1,0},{2,3},{3,2},{4,5},{5,4},{6,7},{7,6},{8,9},{9,8},{10,11... | collective-permute-start | bytes 786440 | tf_op jit(solution)/shard_map/ppermute | solution.py:150
  35.4 1.7 %collective-permute-start.4 = (bf16[4,128,256]{2,1,0:T(8,128)(2,1)S(1)}, bf16[4,128,256]{2,1,0:T(8,128)(2,1)S(1)}, u32[]{:S(2)}, u32[]{:S(2)}) collective-permute-start(bf16[4,128,256]{2,1,0:T(8,128)(2,1)S(1)} %get-tuple-element.47.outer.refs_7_), channel_id=1, source_target_pairs={{0,30},{2,4},{4,2},{6,8},{8,6},{10,12},{12,10},{14,16},{16,14},{18... | collective-permute-start | bytes 786440 | tf_op jit(solution)/shard_map/ppermute | solution.py:161
  37.1 1.2 %collective-permute-start.5 = (bf16[4,128,256]{2,1,0:T(8,128)(2,1)S(1)}, bf16[4,128,256]{2,1,0:T(8,128)(2,1)S(1)}, u32[]{:S(2)}, u32[]{:S(2)}) collective-permute-start(bf16[4,128,256]{2,1,0:T(8,128)(2,1)S(1)} %get-tuple-element.48.inner.refs_8_), channel_id=1, source_target_pairs={{0,2},{2,0},{4,6},{6,4},{8,10},{10,8},{12,14},{14,12},{16,18},{18,... | collective-permute-start | bytes 786440 | tf_op jit(solution)/shard_map/ppermute | solution.py:155
  38.3 3.7 %collective-permute-done.14.refs_2_ = bf16[4,256,128]{2,1,0:T(8,128)(2,1)S(1)} collective-permute-done((bf16[4,256,128]{2,1,0:T(8,128)(2,1)S(1)}, bf16[4,256,128]{2,1,0:T(8,128)(2,1)S(1)}, u32[]{:S(2)}, u32[]{:S(2)}) %collective-permute-start.14) | collective-permute-done | bytes 262176 | tf_op jit(solution)/shard_map/ppermute | solution.py:150
  42.0 1.2 %adjoint.3 = (bf16[4,256,128]{2,1,0:T(8,128)(2,1)S(1)}, bf16[4,256,128]{2,1,0:T(8,128)(2,1)S(1)}, f32[4,256,128]{2,1,0:T(8,128)S(1)}, f32[4,256,128]{2,1,0:T(8,128)S(1)}, bf16[4,256,128]{2,1,0:T(8,128)(2,1)S(1)}) custom-call(f32[5]{0:T(128)S(1)} %copy-done, bf16[4,9,128,128]{3,2,1,0:T(8,128)(2,1)S(1)} %get-tuple-element.40.coded, ...), custom_call_target="tpu_custom_call" | custom-call | flops 268435456 | bytes 1048576 | tf_op jit(solution)/shard_map/adjoint/pallas_call | solution.py:401
  44.1 1.1 %forward.3 = (f32[4,128,256]{2,1,0:T(8,128)S(1)}, bf16[4,128,256]{2,1,0:T(8,128)(2,1)S(1)}) custom-call(f32[5]{0:T(128)S(1)} %copy-done, bf16[4,9,128,128]{3,2,1,0:T(8,128)(2,1)S(1)} %get-tuple-element.40.coded, bf16[4,128,256]{2,1,0:T(8,128)(2,1)S(1)} %collective-permute-done.4.far.refs_6_, bf16[4,128,256]{2,1,0:T(8,128)(2,1)S(1)} %get-tuple-element.47.outer.refs_7_, ...), custom_call_target="tpu_custom_call" | custom-call | flops 268435456 | bytes 1048576 | tf_op jit(solution)/shard_map/forward/pallas_call | solution.py:401
  45.2 1.5 %collective-permute-start.6 = (bf16[4,128,256]{2,1,0:T(8,128)(2,1)S(1)}, bf16[4,128,256]{2,1,0:T(8,128)(2,1)S(1)}, u32[]{:S(2)}, u32[]{:S(2)}) collective-permute-start(bf16[4,128,256]{2,1,0:T(8,128)(2,1)S(1)} %get-tuple-element.50.own_ref), channel_id=1, source_target_pairs={{0,1},{1,0},{2,3},{3,2},{4,5},{5,4},{6,7},{7,6},{8,9},{9,8},{10,11... | collective-permute-start | bytes 786440 | tf_op jit(solution)/shard_map/ppermute | solution.py:150
  46.6 1.9 %middle_gradient.1.before_ref = f32[4,8,128,128]{3,2,1,0:T(8,128)S(1)} custom-call(s32[32]{0:T(128)S(1)} %get-tuple-element.39.slots, bf16[4,256,128]{2,1,0:T(8,128)(2,1)S(1)} %get-tuple-element.67.refs_0_, bf16[4,256,128]{2,1,0:T(8,128)(2,1)S(1)} %get-tuple-element.68.refs_1_, bf16[4,128,256]{2,1,0:T(8,128)(2,1)S(1)} %collective-permute-done.1.far.refs_2_, ...), custom_call_target="tpu_custom_call" | custom-call | flops 536870912 | bytes 1048576 | tf_op jit(solution)/shard_map/middle_gradient/pallas_call | solution.py:401
  48.6 4.2 %collective-permute-done.16.far_ref.refs_4_ = bf16[4,256,128]{2,1,0:T(8,128)(2,1)S(1)} collective-permute-done((bf16[4,256,128]{2,1,0:T(8,128)(2,1)S(1)}, bf16[4,256,128]{2,1,0:T(8,128)(2,1)S(1)}, u32[]{:S(2)}, u32[]{:S(2)}) %collective-permute-start.16) | collective-permute-done | bytes 262176 | tf_op jit(solution)/shard_map/ppermute | solution.py:161
  52.8 1.5 %collective-permute-start.17 = (bf16[4,256,128]{2,1,0:T(8,128)(2,1)S(1)}, bf16[4,256,128]{2,1,0:T(8,128)(2,1)S(1)}, u32[]{:S(2)}, u32[]{:S(2)}) collective-permute-start(bf16[4,256,128]{2,1,0:T(8,128)(2,1)S(1)} %pack_across.5), channel_id=1, source_target_pairs={{0,1},{1,0},{2,3},{3,2},{4,5},{5,4},{6,7},{7,6},{8,9},{9,8},{10,11... | collective-permute-start | bytes 786440 | tf_op jit(solution)/shard_map/ppermute | solution.py:150
  56.5 4.4 %collective-permute-done.17.refs_2_ = bf16[4,256,128]{2,1,0:T(8,128)(2,1)S(1)} collective-permute-done((bf16[4,256,128]{2,1,0:T(8,128)(2,1)S(1)}, bf16[4,256,128]{2,1,0:T(8,128)(2,1)S(1)}, u32[]{:S(2)}, u32[]{:S(2)}) %collective-permute-start.17) | collective-permute-done | bytes 262176 | tf_op jit(solution)/shard_map/ppermute | solution.py:150
  60.9 1.3 %first_gradient.1.refs_7_ = f32[4,8,128,128]{3,2,1,0:T(8,128)S(1)} custom-call(s32[32]{0:T(128)S(1)} %get-tuple-element.39.slots, f32[5]{0:T(128)S(1)} %copy-done, f32[4,256,128]{2,1,0:T(8,128)S(1)} %get-tuple-element.61.older_ref, bf16[16,128,256]{2,1,0:T(8,128)(2,1)S(1)} %get-tuple-element.44.before_ref.start_ref, ...), custom_call_target="tpu_custom_call" | custom-call | flops 268435456 | bytes 1048576 | tf_op jit(solution)/shard_map/first_gradient/pallas_call | solution.py:401
  63.0 2.6 %last.1 = (f32[2,2,128,256]{3,2,1,0:T(8,128)}, bf16[2,2,8,128,128]{4,3,2,1,0:T(8,128)(2,1)}) custom-call(s32[2]{0:T(128)S(1)} %get-tuple-element.38.rows, s32[32]{0:T(128)S(1)} %get-tuple-element.39.slots, f32[5]{0:T(128)S(1)} %copy-done, bf16[4,9,128,128]{3,2,1,0:T(8,128)(2,1)S(1)} %get-tuple-element.40.coded, ...), custom_call_target="tpu_custom_call" | custom-call | flops 536870912 | bytes 1048576 | tf_op jit(solution)/shard_map/last/pallas_call | solution.py:401
  (29 shorter events, 6.4 us)
Async XLA Ops:
  0.6 22.1 %copy-start = (f32[5]{0:T(128)S(1)}, f32[5]{0:T(128)}, u32[]{:S(2)}) copy-start(f32[5]{0:T(128)} %coef.11) | copy-start | bytes 64
  4.6 4.0 %collective-permute-start.9 = (bf16[4,256,128]{2,1,0:T(8,128)(2,1)S(1)}, bf16[4,256,128]{2,1,0:T(8,128)(2,1)S(1)}, u32[]{:S(2)}, u32[]{:S(2)}) collective-permute-start(bf16[4,256,128]{2,1,0:T(8,128)(2,1)S(1)} %get-tuple-element.59), channel_id=1, source_target_pairs={{0,2},{2,0},{4,6},{6,4},{8,10},{10,8},{12,14},{14,12},{16,18},{18,... | collective-permute-start | bytes 786440 | tf_op jit(solution)/shard_map/ppermute | solution.py:155
  4.7 8.8 %collective-permute-start.10 = (bf16[4,256,128]{2,1,0:T(8,128)(2,1)S(1)}, bf16[4,256,128]{2,1,0:T(8,128)(2,1)S(1)}, u32[]{:S(2)}, u32[]{:S(2)}) collective-permute-start(bf16[4,256,128]{2,1,0:T(8,128)(2,1)S(1)} %get-tuple-element.60), channel_id=1, source_target_pairs={{0,30},{2,4},{4,2},{6,8},{8,6},{10,12},{12,10},{14,16},{16,14},{18... | collective-permute-start | bytes 786440 | tf_op jit(solution)/shard_map/ppermute | solution.py:161
  7.3 9.0 %collective-permute-start = (bf16[4,128,256]{2,1,0:T(8,128)(2,1)S(1)}, bf16[4,128,256]{2,1,0:T(8,128)(2,1)S(1)}, u32[]{:S(2)}, u32[]{:S(2)}) collective-permute-start(bf16[4,128,256]{2,1,0:T(8,128)(2,1)S(1)} %get-tuple-element.41.own_ref), channel_id=1, source_target_pairs={{0,1},{1,0},{2,3},{3,2},{4,5},{5,4},{6,7},{7,6},{8,9},{9,8},{10,11... | collective-permute-start | bytes 786440 | tf_op jit(solution)/shard_map/ppermute | solution.py:150
  13.5 9.2 %collective-permute-start.11 = (bf16[4,256,128]{2,1,0:T(8,128)(2,1)S(1)}, bf16[4,256,128]{2,1,0:T(8,128)(2,1)S(1)}, u32[]{:S(2)}, u32[]{:S(2)}) collective-permute-start(bf16[4,256,128]{2,1,0:T(8,128)(2,1)S(1)} %pack_across.3), channel_id=1, source_target_pairs={{0,1},{1,0},{2,3},{3,2},{4,5},{5,4},{6,7},{7,6},{8,9},{9,8},{10,11... | collective-permute-start | bytes 786440 | tf_op jit(solution)/shard_map/ppermute | solution.py:150
  16.4 8.4 %collective-permute-start.1 = (bf16[4,128,256]{2,1,0:T(8,128)(2,1)S(1)}, bf16[4,128,256]{2,1,0:T(8,128)(2,1)S(1)}, u32[]{:S(2)}, u32[]{:S(2)}) collective-permute-start(bf16[4,128,256]{2,1,0:T(8,128)(2,1)S(1)} %get-tuple-element.42.outer.refs_3_), channel_id=1, source_target_pairs={{0,30},{2,4},{4,2},{6,8},{8,6},{10,12},{12,10},{14,16},{16,14},{18... | collective-permute-start | bytes 786440 | tf_op jit(solution)/shard_map/ppermute | solution.py:161
  17.7 7.2 %collective-permute-start.2 = (bf16[4,128,256]{2,1,0:T(8,128)(2,1)S(1)}, bf16[4,128,256]{2,1,0:T(8,128)(2,1)S(1)}, u32[]{:S(2)}, u32[]{:S(2)}) collective-permute-start(bf16[4,128,256]{2,1,0:T(8,128)(2,1)S(1)} %get-tuple-element.43.inner.refs_4_), channel_id=1, source_target_pairs={{0,2},{2,0},{4,6},{6,4},{8,10},{10,8},{12,14},{14,12},{16,18},{18,... | collective-permute-start | bytes 786440 | tf_op jit(solution)/shard_map/ppermute | solution.py:155
  23.9 3.6 %collective-permute-start.12 = (bf16[4,256,128]{2,1,0:T(8,128)(2,1)S(1)}, bf16[4,256,128]{2,1,0:T(8,128)(2,1)S(1)}, u32[]{:S(2)}, u32[]{:S(2)}) collective-permute-start(bf16[4,256,128]{2,1,0:T(8,128)(2,1)S(1)} %get-tuple-element.64), channel_id=1, source_target_pairs={{0,2},{2,0},{4,6},{6,4},{8,10},{10,8},{12,14},{14,12},{16,18},{18,... | collective-permute-start | bytes 786440 | tf_op jit(solution)/shard_map/ppermute | solution.py:155
  24.9 8.9 %collective-permute-start.13 = (bf16[4,256,128]{2,1,0:T(8,128)(2,1)S(1)}, bf16[4,256,128]{2,1,0:T(8,128)(2,1)S(1)}, u32[]{:S(2)}, u32[]{:S(2)}) collective-permute-start(bf16[4,256,128]{2,1,0:T(8,128)(2,1)S(1)} %get-tuple-element.65), channel_id=1, source_target_pairs={{0,30},{2,4},{4,2},{6,8},{8,6},{10,12},{12,10},{14,16},{16,14},{18... | collective-permute-start | bytes 786440 | tf_op jit(solution)/shard_map/ppermute | solution.py:161
  26.0 9.4 %collective-permute-start.3 = (bf16[4,128,256]{2,1,0:T(8,128)(2,1)S(1)}, bf16[4,128,256]{2,1,0:T(8,128)(2,1)S(1)}, u32[]{:S(2)}, u32[]{:S(2)}) collective-permute-start(bf16[4,128,256]{2,1,0:T(8,128)(2,1)S(1)} %get-tuple-element.46.own_ref), channel_id=1, source_target_pairs={{0,1},{1,0},{2,3},{3,2},{4,5},{5,4},{6,7},{7,6},{8,9},{9,8},{10,11... | collective-permute-start | bytes 786440 | tf_op jit(solution)/shard_map/ppermute | solution.py:150
  33.8 8.2 %collective-permute-start.14 = (bf16[4,256,128]{2,1,0:T(8,128)(2,1)S(1)}, bf16[4,256,128]{2,1,0:T(8,128)(2,1)S(1)}, u32[]{:S(2)}, u32[]{:S(2)}) collective-permute-start(bf16[4,256,128]{2,1,0:T(8,128)(2,1)S(1)} %pack_across.4), channel_id=1, source_target_pairs={{0,1},{1,0},{2,3},{3,2},{4,5},{5,4},{6,7},{7,6},{8,9},{9,8},{10,11... | collective-permute-start | bytes 786440 | tf_op jit(solution)/shard_map/ppermute | solution.py:150
  35.4 8.7 %collective-permute-start.4 = (bf16[4,128,256]{2,1,0:T(8,128)(2,1)S(1)}, bf16[4,128,256]{2,1,0:T(8,128)(2,1)S(1)}, u32[]{:S(2)}, u32[]{:S(2)}) collective-permute-start(bf16[4,128,256]{2,1,0:T(8,128)(2,1)S(1)} %get-tuple-element.47.outer.refs_7_), channel_id=1, source_target_pairs={{0,30},{2,4},{4,2},{6,8},{8,6},{10,12},{12,10},{14,16},{16,14},{18... | collective-permute-start | bytes 786440 | tf_op jit(solution)/shard_map/ppermute | solution.py:161
  37.1 7.0 %collective-permute-start.5 = (bf16[4,128,256]{2,1,0:T(8,128)(2,1)S(1)}, bf16[4,128,256]{2,1,0:T(8,128)(2,1)S(1)}, u32[]{:S(2)}, u32[]{:S(2)}) collective-permute-start(bf16[4,128,256]{2,1,0:T(8,128)(2,1)S(1)} %get-tuple-element.48.inner.refs_8_), channel_id=1, source_target_pairs={{0,2},{2,0},{4,6},{6,4},{8,10},{10,8},{12,14},{14,12},{16,18},{18,... | collective-permute-start | bytes 786440 | tf_op jit(solution)/shard_map/ppermute | solution.py:155
  43.1 5.4 %collective-permute-start.15 = (bf16[4,256,128]{2,1,0:T(8,128)(2,1)S(1)}, bf16[4,256,128]{2,1,0:T(8,128)(2,1)S(1)}, u32[]{:S(2)}, u32[]{:S(2)}) collective-permute-start(bf16[4,256,128]{2,1,0:T(8,128)(2,1)S(1)} %get-tuple-element.66), channel_id=1, source_target_pairs={{0,2},{2,0},{4,6},{6,4},{8,10},{10,8},{12,14},{14,12},{16,18},{18,... | collective-permute-start | bytes 786440 | tf_op jit(solution)/shard_map/ppermute | solution.py:155
  43.8 8.9 %collective-permute-start.16 = (bf16[4,256,128]{2,1,0:T(8,128)(2,1)S(1)}, bf16[4,256,128]{2,1,0:T(8,128)(2,1)S(1)}, u32[]{:S(2)}, u32[]{:S(2)}) collective-permute-start(bf16[4,256,128]{2,1,0:T(8,128)(2,1)S(1)} %get-tuple-element.73), channel_id=1, source_target_pairs={{0,30},{2,4},{4,2},{6,8},{8,6},{10,12},{12,10},{14,16},{16,14},{18... | collective-permute-start | bytes 786440 | tf_op jit(solution)/shard_map/ppermute | solution.py:161
  45.2 9.1 %collective-permute-start.6 = (bf16[4,128,256]{2,1,0:T(8,128)(2,1)S(1)}, bf16[4,128,256]{2,1,0:T(8,128)(2,1)S(1)}, u32[]{:S(2)}, u32[]{:S(2)}) collective-permute-start(bf16[4,128,256]{2,1,0:T(8,128)(2,1)S(1)} %get-tuple-element.50.own_ref), channel_id=1, source_target_pairs={{0,1},{1,0},{2,3},{3,2},{4,5},{5,4},{6,7},{7,6},{8,9},{9,8},{10,11... | collective-permute-start | bytes 786440 | tf_op jit(solution)/shard_map/ppermute | solution.py:150
  52.8 8.2 %collective-permute-start.17 = (bf16[4,256,128]{2,1,0:T(8,128)(2,1)S(1)}, bf16[4,256,128]{2,1,0:T(8,128)(2,1)S(1)}, u32[]{:S(2)}, u32[]{:S(2)}) collective-permute-start(bf16[4,256,128]{2,1,0:T(8,128)(2,1)S(1)} %pack_across.5), channel_id=1, source_target_pairs={{0,1},{1,0},{2,3},{3,2},{4,5},{5,4},{6,7},{7,6},{8,9},{9,8},{10,11... | collective-permute-start | bytes 786440 | tf_op jit(solution)/shard_map/ppermute | solution.py:150
  54.4 8.7 %collective-permute-start.7 = (bf16[4,128,256]{2,1,0:T(8,128)(2,1)S(1)}, bf16[4,128,256]{2,1,0:T(8,128)(2,1)S(1)}, u32[]{:S(2)}, u32[]{:S(2)}) collective-permute-start(bf16[4,128,256]{2,1,0:T(8,128)(2,1)S(1)} %get-tuple-element.51.refs_1_), channel_id=1, source_target_pairs={{0,30},{2,4},{4,2},{6,8},{8,6},{10,12},{12,10},{14,16},{16,14},{18... | collective-permute-start | bytes 786440 | tf_op jit(solution)/shard_map/ppermute | solution.py:161
  55.4 7.6 %collective-permute-start.8 = (bf16[4,128,256]{2,1,0:T(8,128)(2,1)S(1)}, bf16[4,128,256]{2,1,0:T(8,128)(2,1)S(1)}, u32[]{:S(2)}, u32[]{:S(2)}) collective-permute-start(bf16[4,128,256]{2,1,0:T(8,128)(2,1)S(1)} %get-tuple-element.52.refs_2_), channel_id=1, source_target_pairs={{0,2},{2,0},{4,6},{6,4},{8,10},{10,8},{12,14},{14,12},{16,18},{18,... | collective-permute-start | bytes 786440 | tf_op jit(solution)/shard_map/ppermute | solution.py:155

commit v5 on v4

--- a/solution.py
+++ b/solution.py
@@ -234,20 +234,26 @@
     gx, gy = position[0], position[1]
     odd = lax.rem(gx, 2)
     rows = (odd, 1 - odd)
-    copies = [
+    listed, width = h_ref.shape[1:3]
+    small = [
         pltpu.make_async_copy(source, target, small_sem.at[at])
         for at, (source, target) in enumerate(((seeds_hbm, seeds_ref), (codes_hbm, codes), (coef_hbm, coef)))
     ]
+    cot_copies, h_copies = [], []
     for at in range(4):
         source = (rows[at // 2], at % 2)
-        copies.append(pltpu.make_async_copy(h_hbm.at[source], h_ref.at[at], h_sem.at[at]))
-        copies.append(pltpu.make_async_copy(cot_hbm.at[source], cot_ref.at[at], cot_sem.at[at]))
-    for copy in copies:
+        cot_copies.append(pltpu.make_async_copy(cot_hbm.at[source], cot_ref.at[at], cot_sem.at[at]))
+        h_copies.append(pltpu.make_async_copy(h_hbm.at[source], h_ref.at[at], h_sem.at[at]))
+    for copy in small + cot_copies + h_copies:
         copy.start()
     coded[...] = jnp.zeros_like(coded)
-    for copy in copies[:3]:
+    for copy in small:
         copy.wait()
-    listed, width = h_ref.shape[1:3]
+    for slot in range(16):
+        local = jnp.where(odd == 0, slot // 4 - 1, 2 - slot // 4)
+        place_x = lax.rem(gx * 2 + local + span_x, span_x)
+        place_y = lax.rem(gy * 2 + slot % 4, span_y)
+        start_ref[slot] = start_signs((place_x * span_y + place_y) * width, seeds_ref[...], width)
     places = []
     for at in range(4):
         for k in range(listed):
@@ -259,11 +265,8 @@
             slots_out[at * listed + k] = (1 + at // 2 + step_x) * 4 + lax.rem(at % 2 + step_y + 4, 4)
     for at in range(2):
         rows_out[at] = rows[at]
-    for copy in copies[3:]:
+    for copy in cot_copies:
         copy.wait()
-    for at in range(4):
-        for k in range(listed):
-            coded[at, places[at * listed + k]] = h_ref[at, k]
     fields = []
     for at in range(4):
         cot = cot_ref[at].astype(f32)
@@ -271,11 +274,11 @@
         cot_t_ref[at] = cot_t.astype(bf16)
         adjoint_ref[at] = (coef[top] * cot).astype(bf16)
         fields.append((coef[top] * cot_t).astype(bf16))
-    for slot in range(16):
-        local = jnp.where(odd == 0, slot // 4 - 1, 2 - slot // 4)
-        place_x = lax.rem(gx * 2 + local + span_x, span_x)
-        place_y = lax.rem(gy * 2 + slot % 4, span_y)
-        start_ref[slot] = start_signs((place_x * span_y + place_y) * width, seeds_ref[...], width)
+    for copy in h_copies:
+        copy.wait()
+    for at in range(4):
+        for k in range(listed):
+            coded[at, places[at * listed + k]] = h_ref[at, k]
     push(coded, fields, *sent_refs)
     for at in range(4):
         value = window_product(at, coded, [start_ref.at[pl.ds(4 * row, 4)] for row in range(4)])

time: 65.8 us -> 65.4 us (level)
  no operation moved by 1% of the time
where the time goes in v5:
time: 65.4 us; the launch traced here: 65.2 us
  waiting for transfers between devices  26.4 us (40%)
  starting transfers between devices  23.9 us (37%)
  Pallas kernels  14.1 us (22%)
  between operations  0.74 us (1%)
    ppermute x6, waiting for transfers between devices, swap_far(): return lax.ppermute(value, 'gx', pairs)  16.3 us
    pallas_call x14, Pallas kernels, call(): pl.pallas_call(kernel, in_specs=[smem] * len(scalars) + (in_specs or [vme...  14.1 us
    ppermute x6, waiting for transfers between devices, swap_y(): return lax.ppermute(value, 'gy', [(0, 1), (1, 0)])  10.1 us
    ppermute x6, starting transfers between devices, swap_y(): return lax.ppermute(value, 'gy', [(0, 1), (1, 0)])  10.1 us
    ppermute x6, starting transfers between devices, swap_near(): return lax.ppermute(value, 'gx', [(i, i ^ 1) for i in range(count)])  7.2 us
    ppermute x6, starting transfers between devices, swap_far(): return lax.ppermute(value, 'gx', pairs)  6.63 us
  transfers between devices with their start and end apart: 18, of which 8 were waited for; matrix products, arithmetic and copies ran while one was open for 0% of the time, Pallas kernels for 12%

profile of v5, /device:TPU:1, one launch (start us, length us, event | category | flops | bytes accessed | tf_op | source)
XLA Modules:
  0.0 65.2 jit_solution(16045018667594401226)
XLA Ops:
  0.7 3.5 %first.1 = (s32[2]{0:T(128)S(1)}, s32[32]{0:T(128)S(1)}, bf16[4,9,128,128]{3,2,1,0:T(8,128)(2,1)S(1)}, bf16[16,128,256]{2,1,0:T(8,128)(2,1)S(1)}, f32[4,128,256]...) custom-call(s32[2]{0:T(128)S(1)} %pad_add_fusion.position, ...), custom_call_target="tpu_custom_call" | custom-call | flops 536870912 | bytes 1048576 | tf_op jit(solution)/shard_map/first/pallas_call | solution.py:404
  4.3 2.7 %collective-permute-start.10 = (bf16[4,256,128]{2,1,0:T(8,128)(2,1)S(1)}, bf16[4,256,128]{2,1,0:T(8,128)(2,1)S(1)}, u32[]{:S(2)}, u32[]{:S(2)}) collective-permute-start(bf16[4,256,128]{2,1,0:T(8,128)(2,1)S(1)} %get-tuple-element.60), channel_id=1, source_target_pairs={{0,30},{2,4},{4,2},{6,8},{8,6},{10,12},{12,10},{14,16},{16,14},{18... | collective-permute-start | bytes 786440 | tf_op jit(solution)/shard_map/ppermute | solution.py:161
  7.0 1.2 %collective-permute-start = (bf16[4,128,256]{2,1,0:T(8,128)(2,1)S(1)}, bf16[4,128,256]{2,1,0:T(8,128)(2,1)S(1)}, u32[]{:S(2)}, u32[]{:S(2)}) collective-permute-start(bf16[4,128,256]{2,1,0:T(8,128)(2,1)S(1)} %get-tuple-element.41.own_ref), channel_id=1, source_target_pairs={{0,1},{1,0},{2,3},{3,2},{4,5},{5,4},{6,7},{7,6},{8,9},{9,8},{10,11... | collective-permute-start | bytes 786440 | tf_op jit(solution)/shard_map/ppermute | solution.py:150
  8.2 4.9 %collective-permute-done.10.far_ref.refs_4_ = bf16[4,256,128]{2,1,0:T(8,128)(2,1)S(1)} collective-permute-done((bf16[4,256,128]{2,1,0:T(8,128)(2,1)S(1)}, bf16[4,256,128]{2,1,0:T(8,128)(2,1)S(1)}, u32[]{:S(2)}, u32[]{:S(2)}) %collective-permute-start.10) | collective-permute-done | bytes 262176 | tf_op jit(solution)/shard_map/ppermute | solution.py:161
  13.1 2.8 %collective-permute-start.11 = (bf16[4,256,128]{2,1,0:T(8,128)(2,1)S(1)}, bf16[4,256,128]{2,1,0:T(8,128)(2,1)S(1)}, u32[]{:S(2)}, u32[]{:S(2)}) collective-permute-start(bf16[4,256,128]{2,1,0:T(8,128)(2,1)S(1)} %pack_across.3), channel_id=1, source_target_pairs={{0,1},{1,0},{2,3},{3,2},{4,5},{5,4},{6,7},{7,6},{8,9},{9,8},{10,11... | collective-permute-start | bytes 786440 | tf_op jit(solution)/shard_map/ppermute | solution.py:150
  16.0 1.3 %collective-permute-start.1 = (bf16[4,128,256]{2,1,0:T(8,128)(2,1)S(1)}, bf16[4,128,256]{2,1,0:T(8,128)(2,1)S(1)}, u32[]{:S(2)}, u32[]{:S(2)}) collective-permute-start(bf16[4,128,256]{2,1,0:T(8,128)(2,1)S(1)} %get-tuple-element.42.outer.refs_3_), channel_id=1, source_target_pairs={{0,30},{2,4},{4,2},{6,8},{8,6},{10,12},{12,10},{14,16},{16,14},{18... | collective-permute-start | bytes 786440 | tf_op jit(solution)/shard_map/ppermute | solution.py:161
  17.3 3.1 %collective-permute-start.2 = (bf16[4,128,256]{2,1,0:T(8,128)(2,1)S(1)}, bf16[4,128,256]{2,1,0:T(8,128)(2,1)S(1)}, u32[]{:S(2)}, u32[]{:S(2)}) collective-permute-start(bf16[4,128,256]{2,1,0:T(8,128)(2,1)S(1)} %get-tuple-element.43.inner.refs_4_), channel_id=1, source_target_pairs={{0,2},{2,0},{4,6},{6,4},{8,10},{10,8},{12,14},{14,12},{16,18},{18,... | collective-permute-start | bytes 786440 | tf_op jit(solution)/shard_map/ppermute | solution.py:155
  20.4 2.0 %collective-permute-done.11.refs_2_ = bf16[4,256,128]{2,1,0:T(8,128)(2,1)S(1)} collective-permute-done((bf16[4,256,128]{2,1,0:T(8,128)(2,1)S(1)}, bf16[4,256,128]{2,1,0:T(8,128)(2,1)S(1)}, u32[]{:S(2)}, u32[]{:S(2)}) %collective-permute-start.11) | collective-permute-done | bytes 262176 | tf_op jit(solution)/shard_map/ppermute | solution.py:150
  22.4 1.1 %adjoint.2 = (bf16[4,256,128]{2,1,0:T(8,128)(2,1)S(1)}, bf16[4,256,128]{2,1,0:T(8,128)(2,1)S(1)}, f32[4,256,128]{2,1,0:T(8,128)S(1)}, f32[4,256,128]{2,1,0:T(8,1...) custom-call(f32[5]{0:T(128)S(1)} %copy-done, ...), custom_call_target="tpu_custom_call" | custom-call | flops 268435456 | bytes 1048576 | tf_op jit(solution)/shard_map/adjoint/pallas_call | solution.py:404
  25.6 1.5 %collective-permute-start.3 = (bf16[4,128,256]{2,1,0:T(8,128)(2,1)S(1)}, bf16[4,128,256]{2,1,0:T(8,128)(2,1)S(1)}, u32[]{:S(2)}, u32[]{:S(2)}) collective-permute-start(bf16[4,128,256]{2,1,0:T(8,128)(2,1)S(1)} %get-tuple-element.46.own_ref), channel_id=1, source_target_pairs={{0,1},{1,0},{2,3},{3,2},{4,5},{5,4},{6,7},{7,6},{8,9},{9,8},{10,11... | collective-permute-start | bytes 786440 | tf_op jit(solution)/shard_map/ppermute | solution.py:150
  27.1 6.3 %collective-permute-done.13.far_ref.refs_4_ = bf16[4,256,128]{2,1,0:T(8,128)(2,1)S(1)} collective-permute-done((bf16[4,256,128]{2,1,0:T(8,128)(2,1)S(1)}, bf16[4,256,128]{2,1,0:T(8,128)(2,1)S(1)}, u32[]{:S(2)}, u32[]{:S(2)}) %collective-permute-start.13) | collective-permute-done | bytes 262176 | tf_op jit(solution)/shard_map/ppermute | solution.py:161
  33.4 1.5 %collective-permute-start.14 = (bf16[4,256,128]{2,1,0:T(8,128)(2,1)S(1)}, bf16[4,256,128]{2,1,0:T(8,128)(2,1)S(1)}, u32[]{:S(2)}, u32[]{:S(2)}) collective-permute-start(bf16[4,256,128]{2,1,0:T(8,128)(2,1)S(1)} %pack_across.4), channel_id=1, source_target_pairs={{0,1},{1,0},{2,3},{3,2},{4,5},{5,4},{6,7},{7,6},{8,9},{9,8},{10,11... | collective-permute-start | bytes 786440 | tf_op jit(solution)/shard_map/ppermute | solution.py:150
  35.0 1.7 %collective-permute-start.4 = (bf16[4,128,256]{2,1,0:T(8,128)(2,1)S(1)}, bf16[4,128,256]{2,1,0:T(8,128)(2,1)S(1)}, u32[]{:S(2)}, u32[]{:S(2)}) collective-permute-start(bf16[4,128,256]{2,1,0:T(8,128)(2,1)S(1)} %get-tuple-element.47.outer.refs_7_), channel_id=1, source_target_pairs={{0,30},{2,4},{4,2},{6,8},{8,6},{10,12},{12,10},{14,16},{16,14},{18... | collective-permute-start | bytes 786440 | tf_op jit(solution)/shard_map/ppermute | solution.py:161
  36.7 1.2 %collective-permute-start.5 = (bf16[4,128,256]{2,1,0:T(8,128)(2,1)S(1)}, bf16[4,128,256]{2,1,0:T(8,128)(2,1)S(1)}, u32[]{:S(2)}, u32[]{:S(2)}) collective-permute-start(bf16[4,128,256]{2,1,0:T(8,128)(2,1)S(1)} %get-tuple-element.48.inner.refs_8_), channel_id=1, source_target_pairs={{0,2},{2,0},{4,6},{6,4},{8,10},{10,8},{12,14},{14,12},{16,18},{18,... | collective-permute-start | bytes 786440 | tf_op jit(solution)/shard_map/ppermute | solution.py:155
  37.9 3.7 %collective-permute-done.14.refs_2_ = bf16[4,256,128]{2,1,0:T(8,128)(2,1)S(1)} collective-permute-done((bf16[4,256,128]{2,1,0:T(8,128)(2,1)S(1)}, bf16[4,256,128]{2,1,0:T(8,128)(2,1)S(1)}, u32[]{:S(2)}, u32[]{:S(2)}) %collective-permute-start.14) | collective-permute-done | bytes 262176 | tf_op jit(solution)/shard_map/ppermute | solution.py:150
  41.6 1.2 %adjoint.3 = (bf16[4,256,128]{2,1,0:T(8,128)(2,1)S(1)}, bf16[4,256,128]{2,1,0:T(8,128)(2,1)S(1)}, f32[4,256,128]{2,1,0:T(8,128)S(1)}, f32[4,256,128]{2,1,0:T(8,128)S(1)}, bf16[4,256,128]{2,1,0:T(8,128)(2,1)S(1)}) custom-call(f32[5]{0:T(128)S(1)} %copy-done, bf16[4,9,128,128]{3,2,1,0:T(8,128)(2,1)S(1)} %get-tuple-element.40.coded, ...), custom_call_target="tpu_custom_call" | custom-call | flops 268435456 | bytes 1048576 | tf_op jit(solution)/shard_map/adjoint/pallas_call | solution.py:404
  43.7 1.1 %forward.3 = (f32[4,128,256]{2,1,0:T(8,128)S(1)}, bf16[4,128,256]{2,1,0:T(8,128)(2,1)S(1)}) custom-call(f32[5]{0:T(128)S(1)} %copy-done, bf16[4,9,128,128]{3,2,1,0:T(8,128)(2,1)S(1)} %get-tuple-element.40.coded, bf16[4,128,256]{2,1,0:T(8,128)(2,1)S(1)} %collective-permute-done.4.far.refs_6_, bf16[4,128,256]{2,1,0:T(8,128)(2,1)S(1)} %get-tuple-element.47.outer.refs_7_, ...), custom_call_target="tpu_custom_call" | custom-call | flops 268435456 | bytes 1048576 | tf_op jit(solution)/shard_map/forward/pallas_call | solution.py:404
  44.8 1.5 %collective-permute-start.6 = (bf16[4,128,256]{2,1,0:T(8,128)(2,1)S(1)}, bf16[4,128,256]{2,1,0:T(8,128)(2,1)S(1)}, u32[]{:S(2)}, u32[]{:S(2)}) collective-permute-start(bf16[4,128,256]{2,1,0:T(8,128)(2,1)S(1)} %get-tuple-element.50.own_ref), channel_id=1, source_target_pairs={{0,1},{1,0},{2,3},{3,2},{4,5},{5,4},{6,7},{7,6},{8,9},{9,8},{10,11... | collective-permute-start | bytes 786440 | tf_op jit(solution)/shard_map/ppermute | solution.py:150
  46.3 1.9 %middle_gradient.1.before_ref = f32[4,8,128,128]{3,2,1,0:T(8,128)S(1)} custom-call(s32[32]{0:T(128)S(1)} %get-tuple-element.39.slots, bf16[4,256,128]{2,1,0:T(8,128)(2,1)S(1)} %get-tuple-element.67.refs_0_, bf16[4,256,128]{2,1,0:T(8,128)(2,1)S(1)} %get-tuple-element.68.refs_1_, bf16[4,128,256]{2,1,0:T(8,128)(2,1)S(1)} %collective-permute-done.1.far.refs_2_, ...), custom_call_target="tpu_custom_call" | custom-call | flops 536870912 | bytes 1048576 | tf_op jit(solution)/shard_map/middle_gradient/pallas_call | solution.py:404
  48.2 4.2 %collective-permute-done.16.far_ref.refs_4_ = bf16[4,256,128]{2,1,0:T(8,128)(2,1)S(1)} collective-permute-done((bf16[4,256,128]{2,1,0:T(8,128)(2,1)S(1)}, bf16[4,256,128]{2,1,0:T(8,128)(2,1)S(1)}, u32[]{:S(2)}, u32[]{:S(2)}) %collective-permute-start.16) | collective-permute-done | bytes 262176 | tf_op jit(solution)/shard_map/ppermute | solution.py:161
  52.4 1.5 %collective-permute-start.17 = (bf16[4,256,128]{2,1,0:T(8,128)(2,1)S(1)}, bf16[4,256,128]{2,1,0:T(8,128)(2,1)S(1)}, u32[]{:S(2)}, u32[]{:S(2)}) collective-permute-start(bf16[4,256,128]{2,1,0:T(8,128)(2,1)S(1)} %pack_across.5), channel_id=1, source_target_pairs={{0,1},{1,0},{2,3},{3,2},{4,5},{5,4},{6,7},{7,6},{8,9},{9,8},{10,11... | collective-permute-start | bytes 786440 | tf_op jit(solution)/shard_map/ppermute | solution.py:150
  56.1 4.4 %collective-permute-done.17.refs_2_ = bf16[4,256,128]{2,1,0:T(8,128)(2,1)S(1)} collective-permute-done((bf16[4,256,128]{2,1,0:T(8,128)(2,1)S(1)}, bf16[4,256,128]{2,1,0:T(8,128)(2,1)S(1)}, u32[]{:S(2)}, u32[]{:S(2)}) %collective-permute-start.17) | collective-permute-done | bytes 262176 | tf_op jit(solution)/shard_map/ppermute | solution.py:150
  60.6 1.3 %first_gradient.1.refs_7_ = f32[4,8,128,128]{3,2,1,0:T(8,128)S(1)} custom-call(s32[32]{0:T(128)S(1)} %get-tuple-element.39.slots, f32[5]{0:T(128)S(1)} %copy-done, f32[4,256,128]{2,1,0:T(8,128)S(1)} %get-tuple-element.61.older_ref, bf16[16,128,256]{2,1,0:T(8,128)(2,1)S(1)} %get-tuple-element.44.before_ref.start_ref, ...), custom_call_target="tpu_custom_call" | custom-call | flops 268435456 | bytes 1048576 | tf_op jit(solution)/shard_map/first_gradient/pallas_call | solution.py:404
  62.7 2.6 %last.1 = (f32[2,2,128,256]{3,2,1,0:T(8,128)}, bf16[2,2,8,128,128]{4,3,2,1,0:T(8,128)(2,1)}) custom-call(s32[2]{0:T(128)S(1)} %get-tuple-element.38.rows, s32[32]{0:T(128)S(1)} %get-tuple-element.39.slots, f32[5]{0:T(128)S(1)} %copy-done, bf16[4,9,128,128]{3,2,1,0:T(8,128)(2,1)S(1)} %get-tuple-element.40.coded, ...), custom_call_target="tpu_custom_call" | custom-call | flops 536870912 | bytes 1048576 | tf_op jit(solution)/shard_map/last/pallas_call | solution.py:404
  (29 shorter events, 6.4 us)
Async XLA Ops:
  0.6 21.7 %copy-start = (f32[5]{0:T(128)S(1)}, f32[5]{0:T(128)}, u32[]{:S(2)}) copy-start(f32[5]{0:T(128)} %coef.11) | copy-start | bytes 64
  4.2 4.0 %collective-permute-start.9 = (bf16[4,256,128]{2,1,0:T(8,128)(2,1)S(1)}, bf16[4,256,128]{2,1,0:T(8,128)(2,1)S(1)}, u32[]{:S(2)}, u32[]{:S(2)}) collective-permute-start(bf16[4,256,128]{2,1,0:T(8,128)(2,1)S(1)} %get-tuple-element.59), channel_id=1, source_target_pairs={{0,2},{2,0},{4,6},{6,4},{8,10},{10,8},{12,14},{14,12},{16,18},{18,... | collective-permute-start | bytes 786440 | tf_op jit(solution)/shard_map/ppermute | solution.py:155
  4.3 8.8 %collective-permute-start.10 = (bf16[4,256,128]{2,1,0:T(8,128)(2,1)S(1)}, bf16[4,256,128]{2,1,0:T(8,128)(2,1)S(1)}, u32[]{:S(2)}, u32[]{:S(2)}) collective-permute-start(bf16[4,256,128]{2,1,0:T(8,128)(2,1)S(1)} %get-tuple-element.60), channel_id=1, source_target_pairs={{0,30},{2,4},{4,2},{6,8},{8,6},{10,12},{12,10},{14,16},{16,14},{18... | collective-permute-start | bytes 786440 | tf_op jit(solution)/shard_map/ppermute | solution.py:161
  7.0 9.0 %collective-permute-start = (bf16[4,128,256]{2,1,0:T(8,128)(2,1)S(1)}, bf16[4,128,256]{2,1,0:T(8,128)(2,1)S(1)}, u32[]{:S(2)}, u32[]{:S(2)}) collective-permute-start(bf16[4,128,256]{2,1,0:T(8,128)(2,1)S(1)} %get-tuple-element.41.own_ref), channel_id=1, source_target_pairs={{0,1},{1,0},{2,3},{3,2},{4,5},{5,4},{6,7},{7,6},{8,9},{9,8},{10,11... | collective-permute-start | bytes 786440 | tf_op jit(solution)/shard_map/ppermute | solution.py:150
  13.1 9.2 %collective-permute-start.11 = (bf16[4,256,128]{2,1,0:T(8,128)(2,1)S(1)}, bf16[4,256,128]{2,1,0:T(8,128)(2,1)S(1)}, u32[]{:S(2)}, u32[]{:S(2)}) collective-permute-start(bf16[4,256,128]{2,1,0:T(8,128)(2,1)S(1)} %pack_across.3), channel_id=1, source_target_pairs={{0,1},{1,0},{2,3},{3,2},{4,5},{5,4},{6,7},{7,6},{8,9},{9,8},{10,11... | collective-permute-start | bytes 786440 | tf_op jit(solution)/shard_map/ppermute | solution.py:150
  16.0 8.4 %collective-permute-start.1 = (bf16[4,128,256]{2,1,0:T(8,128)(2,1)S(1)}, bf16[4,128,256]{2,1,0:T(8,128)(2,1)S(1)}, u32[]{:S(2)}, u32[]{:S(2)}) collective-permute-start(bf16[4,128,256]{2,1,0:T(8,128)(2,1)S(1)} %get-tuple-element.42.outer.refs_3_), channel_id=1, source_target_pairs={{0,30},{2,4},{4,2},{6,8},{8,6},{10,12},{12,10},{14,16},{16,14},{18... | collective-permute-start | bytes 786440 | tf_op jit(solution)/shard_map/ppermute | solution.py:161
  17.3 7.2 %collective-permute-start.2 = (bf16[4,128,256]{2,1,0:T(8,128)(2,1)S(1)}, bf16[4,128,256]{2,1,0:T(8,128)(2,1)S(1)}, u32[]{:S(2)}, u32[]{:S(2)}) collective-permute-start(bf16[4,128,256]{2,1,0:T(8,128)(2,1)S(1)} %get-tuple-element.43.inner.refs_4_), channel_id=1, source_target_pairs={{0,2},{2,0},{4,6},{6,4},{8,10},{10,8},{12,14},{14,12},{16,18},{18,... | collective-permute-start | bytes 786440 | tf_op jit(solution)/shard_map/ppermute | solution.py:155
  23.5 3.6 %collective-permute-start.12 = (bf16[4,256,128]{2,1,0:T(8,128)(2,1)S(1)}, bf16[4,256,128]{2,1,0:T(8,128)(2,1)S(1)}, u32[]{:S(2)}, u32[]{:S(2)}) collective-permute-start(bf16[4,256,128]{2,1,0:T(8,128)(2,1)S(1)} %get-tuple-element.64), channel_id=1, source_target_pairs={{0,2},{2,0},{4,6},{6,4},{8,10},{10,8},{12,14},{14,12},{16,18},{18,... | collective-permute-start | bytes 786440 | tf_op jit(solution)/shard_map/ppermute | solution.py:155
  24.5 8.9 %collective-permute-start.13 = (bf16[4,256,128]{2,1,0:T(8,128)(2,1)S(1)}, bf16[4,256,128]{2,1,0:T(8,128)(2,1)S(1)}, u32[]{:S(2)}, u32[]{:S(2)}) collective-permute-start(bf16[4,256,128]{2,1,0:T(8,128)(2,1)S(1)} %get-tuple-element.65), channel_id=1, source_target_pairs={{0,30},{2,4},{4,2},{6,8},{8,6},{10,12},{12,10},{14,16},{16,14},{18... | collective-permute-start | bytes 786440 | tf_op jit(solution)/shard_map/ppermute | solution.py:161
  25.6 9.4 %collective-permute-start.3 = (bf16[4,128,256]{2,1,0:T(8,128)(2,1)S(1)}, bf16[4,128,256]{2,1,0:T(8,128)(2,1)S(1)}, u32[]{:S(2)}, u32[]{:S(2)}) collective-permute-start(bf16[4,128,256]{2,1,0:T(8,128)(2,1)S(1)} %get-tuple-element.46.own_ref), channel_id=1, source_target_pairs={{0,1},{1,0},{2,3},{3,2},{4,5},{5,4},{6,7},{7,6},{8,9},{9,8},{10,11... | collective-permute-start | bytes 786440 | tf_op jit(solution)/shard_map/ppermute | solution.py:150
  33.4 8.2 %collective-permute-start.14 = (bf16[4,256,128]{2,1,0:T(8,128)(2,1)S(1)}, bf16[4,256,128]{2,1,0:T(8,128)(2,1)S(1)}, u32[]{:S(2)}, u32[]{:S(2)}) collective-permute-start(bf16[4,256,128]{2,1,0:T(8,128)(2,1)S(1)} %pack_across.4), channel_id=1, source_target_pairs={{0,1},{1,0},{2,3},{3,2},{4,5},{5,4},{6,7},{7,6},{8,9},{9,8},{10,11... | collective-permute-start | bytes 786440 | tf_op jit(solution)/shard_map/ppermute | solution.py:150
  35.0 8.7 %collective-permute-start.4 = (bf16[4,128,256]{2,1,0:T(8,128)(2,1)S(1)}, bf16[4,128,256]{2,1,0:T(8,128)(2,1)S(1)}, u32[]{:S(2)}, u32[]{:S(2)}) collective-permute-start(bf16[4,128,256]{2,1,0:T(8,128)(2,1)S(1)} %get-tuple-element.47.outer.refs_7_), channel_id=1, source_target_pairs={{0,30},{2,4},{4,2},{6,8},{8,6},{10,12},{12,10},{14,16},{16,14},{18... | collective-permute-start | bytes 786440 | tf_op jit(solution)/shard_map/ppermute | solution.py:161
  36.7 7.0 %collective-permute-start.5 = (bf16[4,128,256]{2,1,0:T(8,128)(2,1)S(1)}, bf16[4,128,256]{2,1,0:T(8,128)(2,1)S(1)}, u32[]{:S(2)}, u32[]{:S(2)}) collective-permute-start(bf16[4,128,256]{2,1,0:T(8,128)(2,1)S(1)} %get-tuple-element.48.inner.refs_8_), channel_id=1, source_target_pairs={{0,2},{2,0},{4,6},{6,4},{8,10},{10,8},{12,14},{14,12},{16,18},{18,... | collective-permute-start | bytes 786440 | tf_op jit(solution)/shard_map/ppermute | solution.py:155
  42.8 5.4 %collective-permute-start.15 = (bf16[4,256,128]{2,1,0:T(8,128)(2,1)S(1)}, bf16[4,256,128]{2,1,0:T(8,128)(2,1)S(1)}, u32[]{:S(2)}, u32[]{:S(2)}) collective-permute-start(bf16[4,256,128]{2,1,0:T(8,128)(2,1)S(1)} %get-tuple-element.66), channel_id=1, source_target_pairs={{0,2},{2,0},{4,6},{6,4},{8,10},{10,8},{12,14},{14,12},{16,18},{18,... | collective-permute-start | bytes 786440 | tf_op jit(solution)/shard_map/ppermute | solution.py:155
  43.5 8.9 %collective-permute-start.16 = (bf16[4,256,128]{2,1,0:T(8,128)(2,1)S(1)}, bf16[4,256,128]{2,1,0:T(8,128)(2,1)S(1)}, u32[]{:S(2)}, u32[]{:S(2)}) collective-permute-start(bf16[4,256,128]{2,1,0:T(8,128)(2,1)S(1)} %get-tuple-element.73), channel_id=1, source_target_pairs={{0,30},{2,4},{4,2},{6,8},{8,6},{10,12},{12,10},{14,16},{16,14},{18... | collective-permute-start | bytes 786440 | tf_op jit(solution)/shard_map/ppermute | solution.py:161
  44.8 9.1 %collective-permute-start.6 = (bf16[4,128,256]{2,1,0:T(8,128)(2,1)S(1)}, bf16[4,128,256]{2,1,0:T(8,128)(2,1)S(1)}, u32[]{:S(2)}, u32[]{:S(2)}) collective-permute-start(bf16[4,128,256]{2,1,0:T(8,128)(2,1)S(1)} %get-tuple-element.50.own_ref), channel_id=1, source_target_pairs={{0,1},{1,0},{2,3},{3,2},{4,5},{5,4},{6,7},{7,6},{8,9},{9,8},{10,11... | collective-permute-start | bytes 786440 | tf_op jit(solution)/shard_map/ppermute | solution.py:150
  52.4 8.2 %collective-permute-start.17 = (bf16[4,256,128]{2,1,0:T(8,128)(2,1)S(1)}, bf16[4,256,128]{2,1,0:T(8,128)(2,1)S(1)}, u32[]{:S(2)}, u32[]{:S(2)}) collective-permute-start(bf16[4,256,128]{2,1,0:T(8,128)(2,1)S(1)} %pack_across.5), channel_id=1, source_target_pairs={{0,1},{1,0},{2,3},{3,2},{4,5},{5,4},{6,7},{7,6},{8,9},{9,8},{10,11... | collective-permute-start | bytes 786440 | tf_op jit(solution)/shard_map/ppermute | solution.py:150
  54.0 8.7 %collective-permute-start.7 = (bf16[4,128,256]{2,1,0:T(8,128)(2,1)S(1)}, bf16[4,128,256]{2,1,0:T(8,128)(2,1)S(1)}, u32[]{:S(2)}, u32[]{:S(2)}) collective-permute-start(bf16[4,128,256]{2,1,0:T(8,128)(2,1)S(1)} %get-tuple-element.51.refs_1_), channel_id=1, source_target_pairs={{0,30},{2,4},{4,2},{6,8},{8,6},{10,12},{12,10},{14,16},{16,14},{18... | collective-permute-start | bytes 786440 | tf_op jit(solution)/shard_map/ppermute | solution.py:161
  55.0 7.6 %collective-permute-start.8 = (bf16[4,128,256]{2,1,0:T(8,128)(2,1)S(1)}, bf16[4,128,256]{2,1,0:T(8,128)(2,1)S(1)}, u32[]{:S(2)}, u32[]{:S(2)}) collective-permute-start(bf16[4,128,256]{2,1,0:T(8,128)(2,1)S(1)} %get-tuple-element.52.refs_2_), channel_id=1, source_target_pairs={{0,2},{2,0},{4,6},{6,4},{8,10},{10,8},{12,14},{14,12},{16,18},{18,... | collective-permute-start | bytes 786440 | tf_op jit(solution)/shard_map/ppermute | solution.py:155

commit v6 on v5

--- a/solution.py
+++ b/solution.py
@@ -227,11 +227,11 @@
 
 
 def first_kernel(
-    top, span_x, span_y, position, seeds_hbm, coef_hbm, codes_hbm, h_hbm, cot_hbm,
+    top, span_x, span_y, seeds_hbm, coef_hbm, codes_hbm, h_hbm, cot_hbm,
     rows_out, slots_out, coded, start_ref, term_ref, cot_t_ref, adjoint_ref, rounded_ref, *rest,
 ):
     sent_refs, (seeds_ref, coef, codes, h_ref, cot_ref, small_sem, h_sem, cot_sem) = rest[:-8], rest[-8:]
-    gx, gy = position[0], position[1]
+    gx, gy = lax.axis_index("gx"), lax.axis_index("gy")
     odd = lax.rem(gx, 2)
     rows = (odd, 1 - odd)
     listed, width = h_ref.shape[1:3]
@@ -274,9 +274,8 @@
         cot_t_ref[at] = cot_t.astype(bf16)
         adjoint_ref[at] = (coef[top] * cot).astype(bf16)
         fields.append((coef[top] * cot_t).astype(bf16))
-    for copy in h_copies:
-        copy.wait()
-    for at in range(4):
+    for at in range(4):
+        h_copies[at].wait()
         for k in range(listed):
             coded[at, places[at * listed + k]] = h_ref[at, k]
     push(coded, fields, *sent_refs)
@@ -341,14 +340,14 @@
         block_gradients(slots, at, jnp.concatenate(left, axis=1), [windows.at[t] for t in range(count)], listed, store)
 
 
-def first_gradient_kernel(slots, coef, older_ref, start_ref, before_ref, *refs):
+def first_gradient_kernel(scale, slots, coef, older_ref, start_ref, before_ref, *refs):
     arrived, sums_ref = refs[:-1], refs[-1]
     listed = sums_ref.shape[1]
     for at in range(4):
         value = adjoint_value(at, 1, coef, *arrived) - older_ref[at]
 
         def store(k, total, at=at):
-            sums_ref[at, k] = before_ref[at, k] + total
+            sums_ref[at, k] = (before_ref[at, k] + total) * scale
 
         block_gradients(slots, at, jnp.transpose(value).astype(bf16), (start_ref,), listed, store)
 
@@ -366,9 +365,9 @@
         copies[-1].start()
 
         def store(k, total, at=at):
-            grad[at, k] = ((early_ref[at, k] + total) * scale).astype(bf16)
-
-        block_gradients(slots, at, adjoint_ref[at] * bf16(2.0), (window,), listed, store)
+            grad[at, k] = (early_ref[at, k] + total).astype(bf16)
+
+        block_gradients(slots, at, adjoint_ref[at] * bf16(2.0 * scale), (window,), listed, store)
         copies.append(pltpu.make_async_copy(grad.at[at], grad_hbm.at[place], grad_sem.at[at]))
         copies[-1].start()
     for copy in copies:
@@ -419,7 +418,7 @@
     rows, slots, coded, start, term, cot_t, adjoint, rounded, to_near, own, to_across, to_far = call(
         "first",
         functools.partial(first_kernel, top, span_x, span_y),
-        (jnp.stack([lax.axis_index("gx"), lax.axis_index("gy")]).astype(jnp.int32),),
+        (),
         tuple(
             pltpu.with_memory_space_constraint(value, pltpu.HBM)
             for value in (probe_seeds.reshape(1, probes), coefficients, neighbours, hamiltonian, cotangent)
@@ -489,7 +488,7 @@
             older = rest[0]
     early = call(
         "first_gradient",
-        first_gradient_kernel,
+        functools.partial(first_gradient_kernel, 1.0 / probes),
         (slots, coefficients), kept((older, start, middle)) + arrived,
         [gradient_sums],
     )[0]

time: 65.4 us -> 64.8 us (level)
  no operation moved by 1% of the time
where the time goes in v6:
time: 64.8 us; the launch traced here: 64.6 us
  waiting for transfers between devices  26.4 us (41%)
  starting transfers between devices  23.9 us (37%)
  Pallas kernels  13.5 us (21%)
  between operations  0.74 us (1%)
    ppermute x6, waiting for transfers between devices, swap_far(): return lax.ppermute(value, 'gx', pairs)  16.3 us
    pallas_call x14, Pallas kernels, call(): pl.pallas_call(kernel, in_specs=[smem] * len(scalars) + (in_specs or [vme...  13.5 us
    ppermute x6, waiting for transfers between devices, swap_y(): return lax.ppermute(value, 'gy', [(0, 1), (1, 0)])  10.1 us
    ppermute x6, starting transfers between devices, swap_y(): return lax.ppermute(value, 'gy', [(0, 1), (1, 0)])  10.1 us
    ppermute x6, starting transfers between devices, swap_near(): return lax.ppermute(value, 'gx', [(i, i ^ 1) for i in range(count)])  7.2 us
    ppermute x6, starting transfers between devices, swap_far(): return lax.ppermute(value, 'gx', pairs)  6.63 us
  transfers between devices with their start and end apart: 18, of which 8 were waited for; matrix products, arithmetic and copies ran while one was open for 0% of the time, Pallas kernels for 12%

profile of v6, /device:TPU:1, one launch (start us, length us, event | category | flops | bytes accessed | tf_op | source)
XLA Modules:
  0.0 64.6 jit_solution(4419069097780584451)
XLA Ops:
  0.6 2.9 %first.1 = (s32[2]{0:T(128)S(1)}, s32[32]{0:T(128)S(1)}, bf16[4,9,128,128]{3,2,1,0:T(8,128)(2,1)S(1)}, bf16[16,128,256]{2,1,0:T(8,128)(2,1)S(1)}, f32[4,128,256]...) custom-call(s32[1,256]{1,0:T(1,128)} %bitcast.1, ...), custom_call_target="tpu_custom_call" | custom-call | flops 536870912 | bytes 1048576 | tf_op jit(solution)/shard_map/first/pallas_call | solution.py:403
  3.7 2.7 %collective-permute-start.10 = (bf16[4,256,128]{2,1,0:T(8,128)(2,1)S(1)}, bf16[4,256,128]{2,1,0:T(8,128)(2,1)S(1)}, u32[]{:S(2)}, u32[]{:S(2)}) collective-permute-start(bf16[4,256,128]{2,1,0:T(8,128)(2,1)S(1)} %get-tuple-element.60), channel_id=1, source_target_pairs={{0,30},{2,4},{4,2},{6,8},{8,6},{10,12},{12,10},{14,16},{16,14},{18... | collective-permute-start | bytes 786440 | tf_op jit(solution)/shard_map/ppermute | solution.py:161
  6.4 1.2 %collective-permute-start = (bf16[4,128,256]{2,1,0:T(8,128)(2,1)S(1)}, bf16[4,128,256]{2,1,0:T(8,128)(2,1)S(1)}, u32[]{:S(2)}, u32[]{:S(2)}) collective-permute-start(bf16[4,128,256]{2,1,0:T(8,128)(2,1)S(1)} %get-tuple-element.41.own_ref), channel_id=1, source_target_pairs={{0,1},{1,0},{2,3},{3,2},{4,5},{5,4},{6,7},{7,6},{8,9},{9,8},{10,11... | collective-permute-start | bytes 786440 | tf_op jit(solution)/shard_map/ppermute | solution.py:150
  7.6 4.9 %collective-permute-done.10.far_ref.refs_4_ = bf16[4,256,128]{2,1,0:T(8,128)(2,1)S(1)} collective-permute-done((bf16[4,256,128]{2,1,0:T(8,128)(2,1)S(1)}, bf16[4,256,128]{2,1,0:T(8,128)(2,1)S(1)}, u32[]{:S(2)}, u32[]{:S(2)}) %collective-permute-start.10) | collective-permute-done | bytes 262176 | tf_op jit(solution)/shard_map/ppermute | solution.py:161
  12.6 2.8 %collective-permute-start.11 = (bf16[4,256,128]{2,1,0:T(8,128)(2,1)S(1)}, bf16[4,256,128]{2,1,0:T(8,128)(2,1)S(1)}, u32[]{:S(2)}, u32[]{:S(2)}) collective-permute-start(bf16[4,256,128]{2,1,0:T(8,128)(2,1)S(1)} %pack_across.3), channel_id=1, source_target_pairs={{0,1},{1,0},{2,3},{3,2},{4,5},{5,4},{6,7},{7,6},{8,9},{9,8},{10,11... | collective-permute-start | bytes 786440 | tf_op jit(solution)/shard_map/ppermute | solution.py:150
  15.4 1.3 %collective-permute-start.1 = (bf16[4,128,256]{2,1,0:T(8,128)(2,1)S(1)}, bf16[4,128,256]{2,1,0:T(8,128)(2,1)S(1)}, u32[]{:S(2)}, u32[]{:S(2)}) collective-permute-start(bf16[4,128,256]{2,1,0:T(8,128)(2,1)S(1)} %get-tuple-element.42.outer.refs_3_), channel_id=1, source_target_pairs={{0,30},{2,4},{4,2},{6,8},{8,6},{10,12},{12,10},{14,16},{16,14},{18... | collective-permute-start | bytes 786440 | tf_op jit(solution)/shard_map/ppermute | solution.py:161
  16.7 3.1 %collective-permute-start.2 = (bf16[4,128,256]{2,1,0:T(8,128)(2,1)S(1)}, bf16[4,128,256]{2,1,0:T(8,128)(2,1)S(1)}, u32[]{:S(2)}, u32[]{:S(2)}) collective-permute-start(bf16[4,128,256]{2,1,0:T(8,128)(2,1)S(1)} %get-tuple-element.43.inner.refs_4_), channel_id=1, source_target_pairs={{0,2},{2,0},{4,6},{6,4},{8,10},{10,8},{12,14},{14,12},{16,18},{18,... | collective-permute-start | bytes 786440 | tf_op jit(solution)/shard_map/ppermute | solution.py:155
  19.8 2.0 %collective-permute-done.11.refs_2_ = bf16[4,256,128]{2,1,0:T(8,128)(2,1)S(1)} collective-permute-done((bf16[4,256,128]{2,1,0:T(8,128)(2,1)S(1)}, bf16[4,256,128]{2,1,0:T(8,128)(2,1)S(1)}, u32[]{:S(2)}, u32[]{:S(2)}) %collective-permute-start.11) | collective-permute-done | bytes 262176 | tf_op jit(solution)/shard_map/ppermute | solution.py:150
  21.8 1.1 %adjoint.2 = (bf16[4,256,128]{2,1,0:T(8,128)(2,1)S(1)}, bf16[4,256,128]{2,1,0:T(8,128)(2,1)S(1)}, f32[4,256,128]{2,1,0:T(8,128)S(1)}, f32[4,256,128]{2,1,0:T(8,1...) custom-call(f32[5]{0:T(128)S(1)} %copy-done, ...), custom_call_target="tpu_custom_call" | custom-call | flops 268435456 | bytes 1048576 | tf_op jit(solution)/shard_map/adjoint/pallas_call | solution.py:403
  25.0 1.5 %collective-permute-start.3 = (bf16[4,128,256]{2,1,0:T(8,128)(2,1)S(1)}, bf16[4,128,256]{2,1,0:T(8,128)(2,1)S(1)}, u32[]{:S(2)}, u32[]{:S(2)}) collective-permute-start(bf16[4,128,256]{2,1,0:T(8,128)(2,1)S(1)} %get-tuple-element.46.own_ref), channel_id=1, source_target_pairs={{0,1},{1,0},{2,3},{3,2},{4,5},{5,4},{6,7},{7,6},{8,9},{9,8},{10,11... | collective-permute-start | bytes 786440 | tf_op jit(solution)/shard_map/ppermute | solution.py:150
  26.5 6.3 %collective-permute-done.13.far_ref.refs_4_ = bf16[4,256,128]{2,1,0:T(8,128)(2,1)S(1)} collective-permute-done((bf16[4,256,128]{2,1,0:T(8,128)(2,1)S(1)}, bf16[4,256,128]{2,1,0:T(8,128)(2,1)S(1)}, u32[]{:S(2)}, u32[]{:S(2)}) %collective-permute-start.13) | collective-permute-done | bytes 262176 | tf_op jit(solution)/shard_map/ppermute | solution.py:161
  32.8 1.5 %collective-permute-start.14 = (bf16[4,256,128]{2,1,0:T(8,128)(2,1)S(1)}, bf16[4,256,128]{2,1,0:T(8,128)(2,1)S(1)}, u32[]{:S(2)}, u32[]{:S(2)}) collective-permute-start(bf16[4,256,128]{2,1,0:T(8,128)(2,1)S(1)} %pack_across.4), channel_id=1, source_target_pairs={{0,1},{1,0},{2,3},{3,2},{4,5},{5,4},{6,7},{7,6},{8,9},{9,8},{10,11... | collective-permute-start | bytes 786440 | tf_op jit(solution)/shard_map/ppermute | solution.py:150
  34.4 1.7 %collective-permute-start.4 = (bf16[4,128,256]{2,1,0:T(8,128)(2,1)S(1)}, bf16[4,128,256]{2,1,0:T(8,128)(2,1)S(1)}, u32[]{:S(2)}, u32[]{:S(2)}) collective-permute-start(bf16[4,128,256]{2,1,0:T(8,128)(2,1)S(1)} %get-tuple-element.47.outer.refs_7_), channel_id=1, source_target_pairs={{0,30},{2,4},{4,2},{6,8},{8,6},{10,12},{12,10},{14,16},{16,14},{18... | collective-permute-start | bytes 786440 | tf_op jit(solution)/shard_map/ppermute | solution.py:161
  36.1 1.2 %collective-permute-start.5 = (bf16[4,128,256]{2,1,0:T(8,128)(2,1)S(1)}, bf16[4,128,256]{2,1,0:T(8,128)(2,1)S(1)}, u32[]{:S(2)}, u32[]{:S(2)}) collective-permute-start(bf16[4,128,256]{2,1,0:T(8,128)(2,1)S(1)} %get-tuple-element.48.inner.refs_8_), channel_id=1, source_target_pairs={{0,2},{2,0},{4,6},{6,4},{8,10},{10,8},{12,14},{14,12},{16,18},{18,... | collective-permute-start | bytes 786440 | tf_op jit(solution)/shard_map/ppermute | solution.py:155
  37.3 3.7 %collective-permute-done.14.refs_2_ = bf16[4,256,128]{2,1,0:T(8,128)(2,1)S(1)} collective-permute-done((bf16[4,256,128]{2,1,0:T(8,128)(2,1)S(1)}, bf16[4,256,128]{2,1,0:T(8,128)(2,1)S(1)}, u32[]{:S(2)}, u32[]{:S(2)}) %collective-permute-start.14) | collective-permute-done | bytes 262176 | tf_op jit(solution)/shard_map/ppermute | solution.py:150
  41.0 1.2 %adjoint.3 = (bf16[4,256,128]{2,1,0:T(8,128)(2,1)S(1)}, bf16[4,256,128]{2,1,0:T(8,128)(2,1)S(1)}, f32[4,256,128]{2,1,0:T(8,128)S(1)}, f32[4,256,128]{2,1,0:T(8,128)S(1)}, bf16[4,256,128]{2,1,0:T(8,128)(2,1)S(1)}) custom-call(f32[5]{0:T(128)S(1)} %copy-done, bf16[4,9,128,128]{3,2,1,0:T(8,128)(2,1)S(1)} %get-tuple-element.40.coded, ...), custom_call_target="tpu_custom_call" | custom-call | flops 268435456 | bytes 1048576 | tf_op jit(solution)/shard_map/adjoint/pallas_call | solution.py:403
  44.2 1.5 %collective-permute-start.6 = (bf16[4,128,256]{2,1,0:T(8,128)(2,1)S(1)}, bf16[4,128,256]{2,1,0:T(8,128)(2,1)S(1)}, u32[]{:S(2)}, u32[]{:S(2)}) collective-permute-start(bf16[4,128,256]{2,1,0:T(8,128)(2,1)S(1)} %get-tuple-element.50.own_ref), channel_id=1, source_target_pairs={{0,1},{1,0},{2,3},{3,2},{4,5},{5,4},{6,7},{7,6},{8,9},{9,8},{10,11... | collective-permute-start | bytes 786440 | tf_op jit(solution)/shard_map/ppermute | solution.py:150
  45.7 1.9 %middle_gradient.1.before_ref = f32[4,8,128,128]{3,2,1,0:T(8,128)S(1)} custom-call(s32[32]{0:T(128)S(1)} %get-tuple-element.39.slots, bf16[4,256,128]{2,1,0:T(8,128)(2,1)S(1)} %get-tuple-element.67.refs_0_, bf16[4,256,128]{2,1,0:T(8,128)(2,1)S(1)} %get-tuple-element.68.refs_1_, bf16[4,128,256]{2,1,0:T(8,128)(2,1)S(1)} %collective-permute-done.1.far.refs_2_, ...), custom_call_target="tpu_custom_call" | custom-call | flops 536870912 | bytes 1048576 | tf_op jit(solution)/shard_map/middle_gradient/pallas_call | solution.py:403
  47.6 4.2 %collective-permute-done.16.far_ref.refs_4_ = bf16[4,256,128]{2,1,0:T(8,128)(2,1)S(1)} collective-permute-done((bf16[4,256,128]{2,1,0:T(8,128)(2,1)S(1)}, bf16[4,256,128]{2,1,0:T(8,128)(2,1)S(1)}, u32[]{:S(2)}, u32[]{:S(2)}) %collective-permute-start.16) | collective-permute-done | bytes 262176 | tf_op jit(solution)/shard_map/ppermute | solution.py:161
  51.8 1.5 %collective-permute-start.17 = (bf16[4,256,128]{2,1,0:T(8,128)(2,1)S(1)}, bf16[4,256,128]{2,1,0:T(8,128)(2,1)S(1)}, u32[]{:S(2)}, u32[]{:S(2)}) collective-permute-start(bf16[4,256,128]{2,1,0:T(8,128)(2,1)S(1)} %pack_across.5), channel_id=1, source_target_pairs={{0,1},{1,0},{2,3},{3,2},{4,5},{5,4},{6,7},{7,6},{8,9},{9,8},{10,11... | collective-permute-start | bytes 786440 | tf_op jit(solution)/shard_map/ppermute | solution.py:150
  54.4 1.1 %collective-permute-start.8 = (bf16[4,128,256]{2,1,0:T(8,128)(2,1)S(1)}, bf16[4,128,256]{2,1,0:T(8,128)(2,1)S(1)}, u32[]{:S(2)}, u32[]{:S(2)}) collective-permute-start(bf16[4,128,256]{2,1,0:T(8,128)(2,1)S(1)} %get-tuple-element.52.refs_2_), channel_id=1, source_target_pairs={{0,2},{2,0},{4,6},{6,4},{8,10},{10,8},{12,14},{14,12},{16,18},{18,... | collective-permute-start | bytes 786440 | tf_op jit(solution)/shard_map/ppermute | solution.py:155
  55.5 4.4 %collective-permute-done.17.refs_2_ = bf16[4,256,128]{2,1,0:T(8,128)(2,1)S(1)} collective-permute-done((bf16[4,256,128]{2,1,0:T(8,128)(2,1)S(1)}, bf16[4,256,128]{2,1,0:T(8,128)(2,1)S(1)}, u32[]{:S(2)}, u32[]{:S(2)}) %collective-permute-start.17) | collective-permute-done | bytes 262176 | tf_op jit(solution)/shard_map/ppermute | solution.py:150
  60.0 1.3 %first_gradient.1.refs_7_ = f32[4,8,128,128]{3,2,1,0:T(8,128)S(1)} custom-call(s32[32]{0:T(128)S(1)} %get-tuple-element.39.slots, f32[5]{0:T(128)S(1)} %copy-done, f32[4,256,128]{2,1,0:T(8,128)S(1)} %get-tuple-element.61.older_ref, bf16[16,128,256]{2,1,0:T(8,128)(2,1)S(1)} %get-tuple-element.44.before_ref.start_ref, ...), custom_call_target="tpu_custom_call" | custom-call | flops 268435456 | bytes 1048576 | tf_op jit(solution)/shard_map/first_gradient/pallas_call | solution.py:403
  62.1 2.6 %last.1 = (f32[2,2,128,256]{3,2,1,0:T(8,128)}, bf16[2,2,8,128,128]{4,3,2,1,0:T(8,128)(2,1)}) custom-call(s32[2]{0:T(128)S(1)} %get-tuple-element.38.rows, s32[32]{0:T(128)S(1)} %get-tuple-element.39.slots, f32[5]{0:T(128)S(1)} %copy-done, bf16[4,9,128,128]{3,2,1,0:T(8,128)(2,1)S(1)} %get-tuple-element.40.coded, ...), custom_call_target="tpu_custom_call" | custom-call | flops 536870912 | bytes 1048576 | tf_op jit(solution)/shard_map/last/pallas_call | solution.py:403
  (28 shorter events, 6.3 us)
Async XLA Ops:
  0.6 21.1 %copy-start = (f32[5]{0:T(128)S(1)}, f32[5]{0:T(128)}, u32[]{:S(2)}) copy-start(f32[5]{0:T(128)} %coef.11) | copy-start | bytes 64
  3.6 4.0 %collective-permute-start.9 = (bf16[4,256,128]{2,1,0:T(8,128)(2,1)S(1)}, bf16[4,256,128]{2,1,0:T(8,128)(2,1)S(1)}, u32[]{:S(2)}, u32[]{:S(2)}) collective-permute-start(bf16[4,256,128]{2,1,0:T(8,128)(2,1)S(1)} %get-tuple-element.59), channel_id=1, source_target_pairs={{0,2},{2,0},{4,6},{6,4},{8,10},{10,8},{12,14},{14,12},{16,18},{18,... | collective-permute-start | bytes 786440 | tf_op jit(solution)/shard_map/ppermute | solution.py:155
  3.7 8.8 %collective-permute-start.10 = (bf16[4,256,128]{2,1,0:T(8,128)(2,1)S(1)}, bf16[4,256,128]{2,1,0:T(8,128)(2,1)S(1)}, u32[]{:S(2)}, u32[]{:S(2)}) collective-permute-start(bf16[4,256,128]{2,1,0:T(8,128)(2,1)S(1)} %get-tuple-element.60), channel_id=1, source_target_pairs={{0,30},{2,4},{4,2},{6,8},{8,6},{10,12},{12,10},{14,16},{16,14},{18... | collective-permute-start | bytes 786440 | tf_op jit(solution)/shard_map/ppermute | solution.py:161
  6.4 9.0 %collective-permute-start = (bf16[4,128,256]{2,1,0:T(8,128)(2,1)S(1)}, bf16[4,128,256]{2,1,0:T(8,128)(2,1)S(1)}, u32[]{:S(2)}, u32[]{:S(2)}) collective-permute-start(bf16[4,128,256]{2,1,0:T(8,128)(2,1)S(1)} %get-tuple-element.41.own_ref), channel_id=1, source_target_pairs={{0,1},{1,0},{2,3},{3,2},{4,5},{5,4},{6,7},{7,6},{8,9},{9,8},{10,11... | collective-permute-start | bytes 786440 | tf_op jit(solution)/shard_map/ppermute | solution.py:150
  12.6 9.2 %collective-permute-start.11 = (bf16[4,256,128]{2,1,0:T(8,128)(2,1)S(1)}, bf16[4,256,128]{2,1,0:T(8,128)(2,1)S(1)}, u32[]{:S(2)}, u32[]{:S(2)}) collective-permute-start(bf16[4,256,128]{2,1,0:T(8,128)(2,1)S(1)} %pack_across.3), channel_id=1, source_target_pairs={{0,1},{1,0},{2,3},{3,2},{4,5},{5,4},{6,7},{7,6},{8,9},{9,8},{10,11... | collective-permute-start | bytes 786440 | tf_op jit(solution)/shard_map/ppermute | solution.py:150
  15.4 8.4 %collective-permute-start.1 = (bf16[4,128,256]{2,1,0:T(8,128)(2,1)S(1)}, bf16[4,128,256]{2,1,0:T(8,128)(2,1)S(1)}, u32[]{:S(2)}, u32[]{:S(2)}) collective-permute-start(bf16[4,128,256]{2,1,0:T(8,128)(2,1)S(1)} %get-tuple-element.42.outer.refs_3_), channel_id=1, source_target_pairs={{0,30},{2,4},{4,2},{6,8},{8,6},{10,12},{12,10},{14,16},{16,14},{18... | collective-permute-start | bytes 786440 | tf_op jit(solution)/shard_map/ppermute | solution.py:161
  16.7 7.2 %collective-permute-start.2 = (bf16[4,128,256]{2,1,0:T(8,128)(2,1)S(1)}, bf16[4,128,256]{2,1,0:T(8,128)(2,1)S(1)}, u32[]{:S(2)}, u32[]{:S(2)}) collective-permute-start(bf16[4,128,256]{2,1,0:T(8,128)(2,1)S(1)} %get-tuple-element.43.inner.refs_4_), channel_id=1, source_target_pairs={{0,2},{2,0},{4,6},{6,4},{8,10},{10,8},{12,14},{14,12},{16,18},{18,... | collective-permute-start | bytes 786440 | tf_op jit(solution)/shard_map/ppermute | solution.py:155
  22.9 3.6 %collective-permute-start.12 = (bf16[4,256,128]{2,1,0:T(8,128)(2,1)S(1)}, bf16[4,256,128]{2,1,0:T(8,128)(2,1)S(1)}, u32[]{:S(2)}, u32[]{:S(2)}) collective-permute-start(bf16[4,256,128]{2,1,0:T(8,128)(2,1)S(1)} %get-tuple-element.64), channel_id=1, source_target_pairs={{0,2},{2,0},{4,6},{6,4},{8,10},{10,8},{12,14},{14,12},{16,18},{18,... | collective-permute-start | bytes 786440 | tf_op jit(solution)/shard_map/ppermute | solution.py:155
  23.9 8.9 %collective-permute-start.13 = (bf16[4,256,128]{2,1,0:T(8,128)(2,1)S(1)}, bf16[4,256,128]{2,1,0:T(8,128)(2,1)S(1)}, u32[]{:S(2)}, u32[]{:S(2)}) collective-permute-start(bf16[4,256,128]{2,1,0:T(8,128)(2,1)S(1)} %get-tuple-element.65), channel_id=1, source_target_pairs={{0,30},{2,4},{4,2},{6,8},{8,6},{10,12},{12,10},{14,16},{16,14},{18... | collective-permute-start | bytes 786440 | tf_op jit(solution)/shard_map/ppermute | solution.py:161
  25.0 9.4 %collective-permute-start.3 = (bf16[4,128,256]{2,1,0:T(8,128)(2,1)S(1)}, bf16[4,128,256]{2,1,0:T(8,128)(2,1)S(1)}, u32[]{:S(2)}, u32[]{:S(2)}) collective-permute-start(bf16[4,128,256]{2,1,0:T(8,128)(2,1)S(1)} %get-tuple-element.46.own_ref), channel_id=1, source_target_pairs={{0,1},{1,0},{2,3},{3,2},{4,5},{5,4},{6,7},{7,6},{8,9},{9,8},{10,11... | collective-permute-start | bytes 786440 | tf_op jit(solution)/shard_map/ppermute | solution.py:150
  32.8 8.2 %collective-permute-start.14 = (bf16[4,256,128]{2,1,0:T(8,128)(2,1)S(1)}, bf16[4,256,128]{2,1,0:T(8,128)(2,1)S(1)}, u32[]{:S(2)}, u32[]{:S(2)}) collective-permute-start(bf16[4,256,128]{2,1,0:T(8,128)(2,1)S(1)} %pack_across.4), channel_id=1, source_target_pairs={{0,1},{1,0},{2,3},{3,2},{4,5},{5,4},{6,7},{7,6},{8,9},{9,8},{10,11... | collective-permute-start | bytes 786440 | tf_op jit(solution)/shard_map/ppermute | solution.py:150
  34.4 8.7 %collective-permute-start.4 = (bf16[4,128,256]{2,1,0:T(8,128)(2,1)S(1)}, bf16[4,128,256]{2,1,0:T(8,128)(2,1)S(1)}, u32[]{:S(2)}, u32[]{:S(2)}) collective-permute-start(bf16[4,128,256]{2,1,0:T(8,128)(2,1)S(1)} %get-tuple-element.47.outer.refs_7_), channel_id=1, source_target_pairs={{0,30},{2,4},{4,2},{6,8},{8,6},{10,12},{12,10},{14,16},{16,14},{18... | collective-permute-start | bytes 786440 | tf_op jit(solution)/shard_map/ppermute | solution.py:161
  36.1 7.0 %collective-permute-start.5 = (bf16[4,128,256]{2,1,0:T(8,128)(2,1)S(1)}, bf16[4,128,256]{2,1,0:T(8,128)(2,1)S(1)}, u32[]{:S(2)}, u32[]{:S(2)}) collective-permute-start(bf16[4,128,256]{2,1,0:T(8,128)(2,1)S(1)} %get-tuple-element.48.inner.refs_8_), channel_id=1, source_target_pairs={{0,2},{2,0},{4,6},{6,4},{8,10},{10,8},{12,14},{14,12},{16,18},{18,... | collective-permute-start | bytes 786440 | tf_op jit(solution)/shard_map/ppermute | solution.py:155
  42.2 5.4 %collective-permute-start.15 = (bf16[4,256,128]{2,1,0:T(8,128)(2,1)S(1)}, bf16[4,256,128]{2,1,0:T(8,128)(2,1)S(1)}, u32[]{:S(2)}, u32[]{:S(2)}) collective-permute-start(bf16[4,256,128]{2,1,0:T(8,128)(2,1)S(1)} %get-tuple-element.66), channel_id=1, source_target_pairs={{0,2},{2,0},{4,6},{6,4},{8,10},{10,8},{12,14},{14,12},{16,18},{18,... | collective-permute-start | bytes 786440 | tf_op jit(solution)/shard_map/ppermute | solution.py:155
  42.9 8.9 %collective-permute-start.16 = (bf16[4,256,128]{2,1,0:T(8,128)(2,1)S(1)}, bf16[4,256,128]{2,1,0:T(8,128)(2,1)S(1)}, u32[]{:S(2)}, u32[]{:S(2)}) collective-permute-start(bf16[4,256,128]{2,1,0:T(8,128)(2,1)S(1)} %get-tuple-element.73), channel_id=1, source_target_pairs={{0,30},{2,4},{4,2},{6,8},{8,6},{10,12},{12,10},{14,16},{16,14},{18... | collective-permute-start | bytes 786440 | tf_op jit(solution)/shard_map/ppermute | solution.py:161
  44.2 9.1 %collective-permute-start.6 = (bf16[4,128,256]{2,1,0:T(8,128)(2,1)S(1)}, bf16[4,128,256]{2,1,0:T(8,128)(2,1)S(1)}, u32[]{:S(2)}, u32[]{:S(2)}) collective-permute-start(bf16[4,128,256]{2,1,0:T(8,128)(2,1)S(1)} %get-tuple-element.50.own_ref), channel_id=1, source_target_pairs={{0,1},{1,0},{2,3},{3,2},{4,5},{5,4},{6,7},{7,6},{8,9},{9,8},{10,11... | collective-permute-start | bytes 786440 | tf_op jit(solution)/shard_map/ppermute | solution.py:150
  51.8 8.2 %collective-permute-start.17 = (bf16[4,256,128]{2,1,0:T(8,128)(2,1)S(1)}, bf16[4,256,128]{2,1,0:T(8,128)(2,1)S(1)}, u32[]{:S(2)}, u32[]{:S(2)}) collective-permute-start(bf16[4,256,128]{2,1,0:T(8,128)(2,1)S(1)} %pack_across.5), channel_id=1, source_target_pairs={{0,1},{1,0},{2,3},{3,2},{4,5},{5,4},{6,7},{7,6},{8,9},{9,8},{10,11... | collective-permute-start | bytes 786440 | tf_op jit(solution)/shard_map/ppermute | solution.py:150
  53.4 8.7 %collective-permute-start.7 = (bf16[4,128,256]{2,1,0:T(8,128)(2,1)S(1)}, bf16[4,128,256]{2,1,0:T(8,128)(2,1)S(1)}, u32[]{:S(2)}, u32[]{:S(2)}) collective-permute-start(bf16[4,128,256]{2,1,0:T(8,128)(2,1)S(1)} %get-tuple-element.51.refs_1_), channel_id=1, source_target_pairs={{0,30},{2,4},{4,2},{6,8},{8,6},{10,12},{12,10},{14,16},{16,14},{18... | collective-permute-start | bytes 786440 | tf_op jit(solution)/shard_map/ppermute | solution.py:161
  54.4 7.6 %collective-permute-start.8 = (bf16[4,128,256]{2,1,0:T(8,128)(2,1)S(1)}, bf16[4,128,256]{2,1,0:T(8,128)(2,1)S(1)}, u32[]{:S(2)}, u32[]{:S(2)}) collective-permute-start(bf16[4,128,256]{2,1,0:T(8,128)(2,1)S(1)} %get-tuple-element.52.refs_2_), channel_id=1, source_target_pairs={{0,2},{2,0},{4,6},{6,4},{8,10},{10,8},{12,14},{14,12},{16,18},{18,... | collective-permute-start | bytes 786440 | tf_op jit(solution)/shard_map/ppermute | solution.py:155

commit v7 on v6

--- a/solution.py
+++ b/solution.py
@@ -162,8 +162,7 @@
 
 
 def start_signs(rows_from, seeds, width):
-    shape = (width, seeds.shape[1])
-    hashed = (rows_from + lax.broadcasted_iota(jnp.int32, shape, 0)) * jnp.int32(-1640531535)
+    hashed = (rows_from + lax.broadcasted_iota(jnp.int32, (width, 1), 0)) * jnp.int32(-1640531535)
     hashed = hashed ^ seeds
     hashed = hashed ^ hashed >> 15
     hashed = hashed * jnp.int32(739982445)

time: 64.8 us -> 64.8 us (level)
  no operation moved by 1% of the time
where the time goes in v7:
time: 64.8 us; the launch traced here: 64.6 us
  waiting for transfers between devices  26.4 us (41%)
  starting transfers between devices  23.9 us (37%)
  Pallas kernels  13.5 us (21%)
  between operations  0.74 us (1%)
    ppermute x6, waiting for transfers between devices, swap_far(): return lax.ppermute(value, 'gx', pairs)  16.3 us
    pallas_call x14, Pallas kernels, call(): pl.pallas_call(kernel, in_specs=[smem] * len(scalars) + (in_specs or [vme...  13.5 us
    ppermute x6, waiting for transfers between devices, swap_y(): return lax.ppermute(value, 'gy', [(0, 1), (1, 0)])  10.1 us
    ppermute x6, starting transfers between devices, swap_y(): return lax.ppermute(value, 'gy', [(0, 1), (1, 0)])  10.1 us
    ppermute x6, starting transfers between devices, swap_near(): return lax.ppermute(value, 'gx', [(i, i ^ 1) for i in range(count)])  7.2 us
    ppermute x6, starting transfers between devices, swap_far(): return lax.ppermute(value, 'gx', pairs)  6.63 us
  transfers between devices with their start and end apart: 18, of which 8 were waited for; matrix products, arithmetic and copies ran while one was open for 0% of the time, Pallas kernels for 12%

profile of v7, /device:TPU:1, one launch (start us, length us, event | category | flops | bytes accessed | tf_op | source)
XLA Modules:
  0.0 64.6 jit_solution(4419069097780584451)
XLA Ops:
  0.6 2.9 %first.1 = (s32[2]{0:T(128)S(1)}, s32[32]{0:T(128)S(1)}, bf16[4,9,128,128]{3,2,1,0:T(8,128)(2,1)S(1)}, bf16[16,128,256]{2,1,0:T(8,128)(2,1)S(1)}, f32[4,128,256]...) custom-call(s32[1,256]{1,0:T(1,128)} %bitcast.1, ...), custom_call_target="tpu_custom_call" | custom-call | flops 536870912 | bytes 1048576 | tf_op jit(solution)/shard_map/first/pallas_call | solution.py:402
  3.7 2.7 %collective-permute-start.10 = (bf16[4,256,128]{2,1,0:T(8,128)(2,1)S(1)}, bf16[4,256,128]{2,1,0:T(8,128)(2,1)S(1)}, u32[]{:S(2)}, u32[]{:S(2)}) collective-permute-start(bf16[4,256,128]{2,1,0:T(8,128)(2,1)S(1)} %get-tuple-element.60), channel_id=1, source_target_pairs={{0,30},{2,4},{4,2},{6,8},{8,6},{10,12},{12,10},{14,16},{16,14},{18... | collective-permute-start | bytes 786440 | tf_op jit(solution)/shard_map/ppermute | solution.py:161
  6.4 1.2 %collective-permute-start = (bf16[4,128,256]{2,1,0:T(8,128)(2,1)S(1)}, bf16[4,128,256]{2,1,0:T(8,128)(2,1)S(1)}, u32[]{:S(2)}, u32[]{:S(2)}) collective-permute-start(bf16[4,128,256]{2,1,0:T(8,128)(2,1)S(1)} %get-tuple-element.41.own_ref), channel_id=1, source_target_pairs={{0,1},{1,0},{2,3},{3,2},{4,5},{5,4},{6,7},{7,6},{8,9},{9,8},{10,11... | collective-permute-start | bytes 786440 | tf_op jit(solution)/shard_map/ppermute | solution.py:150
  7.6 4.9 %collective-permute-done.10.far_ref.refs_4_ = bf16[4,256,128]{2,1,0:T(8,128)(2,1)S(1)} collective-permute-done((bf16[4,256,128]{2,1,0:T(8,128)(2,1)S(1)}, bf16[4,256,128]{2,1,0:T(8,128)(2,1)S(1)}, u32[]{:S(2)}, u32[]{:S(2)}) %collective-permute-start.10) | collective-permute-done | bytes 262176 | tf_op jit(solution)/shard_map/ppermute | solution.py:161
  12.6 2.8 %collective-permute-start.11 = (bf16[4,256,128]{2,1,0:T(8,128)(2,1)S(1)}, bf16[4,256,128]{2,1,0:T(8,128)(2,1)S(1)}, u32[]{:S(2)}, u32[]{:S(2)}) collective-permute-start(bf16[4,256,128]{2,1,0:T(8,128)(2,1)S(1)} %pack_across.3), channel_id=1, source_target_pairs={{0,1},{1,0},{2,3},{3,2},{4,5},{5,4},{6,7},{7,6},{8,9},{9,8},{10,11... | collective-permute-start | bytes 786440 | tf_op jit(solution)/shard_map/ppermute | solution.py:150
  15.4 1.3 %collective-permute-start.1 = (bf16[4,128,256]{2,1,0:T(8,128)(2,1)S(1)}, bf16[4,128,256]{2,1,0:T(8,128)(2,1)S(1)}, u32[]{:S(2)}, u32[]{:S(2)}) collective-permute-start(bf16[4,128,256]{2,1,0:T(8,128)(2,1)S(1)} %get-tuple-element.42.outer.refs_3_), channel_id=1, source_target_pairs={{0,30},{2,4},{4,2},{6,8},{8,6},{10,12},{12,10},{14,16},{16,14},{18... | collective-permute-start | bytes 786440 | tf_op jit(solution)/shard_map/ppermute | solution.py:161
  16.7 3.1 %collective-permute-start.2 = (bf16[4,128,256]{2,1,0:T(8,128)(2,1)S(1)}, bf16[4,128,256]{2,1,0:T(8,128)(2,1)S(1)}, u32[]{:S(2)}, u32[]{:S(2)}) collective-permute-start(bf16[4,128,256]{2,1,0:T(8,128)(2,1)S(1)} %get-tuple-element.43.inner.refs_4_), channel_id=1, source_target_pairs={{0,2},{2,0},{4,6},{6,4},{8,10},{10,8},{12,14},{14,12},{16,18},{18,... | collective-permute-start | bytes 786440 | tf_op jit(solution)/shard_map/ppermute | solution.py:155
  19.8 2.0 %collective-permute-done.11.refs_2_ = bf16[4,256,128]{2,1,0:T(8,128)(2,1)S(1)} collective-permute-done((bf16[4,256,128]{2,1,0:T(8,128)(2,1)S(1)}, bf16[4,256,128]{2,1,0:T(8,128)(2,1)S(1)}, u32[]{:S(2)}, u32[]{:S(2)}) %collective-permute-start.11) | collective-permute-done | bytes 262176 | tf_op jit(solution)/shard_map/ppermute | solution.py:150
  21.8 1.1 %adjoint.2 = (bf16[4,256,128]{2,1,0:T(8,128)(2,1)S(1)}, bf16[4,256,128]{2,1,0:T(8,128)(2,1)S(1)}, f32[4,256,128]{2,1,0:T(8,128)S(1)}, f32[4,256,128]{2,1,0:T(8,1...) custom-call(f32[5]{0:T(128)S(1)} %copy-done, ...), custom_call_target="tpu_custom_call" | custom-call | flops 268435456 | bytes 1048576 | tf_op jit(solution)/shard_map/adjoint/pallas_call | solution.py:402
  25.0 1.5 %collective-permute-start.3 = (bf16[4,128,256]{2,1,0:T(8,128)(2,1)S(1)}, bf16[4,128,256]{2,1,0:T(8,128)(2,1)S(1)}, u32[]{:S(2)}, u32[]{:S(2)}) collective-permute-start(bf16[4,128,256]{2,1,0:T(8,128)(2,1)S(1)} %get-tuple-element.46.own_ref), channel_id=1, source_target_pairs={{0,1},{1,0},{2,3},{3,2},{4,5},{5,4},{6,7},{7,6},{8,9},{9,8},{10,11... | collective-permute-start | bytes 786440 | tf_op jit(solution)/shard_map/ppermute | solution.py:150
  26.5 6.3 %collective-permute-done.13.far_ref.refs_4_ = bf16[4,256,128]{2,1,0:T(8,128)(2,1)S(1)} collective-permute-done((bf16[4,256,128]{2,1,0:T(8,128)(2,1)S(1)}, bf16[4,256,128]{2,1,0:T(8,128)(2,1)S(1)}, u32[]{:S(2)}, u32[]{:S(2)}) %collective-permute-start.13) | collective-permute-done | bytes 262176 | tf_op jit(solution)/shard_map/ppermute | solution.py:161
  32.8 1.5 %collective-permute-start.14 = (bf16[4,256,128]{2,1,0:T(8,128)(2,1)S(1)}, bf16[4,256,128]{2,1,0:T(8,128)(2,1)S(1)}, u32[]{:S(2)}, u32[]{:S(2)}) collective-permute-start(bf16[4,256,128]{2,1,0:T(8,128)(2,1)S(1)} %pack_across.4), channel_id=1, source_target_pairs={{0,1},{1,0},{2,3},{3,2},{4,5},{5,4},{6,7},{7,6},{8,9},{9,8},{10,11... | collective-permute-start | bytes 786440 | tf_op jit(solution)/shard_map/ppermute | solution.py:150
  34.4 1.7 %collective-permute-start.4 = (bf16[4,128,256]{2,1,0:T(8,128)(2,1)S(1)}, bf16[4,128,256]{2,1,0:T(8,128)(2,1)S(1)}, u32[]{:S(2)}, u32[]{:S(2)}) collective-permute-start(bf16[4,128,256]{2,1,0:T(8,128)(2,1)S(1)} %get-tuple-element.47.outer.refs_7_), channel_id=1, source_target_pairs={{0,30},{2,4},{4,2},{6,8},{8,6},{10,12},{12,10},{14,16},{16,14},{18... | collective-permute-start | bytes 786440 | tf_op jit(solution)/shard_map/ppermute | solution.py:161
  36.1 1.2 %collective-permute-start.5 = (bf16[4,128,256]{2,1,0:T(8,128)(2,1)S(1)}, bf16[4,128,256]{2,1,0:T(8,128)(2,1)S(1)}, u32[]{:S(2)}, u32[]{:S(2)}) collective-permute-start(bf16[4,128,256]{2,1,0:T(8,128)(2,1)S(1)} %get-tuple-element.48.inner.refs_8_), channel_id=1, source_target_pairs={{0,2},{2,0},{4,6},{6,4},{8,10},{10,8},{12,14},{14,12},{16,18},{18,... | collective-permute-start | bytes 786440 | tf_op jit(solution)/shard_map/ppermute | solution.py:155
  37.3 3.7 %collective-permute-done.14.refs_2_ = bf16[4,256,128]{2,1,0:T(8,128)(2,1)S(1)} collective-permute-done((bf16[4,256,128]{2,1,0:T(8,128)(2,1)S(1)}, bf16[4,256,128]{2,1,0:T(8,128)(2,1)S(1)}, u32[]{:S(2)}, u32[]{:S(2)}) %collective-permute-start.14) | collective-permute-done | bytes 262176 | tf_op jit(solution)/shard_map/ppermute | solution.py:150
  41.0 1.2 %adjoint.3 = (bf16[4,256,128]{2,1,0:T(8,128)(2,1)S(1)}, bf16[4,256,128]{2,1,0:T(8,128)(2,1)S(1)}, f32[4,256,128]{2,1,0:T(8,128)S(1)}, f32[4,256,128]{2,1,0:T(8,128)S(1)}, bf16[4,256,128]{2,1,0:T(8,128)(2,1)S(1)}) custom-call(f32[5]{0:T(128)S(1)} %copy-done, bf16[4,9,128,128]{3,2,1,0:T(8,128)(2,1)S(1)} %get-tuple-element.40.coded, ...), custom_call_target="tpu_custom_call" | custom-call | flops 268435456 | bytes 1048576 | tf_op jit(solution)/shard_map/adjoint/pallas_call | solution.py:402
  44.2 1.5 %collective-permute-start.6 = (bf16[4,128,256]{2,1,0:T(8,128)(2,1)S(1)}, bf16[4,128,256]{2,1,0:T(8,128)(2,1)S(1)}, u32[]{:S(2)}, u32[]{:S(2)}) collective-permute-start(bf16[4,128,256]{2,1,0:T(8,128)(2,1)S(1)} %get-tuple-element.50.own_ref), channel_id=1, source_target_pairs={{0,1},{1,0},{2,3},{3,2},{4,5},{5,4},{6,7},{7,6},{8,9},{9,8},{10,11... | collective-permute-start | bytes 786440 | tf_op jit(solution)/shard_map/ppermute | solution.py:150
  45.7 1.9 %middle_gradient.1.before_ref = f32[4,8,128,128]{3,2,1,0:T(8,128)S(1)} custom-call(s32[32]{0:T(128)S(1)} %get-tuple-element.39.slots, bf16[4,256,128]{2,1,0:T(8,128)(2,1)S(1)} %get-tuple-element.67.refs_0_, bf16[4,256,128]{2,1,0:T(8,128)(2,1)S(1)} %get-tuple-element.68.refs_1_, bf16[4,128,256]{2,1,0:T(8,128)(2,1)S(1)} %collective-permute-done.1.far.refs_2_, ...), custom_call_target="tpu_custom_call" | custom-call | flops 536870912 | bytes 1048576 | tf_op jit(solution)/shard_map/middle_gradient/pallas_call | solution.py:402
  47.6 4.2 %collective-permute-done.16.far_ref.refs_4_ = bf16[4,256,128]{2,1,0:T(8,128)(2,1)S(1)} collective-permute-done((bf16[4,256,128]{2,1,0:T(8,128)(2,1)S(1)}, bf16[4,256,128]{2,1,0:T(8,128)(2,1)S(1)}, u32[]{:S(2)}, u32[]{:S(2)}) %collective-permute-start.16) | collective-permute-done | bytes 262176 | tf_op jit(solution)/shard_map/ppermute | solution.py:161
  51.8 1.5 %collective-permute-start.17 = (bf16[4,256,128]{2,1,0:T(8,128)(2,1)S(1)}, bf16[4,256,128]{2,1,0:T(8,128)(2,1)S(1)}, u32[]{:S(2)}, u32[]{:S(2)}) collective-permute-start(bf16[4,256,128]{2,1,0:T(8,128)(2,1)S(1)} %pack_across.5), channel_id=1, source_target_pairs={{0,1},{1,0},{2,3},{3,2},{4,5},{5,4},{6,7},{7,6},{8,9},{9,8},{10,11... | collective-permute-start | bytes 786440 | tf_op jit(solution)/shard_map/ppermute | solution.py:150
  54.4 1.1 %collective-permute-start.8 = (bf16[4,128,256]{2,1,0:T(8,128)(2,1)S(1)}, bf16[4,128,256]{2,1,0:T(8,128)(2,1)S(1)}, u32[]{:S(2)}, u32[]{:S(2)}) collective-permute-start(bf16[4,128,256]{2,1,0:T(8,128)(2,1)S(1)} %get-tuple-element.52.refs_2_), channel_id=1, source_target_pairs={{0,2},{2,0},{4,6},{6,4},{8,10},{10,8},{12,14},{14,12},{16,18},{18,... | collective-permute-start | bytes 786440 | tf_op jit(solution)/shard_map/ppermute | solution.py:155
  55.5 4.4 %collective-permute-done.17.refs_2_ = bf16[4,256,128]{2,1,0:T(8,128)(2,1)S(1)} collective-permute-done((bf16[4,256,128]{2,1,0:T(8,128)(2,1)S(1)}, bf16[4,256,128]{2,1,0:T(8,128)(2,1)S(1)}, u32[]{:S(2)}, u32[]{:S(2)}) %collective-permute-start.17) | collective-permute-done | bytes 262176 | tf_op jit(solution)/shard_map/ppermute | solution.py:150
  60.0 1.3 %first_gradient.1.refs_7_ = f32[4,8,128,128]{3,2,1,0:T(8,128)S(1)} custom-call(s32[32]{0:T(128)S(1)} %get-tuple-element.39.slots, f32[5]{0:T(128)S(1)} %copy-done, f32[4,256,128]{2,1,0:T(8,128)S(1)} %get-tuple-element.61.older_ref, bf16[16,128,256]{2,1,0:T(8,128)(2,1)S(1)} %get-tuple-element.44.before_ref.start_ref, ...), custom_call_target="tpu_custom_call" | custom-call | flops 268435456 | bytes 1048576 | tf_op jit(solution)/shard_map/first_gradient/pallas_call | solution.py:402
  62.1 2.6 %last.1 = (f32[2,2,128,256]{3,2,1,0:T(8,128)}, bf16[2,2,8,128,128]{4,3,2,1,0:T(8,128)(2,1)}) custom-call(s32[2]{0:T(128)S(1)} %get-tuple-element.38.rows, s32[32]{0:T(128)S(1)} %get-tuple-element.39.slots, f32[5]{0:T(128)S(1)} %copy-done, bf16[4,9,128,128]{3,2,1,0:T(8,128)(2,1)S(1)} %get-tuple-element.40.coded, ...), custom_call_target="tpu_custom_call" | custom-call | flops 536870912 | bytes 1048576 | tf_op jit(solution)/shard_map/last/pallas_call | solution.py:402
  (28 shorter events, 6.3 us)
Async XLA Ops:
  0.6 21.1 %copy-start = (f32[5]{0:T(128)S(1)}, f32[5]{0:T(128)}, u32[]{:S(2)}) copy-start(f32[5]{0:T(128)} %coef.11) | copy-start | bytes 64
  3.6 4.0 %collective-permute-start.9 = (bf16[4,256,128]{2,1,0:T(8,128)(2,1)S(1)}, bf16[4,256,128]{2,1,0:T(8,128)(2,1)S(1)}, u32[]{:S(2)}, u32[]{:S(2)}) collective-permute-start(bf16[4,256,128]{2,1,0:T(8,128)(2,1)S(1)} %get-tuple-element.59), channel_id=1, source_target_pairs={{0,2},{2,0},{4,6},{6,4},{8,10},{10,8},{12,14},{14,12},{16,18},{18,... | collective-permute-start | bytes 786440 | tf_op jit(solution)/shard_map/ppermute | solution.py:155
  3.7 8.8 %collective-permute-start.10 = (bf16[4,256,128]{2,1,0:T(8,128)(2,1)S(1)}, bf16[4,256,128]{2,1,0:T(8,128)(2,1)S(1)}, u32[]{:S(2)}, u32[]{:S(2)}) collective-permute-start(bf16[4,256,128]{2,1,0:T(8,128)(2,1)S(1)} %get-tuple-element.60), channel_id=1, source_target_pairs={{0,30},{2,4},{4,2},{6,8},{8,6},{10,12},{12,10},{14,16},{16,14},{18... | collective-permute-start | bytes 786440 | tf_op jit(solution)/shard_map/ppermute | solution.py:161
  6.4 9.0 %collective-permute-start = (bf16[4,128,256]{2,1,0:T(8,128)(2,1)S(1)}, bf16[4,128,256]{2,1,0:T(8,128)(2,1)S(1)}, u32[]{:S(2)}, u32[]{:S(2)}) collective-permute-start(bf16[4,128,256]{2,1,0:T(8,128)(2,1)S(1)} %get-tuple-element.41.own_ref), channel_id=1, source_target_pairs={{0,1},{1,0},{2,3},{3,2},{4,5},{5,4},{6,7},{7,6},{8,9},{9,8},{10,11... | collective-permute-start | bytes 786440 | tf_op jit(solution)/shard_map/ppermute | solution.py:150
  12.6 9.2 %collective-permute-start.11 = (bf16[4,256,128]{2,1,0:T(8,128)(2,1)S(1)}, bf16[4,256,128]{2,1,0:T(8,128)(2,1)S(1)}, u32[]{:S(2)}, u32[]{:S(2)}) collective-permute-start(bf16[4,256,128]{2,1,0:T(8,128)(2,1)S(1)} %pack_across.3), channel_id=1, source_target_pairs={{0,1},{1,0},{2,3},{3,2},{4,5},{5,4},{6,7},{7,6},{8,9},{9,8},{10,11... | collective-permute-start | bytes 786440 | tf_op jit(solution)/shard_map/ppermute | solution.py:150
  15.4 8.4 %collective-permute-start.1 = (bf16[4,128,256]{2,1,0:T(8,128)(2,1)S(1)}, bf16[4,128,256]{2,1,0:T(8,128)(2,1)S(1)}, u32[]{:S(2)}, u32[]{:S(2)}) collective-permute-start(bf16[4,128,256]{2,1,0:T(8,128)(2,1)S(1)} %get-tuple-element.42.outer.refs_3_), channel_id=1, source_target_pairs={{0,30},{2,4},{4,2},{6,8},{8,6},{10,12},{12,10},{14,16},{16,14},{18... | collective-permute-start | bytes 786440 | tf_op jit(solution)/shard_map/ppermute | solution.py:161
  16.7 7.2 %collective-permute-start.2 = (bf16[4,128,256]{2,1,0:T(8,128)(2,1)S(1)}, bf16[4,128,256]{2,1,0:T(8,128)(2,1)S(1)}, u32[]{:S(2)}, u32[]{:S(2)}) collective-permute-start(bf16[4,128,256]{2,1,0:T(8,128)(2,1)S(1)} %get-tuple-element.43.inner.refs_4_), channel_id=1, source_target_pairs={{0,2},{2,0},{4,6},{6,4},{8,10},{10,8},{12,14},{14,12},{16,18},{18,... | collective-permute-start | bytes 786440 | tf_op jit(solution)/shard_map/ppermute | solution.py:155
  22.9 3.6 %collective-permute-start.12 = (bf16[4,256,128]{2,1,0:T(8,128)(2,1)S(1)}, bf16[4,256,128]{2,1,0:T(8,128)(2,1)S(1)}, u32[]{:S(2)}, u32[]{:S(2)}) collective-permute-start(bf16[4,256,128]{2,1,0:T(8,128)(2,1)S(1)} %get-tuple-element.64), channel_id=1, source_target_pairs={{0,2},{2,0},{4,6},{6,4},{8,10},{10,8},{12,14},{14,12},{16,18},{18,... | collective-permute-start | bytes 786440 | tf_op jit(solution)/shard_map/ppermute | solution.py:155
  23.9 8.9 %collective-permute-start.13 = (bf16[4,256,128]{2,1,0:T(8,128)(2,1)S(1)}, bf16[4,256,128]{2,1,0:T(8,128)(2,1)S(1)}, u32[]{:S(2)}, u32[]{:S(2)}) collective-permute-start(bf16[4,256,128]{2,1,0:T(8,128)(2,1)S(1)} %get-tuple-element.65), channel_id=1, source_target_pairs={{0,30},{2,4},{4,2},{6,8},{8,6},{10,12},{12,10},{14,16},{16,14},{18... | collective-permute-start | bytes 786440 | tf_op jit(solution)/shard_map/ppermute | solution.py:161
  25.0 9.4 %collective-permute-start.3 = (bf16[4,128,256]{2,1,0:T(8,128)(2,1)S(1)}, bf16[4,128,256]{2,1,0:T(8,128)(2,1)S(1)}, u32[]{:S(2)}, u32[]{:S(2)}) collective-permute-start(bf16[4,128,256]{2,1,0:T(8,128)(2,1)S(1)} %get-tuple-element.46.own_ref), channel_id=1, source_target_pairs={{0,1},{1,0},{2,3},{3,2},{4,5},{5,4},{6,7},{7,6},{8,9},{9,8},{10,11... | collective-permute-start | bytes 786440 | tf_op jit(solution)/shard_map/ppermute | solution.py:150
  32.8 8.2 %collective-permute-start.14 = (bf16[4,256,128]{2,1,0:T(8,128)(2,1)S(1)}, bf16[4,256,128]{2,1,0:T(8,128)(2,1)S(1)}, u32[]{:S(2)}, u32[]{:S(2)}) collective-permute-start(bf16[4,256,128]{2,1,0:T(8,128)(2,1)S(1)} %pack_across.4), channel_id=1, source_target_pairs={{0,1},{1,0},{2,3},{3,2},{4,5},{5,4},{6,7},{7,6},{8,9},{9,8},{10,11... | collective-permute-start | bytes 786440 | tf_op jit(solution)/shard_map/ppermute | solution.py:150
  34.4 8.7 %collective-permute-start.4 = (bf16[4,128,256]{2,1,0:T(8,128)(2,1)S(1)}, bf16[4,128,256]{2,1,0:T(8,128)(2,1)S(1)}, u32[]{:S(2)}, u32[]{:S(2)}) collective-permute-start(bf16[4,128,256]{2,1,0:T(8,128)(2,1)S(1)} %get-tuple-element.47.outer.refs_7_), channel_id=1, source_target_pairs={{0,30},{2,4},{4,2},{6,8},{8,6},{10,12},{12,10},{14,16},{16,14},{18... | collective-permute-start | bytes 786440 | tf_op jit(solution)/shard_map/ppermute | solution.py:161
  36.1 7.0 %collective-permute-start.5 = (bf16[4,128,256]{2,1,0:T(8,128)(2,1)S(1)}, bf16[4,128,256]{2,1,0:T(8,128)(2,1)S(1)}, u32[]{:S(2)}, u32[]{:S(2)}) collective-permute-start(bf16[4,128,256]{2,1,0:T(8,128)(2,1)S(1)} %get-tuple-element.48.inner.refs_8_), channel_id=1, source_target_pairs={{0,2},{2,0},{4,6},{6,4},{8,10},{10,8},{12,14},{14,12},{16,18},{18,... | collective-permute-start | bytes 786440 | tf_op jit(solution)/shard_map/ppermute | solution.py:155
  42.2 5.4 %collective-permute-start.15 = (bf16[4,256,128]{2,1,0:T(8,128)(2,1)S(1)}, bf16[4,256,128]{2,1,0:T(8,128)(2,1)S(1)}, u32[]{:S(2)}, u32[]{:S(2)}) collective-permute-start(bf16[4,256,128]{2,1,0:T(8,128)(2,1)S(1)} %get-tuple-element.66), channel_id=1, source_target_pairs={{0,2},{2,0},{4,6},{6,4},{8,10},{10,8},{12,14},{14,12},{16,18},{18,... | collective-permute-start | bytes 786440 | tf_op jit(solution)/shard_map/ppermute | solution.py:155
  42.9 8.9 %collective-permute-start.16 = (bf16[4,256,128]{2,1,0:T(8,128)(2,1)S(1)}, bf16[4,256,128]{2,1,0:T(8,128)(2,1)S(1)}, u32[]{:S(2)}, u32[]{:S(2)}) collective-permute-start(bf16[4,256,128]{2,1,0:T(8,128)(2,1)S(1)} %get-tuple-element.73), channel_id=1, source_target_pairs={{0,30},{2,4},{4,2},{6,8},{8,6},{10,12},{12,10},{14,16},{16,14},{18... | collective-permute-start | bytes 786440 | tf_op jit(solution)/shard_map/ppermute | solution.py:161
  44.2 9.1 %collective-permute-start.6 = (bf16[4,128,256]{2,1,0:T(8,128)(2,1)S(1)}, bf16[4,128,256]{2,1,0:T(8,128)(2,1)S(1)}, u32[]{:S(2)}, u32[]{:S(2)}) collective-permute-start(bf16[4,128,256]{2,1,0:T(8,128)(2,1)S(1)} %get-tuple-element.50.own_ref), channel_id=1, source_target_pairs={{0,1},{1,0},{2,3},{3,2},{4,5},{5,4},{6,7},{7,6},{8,9},{9,8},{10,11... | collective-permute-start | bytes 786440 | tf_op jit(solution)/shard_map/ppermute | solution.py:150
  51.8 8.2 %collective-permute-start.17 = (bf16[4,256,128]{2,1,0:T(8,128)(2,1)S(1)}, bf16[4,256,128]{2,1,0:T(8,128)(2,1)S(1)}, u32[]{:S(2)}, u32[]{:S(2)}) collective-permute-start(bf16[4,256,128]{2,1,0:T(8,128)(2,1)S(1)} %pack_across.5), channel_id=1, source_target_pairs={{0,1},{1,0},{2,3},{3,2},{4,5},{5,4},{6,7},{7,6},{8,9},{9,8},{10,11... | collective-permute-start | bytes 786440 | tf_op jit(solution)/shard_map/ppermute | solution.py:150
  53.4 8.7 %collective-permute-start.7 = (bf16[4,128,256]{2,1,0:T(8,128)(2,1)S(1)}, bf16[4,128,256]{2,1,0:T(8,128)(2,1)S(1)}, u32[]{:S(2)}, u32[]{:S(2)}) collective-permute-start(bf16[4,128,256]{2,1,0:T(8,128)(2,1)S(1)} %get-tuple-element.51.refs_1_), channel_id=1, source_target_pairs={{0,30},{2,4},{4,2},{6,8},{8,6},{10,12},{12,10},{14,16},{16,14},{18... | collective-permute-start | bytes 786440 | tf_op jit(solution)/shard_map/ppermute | solution.py:161
  54.4 7.6 %collective-permute-start.8 = (bf16[4,128,256]{2,1,0:T(8,128)(2,1)S(1)}, bf16[4,128,256]{2,1,0:T(8,128)(2,1)S(1)}, u32[]{:S(2)}, u32[]{:S(2)}) collective-permute-start(bf16[4,128,256]{2,1,0:T(8,128)(2,1)S(1)} %get-tuple-element.52.refs_2_), channel_id=1, source_target_pairs={{0,2},{2,0},{4,6},{6,4},{8,10},{10,8},{12,14},{14,12},{16,18},{18,... | collective-permute-start | bytes 786440 | tf_op jit(solution)/shard_map/ppermute | solution.py:155
